TPU v7x, 32 devices: a whole 2x2x4 slice. The times are simulated.
32 devices in a mesh: chain: 8 (over y, x, core), space: 4 (over z).
Axes of the slice: x: 2, y: 2, z: 4, core: 2. Of those that a mesh axis runs over, the one named last changes fastest.
Arguments:
- positions: float32 [3, 262144], P(None, ('chain', 'space')), may hold values from -6 to 6
- noise: float32 [2, 3, 262144], P(None, None, ('chain', 'space')), may hold values from -6 to 6
- cell_owner: int32 [262144, 1], P(('chain', 'space')), may hold values from 0 to 31; in each aligned block of 8192 rows (0 to 8191, 8192 to 16383, ...) at most 512 rows name the same one
- tile_rows: int32 [16384], P(('chain', 'space')), may hold values from 0 to 127
- tile_cols: int32 [16384], P(('chain', 'space')), may hold values from 0 to 383
- loop_left: int32 [512], P(('chain', 'space')), may hold values from 0 to 258047, as said below
- loop_span: int32 [512], P(('chain', 'space')), may hold values from 1 to 4096
Outputs:
- final_positions: float32 [3, 262144], P(None, ('chain', 'space'))
Inputs may be any that keep to these rules, and one draw needn't show every extreme that they name: `cell_owner`: among the monomers of one device at most 512 name the same owner, a bound that some block reaches of them. Extruders e * 16 to e * 16 + 15 have their left anchor among the monomers of device e, and loop_left + loop_span < 262144.
All inputs are finite; a program needn't handle non-finite values.
Results may differ from a plain program's by a relative error of at most 0.0003.
Values sent between devices are 32-bit elements; how exact they have to be, the bound alone decides.
No kernel may reach another device: no remote copies, remote signals or barrier semaphores. Data moves between devices by JAX's collectives and lax.ppermute only.
A program may use at most 128 MiB of HBM per device.

v0:
```python
import math

import jax
import jax.numpy as jnp
from jax import lax
from jax.sharding import PartitionSpec as P

time_step = 0.05
bond_stiff = 1.0
loop_stiff = 2.0
cutoff_sq = 2.25
contact_coef = 0.4 / 2.25
noise_gain = math.sqrt(0.1)


def padded(shard, sides, width):
    for axis, dim in sides:
        count, length = (lax.axis_size(axis), shard.shape[dim])
        up = [(i, (i + 1) % count) for i in range(count - 1)]
        down = [(j, i) for i, j in up]
        last = lax.slice_in_dim(shard, length - width, length, axis=dim)
        first = lax.slice_in_dim(shard, 0, width, axis=dim)
        before = lax.ppermute(last, axis, up)
        after = lax.ppermute(first, axis, down)
        shard = jnp.concatenate([before, shard, after], axis=dim)
    return shard


def shifted(value, axis, steps):
    count = lax.axis_size(axis)
    first, last = (max(0, -steps), min(count, count - steps))
    return lax.ppermute(value, axis, [(source, source + steps) for source in range(first, last)])


def slot_ranks(owners, devices):
    count_rows = owners.shape[0]
    ordering = jnp.argsort(owners, stable=True)
    sorted_owner = owners[ordering]
    group_first = jnp.searchsorted(sorted_owner, jnp.arange(devices, dtype=jnp.int32))
    placed = jnp.arange(count_rows, dtype=jnp.int32) - group_first[sorted_owner]
    return jnp.zeros((count_rows,), jnp.int32).at[ordering].set(placed)


def tile_force(near_block, far_block, same_block):
    difference = near_block[:3, :, None] - far_block[:3, None, :]
    dist_sq = jnp.sum(difference * difference, axis=0)
    weight = (
        contact_coef
        * jnp.maximum(1.0 - dist_sq / cutoff_sq, 0.0)
        * near_block[3][:, None]
        * far_block[3][None, :]
    )
    diagonal = jnp.arange(128)[:, None] == jnp.arange(128)[None, :]
    weight = jnp.where(jnp.logical_and(same_block, diagonal), 0.0, weight)
    return jnp.sum(weight[None] * difference, axis=2)


def pick_blocks(table, picked):
    selector = (picked[:, None] == jnp.arange(table.shape[0], dtype=jnp.int32)[None, :]).astype(
        jnp.float32
    )
    return (
        jnp.dot(
            selector, table, precision=lax.Precision.HIGHEST, preferred_element_type=jnp.float32
        ),
        selector,
    )


def contact_forces(cells, extended, row_ids, col_ids):
    blocks = cells.shape[1] // 128
    own_table = cells.reshape(4, blocks, 128).transpose(1, 0, 2).reshape(blocks, 512)
    wide_table = extended.reshape(4, 3 * blocks, 128).transpose(1, 0, 2).reshape(3 * blocks, 512)
    group_size = min(row_ids.shape[0], 32)
    row_groups = row_ids.reshape(-1, group_size)
    col_groups = col_ids.reshape(-1, group_size)

    def accumulate(running, entry):
        rows_now, cols_now = entry
        near_flat, row_select = pick_blocks(own_table, rows_now)
        far_flat, unused_select = pick_blocks(wide_table, cols_now)
        near_blocks = near_flat.reshape(group_size, 4, 128)
        far_blocks = far_flat.reshape(group_size, 4, 128)
        tile_terms = jax.vmap(tile_force)(near_blocks, far_blocks, cols_now == rows_now + blocks)
        added = jnp.dot(
            row_select.T,
            tile_terms.reshape(group_size, 384),
            precision=lax.Precision.HIGHEST,
            preferred_element_type=jnp.float32,
        )
        return (running + added, None)

    start_total = jnp.zeros((blocks, 384), jnp.float32)
    running, unused = lax.scan(accumulate, start_total, (row_groups, col_groups))
    return running.reshape(blocks, 3, 128).transpose(1, 0, 2).reshape(3, blocks * 128)


def local(positions, noise, cell_owner, tile_rows, tile_cols, loop_left, loop_span):
    devices = lax.axis_size(("chain", "space"))
    mono_dev = positions.shape[1]
    capacity = 2 * mono_dev // devices
    slot_total = devices * capacity
    device_id = lax.axis_index(("chain", "space"))
    start_mono = device_id * mono_dev
    owners = cell_owner[:, 0]
    ranks = slot_ranks(owners, devices)
    left_local = loop_left - start_mono
    anchor_a = jnp.concatenate([left_local, jnp.full((1,), mono_dev - 1, jnp.int32)])
    anchor_b = jnp.concatenate([left_local + loop_span, jnp.full((1,), mono_dev, jnp.int32)])
    last_device = device_id == devices - 1
    boundary_stiff = jnp.where(last_device, 0.0, bond_stiff).astype(jnp.float32)[None]
    stiffness = jnp.concatenate(
        [jnp.full(loop_left.shape, loop_stiff, jnp.float32), boundary_stiff]
    )
    current = positions
    for step_index in range(noise.shape[0]):
        payload = jnp.concatenate([current, jnp.ones((1, mono_dev), jnp.float32)], axis=0)
        row_count = payload.shape[0]
        outgoing = (
            jnp.zeros((row_count, devices, capacity), jnp.float32).at[:, owners, ranks].set(payload)
        )
        arrived = lax.all_to_all(
            outgoing, ("chain", "space"), split_axis=1, concat_axis=1, tiled=True
        ).reshape(row_count, slot_total)
        extended = padded(arrived, (("space", 1),), slot_total)
        contact = contact_forces(arrived, extended, tile_rows, tile_cols)
        returned = lax.all_to_all(
            contact.reshape(3, devices, capacity),
            ("chain", "space"),
            split_axis=1,
            concat_axis=1,
            tiled=True,
        )
        excluded = returned[:, owners, ranks]
        step_diff = current[:, 1:] - current[:, :-1]
        bond = bond_stiff * (
            jnp.pad(step_diff, ((0, 0), (0, 1))) - jnp.pad(step_diff, ((0, 0), (1, 0)))
        )
        following = shifted(current, ("chain", "space"), -1)
        joined = jnp.concatenate([current, following], axis=1)
        tension = stiffness[None] * (joined[:, anchor_b] - current[:, anchor_a])
        spread = (
            jnp.zeros((3, 2 * mono_dev), jnp.float32)
            .at[:, anchor_a]
            .add(tension)
            .at[:, anchor_b]
            .add(-tension)
        )
        carried = shifted(spread[:, mono_dev:], ("chain", "space"), 1)
        linked = spread[:, :mono_dev] + carried
        current = current + time_step * (excluded + bond + linked) + noise_gain * noise[step_index]
    return current


def solution(mesh):
    in_specs = (
        P(None, ("chain", "space")),
        P(None, None, ("chain", "space")),
        P(("chain", "space"), None),
        P(("chain", "space")),
        P(("chain", "space")),
        P(("chain", "space")),
        P(("chain", "space")),
    )
    out_specs = P(None, ("chain", "space"))
    return jax.shard_map(local, mesh=mesh, in_specs=in_specs, out_specs=out_specs, check_vma=False)
```

profile of v0, /device:TPU:0, one launch (start us, length us, event | category | flops | bytes accessed | tf_op | source)
XLA Modules:
  0.0 829.6 jit_solution(18340309540960465966)
XLA Ops:
  1.5 7.5 sort.17
  9.0 45.5 %gather_fusion.1 = s32[8192]{0:T(1024)S(1)} fusion(s32[8192]{0:T(1024)S(1)} %bitcast.181, s32[8192]{0:T(1024)S(1)} %get-tuple-element.345), kind=kCustom, calls=%fused_computation.1 | custom fusion | bytes 98304 | tf_op jit(solution)/shard_map/gather | solution.py:38
  54.6 10.5 %while.46 = (s32[]{:T(128)}, u32[32]{0:T(128)S(1)}, u32[32]{0:T(128)S(1)}, s32[8192]{0:T(1024)S(1)}, s32[]{:T(128)}, /*index=5*/s32[]{:T(128)}, s32[]{}) while((s32[]{:T(128)}, u32[32]{0:T(128)S(1)}, u32[32]{0:T(128)S(1)}, s32[8192]{0:T(1024)S(1)}, s32[]{:T(128)}, /*index=5*/s32[]{:T(128)}, s32[]{}) %tuple.150), condition=%wide.region_2.3_spmd.clone, body=%wide.region_1.2_spmd.clone.sunk | while | flops 1444 | bytes 5732 | solution.py:39
  73.6 15.8 %select_subtract_fusion = s32[8192]{0:T(1024)S(1)} fusion(pred[8192]{0:T(1024)(128)(4,1)S(1)} %get-tuple-element.294, pred[8192]{0:T(1024)(128)(4,1)S(1)} %get-tuple-element.293, pred[8192]{0:T(1024)(128)(4,1)S(1)} %get-tuple-element.292, pred[8192]{0:T(1024)(128)(4,1)S(1)} %get-tuple-element.291, pred[8192]{0:T(1024)(128)(4,1)S(1)} %get-tuple-element.290, ...), kind=kLoop, calls=%fused_computation.136 | loop fusion | flops 212992 | bytes 270436 | tf_op jit(solution)/shard_map/sub | solution.py:40
  89.4 30.5 %scatter_custom_fusion = s32[8192]{0:T(1024)S(1)} fusion(s32[8192]{0:T(1024)S(1)} %get-tuple-element.346, s32[8192]{0:T(1024)S(1)} %select_subtract_fusion, s32[]{:T(128)} %constant.99.clone.1), kind=kCustom, calls=%fused_computation.139 | custom fusion | bytes 32772 | tf_op jit(solution)/shard_map/scatter | solution.py:41
  123.1 24.5 %scatter_custom_fusion.5 = f32[4,16384]{0,1:T(8,128)} fusion(s32[8192]{0:T(1024)S(1)} %broadcast_select_fusion.2, f32[8192,4]{1,0:T(8,128)} %copy.206, f32[]{:T(128)} %constant.100.clone.1), kind=kCustom, calls=%fused_computation.65 | custom fusion | bytes 262656
  147.6 5.9 copy.207
  153.5 8.4 %all-to-all-start = ((f32[4,32,512]{2,0,1:T(4,128)}), f32[4,32,512]{2,0,1:T(4,128)S(1)}, u32[]{:S(2)}, u32[]{:S(2)}) async-start(f32[4,32,512]{2,0,1:T(4,128)} %copy.207), calls=%async_computation | async-start | bytes 524288 | tf_op jit(solution)/shard_map/all_to_all | solution.py:122
  167.9 5.1 copy.218
  181.4 7.3 scatter_custom_fusion.2
  194.5 7.3 fusion.50
  209.4 124.9 %while.47 = (s32[]{:T(128)}, f32[128,384]{1,0:T(8,128)S(1)}, s32[16,32]{1,0:T(8,128)S(1)}, s32[16,32]{1,0:T(8,128)S(1)}, f32[128,512]{1,0:T(8,128)S(1)}, /*index=5*/f32[384,512]{1,0:T(8,128)S(1)}, s32[]{:T(128)}, s32[]{:T(128)}) while((s32[]{:T(128)}, f32[128,384]{1,0:T(8,128)S(1)}, s32[16,32]{1,0:T(8,128)S(1)}, ...), condition=%wide.region_8.9_spmd.clone, body=%wide.region_5.8_spmd.clone.sunk | while | flops 132247616 | bytes 10650659 | solution.py:94
  342.7 7.2 all-to-all-done.1
  349.9 4.8 copy.216
  354.7 118.5 %gather_fusion.2 = f32[8192,3]{1,0:T(8,128)} fusion(f32[3,32,512]{0,2,1:T(8,128)} %copy.216, s32[8192]{0:T(1024)S(1)} %bitcast.182), kind=kCustom, calls=%fused_computation.2 | custom fusion | bytes 262144 | tf_op jit(solution)/shard_map/gather | solution.py:134
  485.9 24.5 %scatter_custom_fusion.6 = f32[4,16384]{0,1:T(8,128)} fusion(s32[8192]{0:T(1024)S(1)} %broadcast_select_fusion.2, f32[8192,4]{1,0:T(8,128)} %copy.223, f32[]{:T(128)} %constant.100.clone.1), kind=kCustom, calls=%fused_computation.63 | custom fusion | bytes 262656
  510.4 5.9 copy.224
  520.4 5.1 copy.235
  533.9 7.3 scatter_custom_fusion.4
  547.0 7.3 fusion.49
  561.9 124.9 %while.48 = (s32[]{:T(128)}, f32[128,384]{1,0:T(8,128)S(1)}, s32[16,32]{1,0:T(8,128)S(1)}, s32[16,32]{1,0:T(8,128)S(1)}, f32[128,512]{1,0:T(8,128)S(1)}, /*index=5*/f32[384,512]{1,0:T(8,128)S(1)}, s32[]{:T(128)}, s32[]{:T(128)}) while((s32[]{:T(128)}, f32[128,384]{1,0:T(8,128)S(1)}, s32[16,32]{1,0:T(8,128)S(1)}, ...), condition=%wide.region_15.16_spmd.clone, body=%wide.region_12.15_spmd.clone.sunk | while | flops 132247616 | bytes 10650659 | solution.py:94
  695.3 7.2 all-to-all-done.3
  702.5 4.8 copy.233
  707.4 118.5 %gather_fusion.5 = f32[8192,3]{1,0:T(8,128)} fusion(f32[3,32,512]{0,2,1:T(8,128)} %copy.233, s32[8192]{0:T(1024)S(1)} %bitcast.183), kind=kCustom, calls=%fused_computation.5 | custom fusion | bytes 262144 | tf_op jit(solution)/shard_map/gather | solution.py:134
  (553 shorter events, 356.1 us)
Async XLA Ops:
  0.0 9.0 %copy-start = (s32[8192,1]{0,1:T(1,128)S(1)}, s32[8192,1]{0,1:T(1,128)}, u32[]{:S(2)}) copy-start(s32[8192,1]{0,1:T(1,128)} %param.15) | copy-start | bytes 98308
  0.0 167.8 %collective-permute-start.2 = (f32[3,8192]{1,0:T(4,128)}, f32[3,8192]{1,0:T(4,128)S(1)}, u32[]{:S(2)}, u32[]{:S(2)}) collective-permute-start(f32[3,8192]{1,0:T(4,128)} %param.13), channel_id=1, source_target_pairs={{1,0},{2,1},{3,2},{4,3},{5,4},{6,5},{7,6},{8,7},{9,8},{10,9},{11,1... | collective-permute-start | bytes 294920 | tf_op jit(solution)/shard_map/ppermute | solution.py:32
  9.0 57.6 %copy-start.1 = (f32[3,8192]{1,0:T(4,128)S(1)}, f32[3,8192]{1,0:T(4,128)}, u32[]{:S(2)}) copy-start(f32[3,8192]{1,0:T(4,128)} %param.13) | copy-start | bytes 294916
  54.6 65.5 %copy-start.6 = (s32[2]{0:T(128)S(1)}, s32[2]{0:T(128)}, u32[]{:S(2)}) copy-start(s32[2]{0:T(128)} %constant.134) | copy-start | bytes 28
  54.6 65.7 %copy-start.5 = (s32[2]{0:T(128)S(1)}, s32[2]{0:T(128)}, u32[]{:S(2)}) copy-start(s32[2]{0:T(128)} %constant.137) | copy-start | bytes 28
  153.5 11.0 %copy-start.3 = (s32[512]{0:T(512)S(1)}, s32[512]{0:T(512)}, u32[]{:S(2)}) copy-start(s32[512]{0:T(512)} %param.16) | copy-start | bytes 6148
  153.5 11.1 %copy-start.4 = (s32[512]{0:T(512)S(1)}, s32[512]{0:T(512)}, u32[]{:S(2)}) copy-start(s32[512]{0:T(512)} %param.17) | copy-start | bytes 6148
  153.5 11.2 %copy-start.7 = (s32[16]{0:T(128)S(1)}, s32[16]{0:T(128)}, u32[]{:S(2)}) copy-start(s32[16]{0:T(128)} %param.19) | copy-start | bytes 196
  153.5 11.2 %copy-start.8 = (s32[16]{0:T(128)S(1)}, s32[16]{0:T(128)}, u32[]{:S(2)}) copy-start(s32[16]{0:T(128)} %param.18) | copy-start | bytes 196
  153.5 11.3 %copy-start.2 = (f32[2,3,8192]{2,0,1:T(2,128)S(1)}, f32[2,3,8192]{2,0,1:T(2,128)}, u32[]{:S(2)}) copy-start(f32[2,3,8192]{2,0,1:T(2,128)} %param.14) | copy-start | bytes 589828
  153.5 35.1 %all-to-all-start = ((f32[4,32,512]{2,0,1:T(4,128)}), f32[4,32,512]{2,0,1:T(4,128)S(1)}, u32[]{:S(2)}, u32[]{:S(2)}) async-start(f32[4,32,512]{2,0,1:T(4,128)} %copy.207), calls=%async_computation | async-start | bytes 524288 | tf_op jit(solution)/shard_map/all_to_all | solution.py:122
  188.6 20.1 %collective-permute-start.1 = (f32[4,16384]{1,0:T(4,128)S(1)}, f32[4,16384]{1,0:T(4,128)S(1)}, u32[]{:S(2)}, u32[]{:S(2)}) collective-permute-start(f32[4,16384]{1,0:T(4,128)S(1)} %bitcast.205), channel_id=1, source_target_pairs={{1,0},{2,1},{3,2},{5,4},{6,5},{7,6},{9,8},{10,9},{11,10},{13,12},{... | collective-permute-start | bytes 786440 | tf_op jit(solution)/shard_map/ppermute | solution.py:24
  189.9 18.8 %collective-permute-start = (f32[4,16384]{1,0:T(4,128)S(1)}, f32[4,16384]{1,0:T(4,128)S(1)}, u32[]{:S(2)}, u32[]{:S(2)}) collective-permute-start(f32[4,16384]{1,0:T(4,128)S(1)} %bitcast.206), channel_id=1, source_target_pairs={{0,1},{1,2},{2,3},{4,5},{5,6},{6,7},{8,9},{9,10},{10,11},{12,13},{... | collective-permute-start | bytes 786440 | tf_op jit(solution)/shard_map/ppermute | solution.py:23
  204.6 271.5 %collective-permute-start.3 = (f32[3,8192]{1,0:T(4,128)S(1)}, f32[3,8192]{1,0:T(4,128)S(1)}, u32[]{:S(2)}, u32[]{:S(2)}) collective-permute-start(f32[3,8192]{1,0:T(4,128)S(1)} %copy.221), channel_id=1, source_target_pairs={{0,1},{1,2},{2,3},{3,4},{4,5},{5,6},{6,7},{7,8},{8,9},{9,10},{10,1... | collective-permute-start | bytes 294920 | tf_op jit(solution)/shard_map/ppermute | solution.py:32
  335.4 14.5 %all-to-all-start.1 = ((f32[3,32,512]{2,0,1:T(4,128)}), f32[3,32,512]{2,0,1:T(4,128)S(1)}, u32[]{:S(2)}, u32[]{:S(2)}) async-start(f32[3,32,512]{2,0,1:T(4,128)} %copy.215), calls=%async_computation.1 | async-start | bytes 524288 | tf_op jit(solution)/shard_map/all_to_all | solution.py:127
  476.3 44.1 %collective-permute-start.6 = (f32[3,8192]{1,0:T(4,128)S(1)}, f32[3,8192]{1,0:T(4,128)S(1)}, u32[]{:S(2)}, u32[]{:S(2)}) collective-permute-start(f32[3,8192]{1,0:T(4,128)S(1)} %fusion.33), channel_id=1, source_target_pairs={{1,0},{2,1},{3,2},{4,3},{5,4},{6,5},{7,6},{8,7},{9,8},{10,9},{11,1... | collective-permute-start | bytes 294920 | tf_op jit(solution)/shard_map/ppermute | solution.py:32
  516.3 24.8 %all-to-all-start.2 = ((f32[4,32,512]{2,0,1:T(4,128)}), f32[4,32,512]{2,0,1:T(4,128)S(1)}, u32[]{:S(2)}, u32[]{:S(2)}) async-start(f32[4,32,512]{2,0,1:T(4,128)} %copy.224), calls=%async_computation.2 | async-start | bytes 524288 | tf_op jit(solution)/shard_map/all_to_all | solution.py:122
  541.2 20.1 %collective-permute-start.5 = (f32[4,16384]{1,0:T(4,128)S(1)}, f32[4,16384]{1,0:T(4,128)S(1)}, u32[]{:S(2)}, u32[]{:S(2)}) collective-permute-start(f32[4,16384]{1,0:T(4,128)S(1)} %bitcast.207), channel_id=1, source_target_pairs={{1,0},{2,1},{3,2},{5,4},{6,5},{7,6},{9,8},{10,9},{11,10},{13,12},{... | collective-permute-start | bytes 786440 | tf_op jit(solution)/shard_map/ppermute | solution.py:24
  542.4 18.8 %collective-permute-start.4 = (f32[4,16384]{1,0:T(4,128)S(1)}, f32[4,16384]{1,0:T(4,128)S(1)}, u32[]{:S(2)}, u32[]{:S(2)}) collective-permute-start(f32[4,16384]{1,0:T(4,128)S(1)} %bitcast.208), channel_id=1, source_target_pairs={{0,1},{1,2},{2,3},{4,5},{5,6},{6,7},{8,9},{9,10},{10,11},{12,13},{... | collective-permute-start | bytes 786440 | tf_op jit(solution)/shard_map/ppermute | solution.py:23
  557.1 271.6 %collective-permute-start.7 = (f32[3,8192]{1,0:T(4,128)S(1)}, f32[3,8192]{1,0:T(4,128)S(1)}, u32[]{:S(2)}, u32[]{:S(2)}) collective-permute-start(f32[3,8192]{1,0:T(4,128)S(1)} %copy.238), channel_id=1, source_target_pairs={{0,1},{1,2},{2,3},{3,4},{4,5},{5,6},{6,7},{7,8},{8,9},{9,10},{10,1... | collective-permute-start | bytes 294920 | tf_op jit(solution)/shard_map/ppermute | solution.py:32
  687.9 14.6 %all-to-all-start.3 = ((f32[3,32,512]{2,0,1:T(4,128)}), f32[3,32,512]{2,0,1:T(4,128)S(1)}, u32[]{:S(2)}, u32[]{:S(2)}) async-start(f32[3,32,512]{2,0,1:T(4,128)} %copy.232), calls=%async_computation.3 | async-start | bytes 524288 | tf_op jit(solution)/shard_map/all_to_all | solution.py:127
where the time goes:
time: 832 us; the launch traced here: 830 us
  local copies, waits for them, and re-layouts  467 us (56%)
  other arithmetic  268 us (32%)
  starting transfers between devices  43 us (5%)
  matrix products  32.4 us (4%)
  waiting for transfers between devices  14.4 us (2%)
    gather x4, local copies, waits for them, and re-layouts, local(): excluded = returned[:, owners, ranks]  243 us
    reduce_sum x32, other arithmetic, tile_force(): return jnp.sum(weight[None] * difference, axis=2)  118 us
    reduce_sum x32, other arithmetic, tile_force(): dist_sq = jnp.sum(difference * difference, axis=0)  66 us
    unnamed x31, local copies, waits for them, and re-layouts  58.3 us
    gather x1, local copies, waits for them, and re-layouts, slot_ranks(): sorted_owner = owners[ordering]  45.5 us
    scatter x1, local copies, waits for them, and re-layouts, slot_ranks(): return jnp.zeros((count_rows,), jnp.int32).at[ordering].set(placed)  30.5 us
    select_n x32, other arithmetic, tile_force(): weight = jnp.where(jnp.logical_and(same_block, diagonal), 0.0, weight)  26.1 us
    scatter-add x4, other arithmetic, local(): spread = jnp.zeros((3, 2 * mono_dev), jnp.float32).at[:, anchor_a].add(te...  23.4 us
  transfers between devices with their start and end apart: 12, of which 2 were waited for; matrix products, arithmetic and copies ran while one was open for 92% of the time, Pallas kernels for 0%

commit v1 on v0

v1 whole, which is shorter than its diff:
```python
import functools
import math

import jax
import jax.numpy as jnp
from jax import lax
from jax.experimental import pallas as pl
from jax.experimental.pallas import tpu as pltpu
from jax.sharding import PartitionSpec as P

time_step = 0.05
bond_stiff = 1.0
loop_stiff = 2.0
cutoff_sq = 2.25
contact_coef = 0.4 / 2.25
noise_gain = math.sqrt(0.1)
longest_loop = 4096
lanes = 128
far_away = 1e15

vmem = pl.BlockSpec(memory_space=pltpu.VMEM)
smem = pl.BlockSpec(memory_space=pltpu.SMEM)
f32 = jnp.float32
bf16 = jnp.bfloat16


def call(body, outs, in_specs, args, scratch=(), flops=0, moved=2_000_000):
    many = isinstance(outs, list)
    return pl.pallas_call(
        body,
        out_shape=outs,
        in_specs=in_specs,
        out_specs=[vmem] * len(outs) if many else vmem,
        scratch_shapes=list(scratch),
        compiler_params=pltpu.CompilerParams(vmem_limit_bytes=32 * 1024 * 1024),
        cost_estimate=pl.CostEstimate(flops=flops, bytes_accessed=moved, transcendentals=0),
    )(*args)


def iota(shape, dim):
    return lax.broadcasted_iota(jnp.int32, shape, dim)


def pick(row, where_to):
    return jnp.take_along_axis(
        jnp.broadcast_to(row, where_to.shape), where_to, axis=1, mode="promise_in_bounds"
    )


def fill_slots(index_ref, source_ref, out_ref, per_owner):
    rows = source_ref.shape[1] // lanes
    fields = source_ref.shape[0]

    def one(group, carry):
        code = index_ref[pl.ds(pl.multiple_of(group * 8, 8), 8), :]
        row_of = (code >> 7) - 1
        lane_of = code & 127
        held = [jnp.full((8, lanes), far_away, f32) for _ in range(fields)]
        for j in range(rows):
            here = row_of == j
            for c in range(fields):
                row = source_ref[c : c + 1, j * lanes : (j + 1) * lanes]
                held[c] = jnp.where(here, pick(row, lane_of), held[c])
        owners_here = 8 // per_owner
        for i in range(owners_here):
            for c in range(fields):
                out_ref[group * owners_here + i, c * per_owner : (c + 1) * per_owner, :] = held[c][
                    i * per_owner : (i + 1) * per_owner, :
                ]
        return carry

    lax.fori_loop(0, index_ref.shape[0] // 8, one, 0)


def take_slots(slot_ref, source_ref, group, per_owner):
    slot = slot_ref[pl.ds(pl.multiple_of(group * 8, 8), 8), :]
    row_of = slot >> 7
    lane_of = slot & 127
    fields = source_ref.shape[1] // per_owner
    held = [jnp.zeros((8, lanes), f32) for _ in range(fields)]
    for s in range(source_ref.shape[0] * per_owner):
        here = row_of == s
        for c in range(fields):
            at = c * per_owner + s % per_owner
            row = source_ref[s // per_owner, at : at + 1, :]
            held[c] = jnp.where(here, pick(row, lane_of), held[c])
    return held


def index_kernel(capacity, owner_ref, x_ref, out_ref, index_ref, slot_ref, total_ref):
    rows = owner_ref.shape[0]
    devices = out_ref.shape[0]
    own = owner_ref[...]
    lane = iota((rows, lanes), 1)
    tri = jnp.where(
        iota((lanes, 2 * lanes), 1) >= lanes,
        1.0,
        jnp.where(iota((lanes, 2 * lanes), 0) < iota((lanes, 2 * lanes), 1), 1.0, 0.0),
    ).astype(bf16)

    def count(chunk, carry):
        prefix, total = carry
        masks = jnp.concatenate(
            [jnp.where(own == chunk * 8 + i, 1.0, 0.0) for i in range(8)], axis=0
        ).astype(bf16)
        both = jnp.dot(masks, tri, preferred_element_type=f32)
        for i in range(8):
            o = chunk * 8 + i
            part = both[i * rows : (i + 1) * rows]
            prefix = jnp.where(own == o, part[:, :lanes], prefix)
            total = jnp.where(lane == o, part[:, lanes:], total)
        return prefix, total

    zero = jnp.zeros((rows, lanes), f32)
    prefix, total = lax.fori_loop(0, devices // 8, count, (zero, zero))
    lower = jnp.where(iota((rows, rows), 1) < iota((rows, rows), 0), 1.0, 0.0).astype(bf16)
    above = jnp.dot(lower, total.astype(bf16), preferred_element_type=f32)
    offset = jnp.take_along_axis(above, own, axis=1, mode="promise_in_bounds")
    slot_ref[...] = own * capacity + (prefix + offset).astype(jnp.int32)

    down = iota((lanes, lanes), 0)
    lane_code = iota((lanes, lanes), 1).astype(f32)
    total_ref[...] = jnp.zeros_like(total_ref)

    def spread(j, carry):
        slot = slot_ref[pl.ds(j, 1), :]
        high = (slot >> 7) == down
        low = jnp.where((slot & 127) == down, 1.0, 0.0).astype(bf16)
        row_code = ((j + 1) * lanes).astype(f32)
        left = jnp.concatenate(
            [jnp.where(high, lane_code, 0.0), jnp.where(high, row_code, 0.0)], axis=1
        ).astype(bf16)
        right = jnp.concatenate([low, low], axis=1)
        total_ref[...] += lax.dot_general(
            left, right, (((1,), (1,)), ((), ())), preferred_element_type=f32
        )
        return carry

    lax.fori_loop(0, rows, spread, 0)
    index_ref[...] = total_ref[...].astype(jnp.int32)
    fill_slots(index_ref, x_ref, out_ref, out_ref.shape[1] // 3)


def chain_forces(ends_ref, x_ref, after_ref, before_ref, wide_ref, force_ref):
    mono_dev = x_ref.shape[1]
    blocks = mono_dev // lanes
    wide_ref[...] = jnp.zeros_like(wide_ref)
    wide_ref[0:3, 0:lanes] = before_ref[:, mono_dev - lanes :]
    wide_ref[0:3, lanes : lanes + mono_dev] = x_ref[...]
    wide_ref[0:3, lanes + mono_dev :] = after_ref[...]
    lane = iota((8, lanes), 1)
    has_before = ends_ref[0, 0].astype(f32)
    has_after = ends_ref[0, 1].astype(f32)
    for j in range(blocks):
        here = wide_ref[:, (j + 1) * lanes : (j + 2) * lanes]
        left = wide_ref[:, j * lanes : (j + 1) * lanes]
        right = wide_ref[:, (j + 2) * lanes : (j + 3) * lanes]
        down = pltpu.roll(jnp.where(lane == lanes - 1, left, here), 1, 1) - here
        up = pltpu.roll(jnp.where(lane == 0, right, here), lanes - 1, 1) - here
        if j == 0:
            down = jnp.where(lane == 0, down * has_before, down)
        if j == blocks - 1:
            up = jnp.where(lane == lanes - 1, up * has_after, up)
        force_ref[:, j * lanes : (j + 1) * lanes] = bond_stiff * down + bond_stiff * up

    def window(ref, at):
        return ref.at[:, pl.ds(pl.multiple_of((at >> 7) * lanes, lanes), lanes)]

    def value(block, at):
        return jnp.sum(jnp.where(lane[: block.shape[0]] == (at & 127), block, 0.0), axis=1, keepdims=True)

    todo = []
    for e in range(ends_ref.shape[1]):
        a, b = ends_ref[1, e], ends_ref[2, e]
        pull = loop_stiff * (value(window(wide_ref, b + lanes)[...], b) - value(window(wide_ref, a + lanes)[...], a))
        todo.append((a, pull))
        todo.append((jnp.minimum(b, mono_dev - 1), jnp.where(b < mono_dev, -pull, 0.0)))
    for e in range(ends_ref.shape[1]):
        a, b = ends_ref[3, e], ends_ref[4, e] - mono_dev
        b_in = jnp.maximum(b, 0)
        far_end = value(window(before_ref, a)[...], a)
        pull = loop_stiff * (value(window(wide_ref, b_in + lanes)[...], b_in)[0:3] - far_end)
        wanted = jnp.logical_and(b >= 0, ends_ref[0, 0] > 0)
        pull = jnp.where(wanted, -pull, 0.0)
        todo.append((b_in, jnp.concatenate([pull, jnp.zeros((5, 1), f32)], axis=0)))
    for at, pull in todo:
        spot = window(force_ref, at)
        spot[...] = spot[...] + jnp.where(lane == (at & 127), pull, 0.0)


def chain_step(step, ends_ref, x_ref, after_ref, before_ref, noise_ref, out_ref, wide_ref, force_ref):
    chain_forces(ends_ref, x_ref, after_ref, before_ref, wide_ref, force_ref)
    for c in range(3):
        out_ref[c : c + 1, :] = (
            x_ref[c : c + 1, :]
            + time_step * force_ref[c : c + 1, :]
            + noise_gain * noise_ref[c, step : step + 1, :]
        )


def first_kernel(ends_ref, x_ref, after_ref, before_ref, noise_ref, index_ref, y_ref, out_ref, wide_ref, force_ref):
    chain_step(0, ends_ref, x_ref, after_ref, before_ref, noise_ref, y_ref, wide_ref, force_ref)
    fill_slots(index_ref, y_ref, out_ref, out_ref.shape[1] // 3)


def contact_kernel(ends_ref, rows_ref, cols_ref, own_ref, below_ref, above_ref, out_ref, table, near, far, pulled, total):
    devices = own_ref.shape[0]
    per_owner = own_ref.shape[1] // 3
    blocks = devices * per_owner
    scale = 1.0 / math.sqrt(cutoff_sq)
    has_below = jnp.full((1, lanes), ends_ref[0], jnp.int32) > 0
    has_above = jnp.full((1, lanes), ends_ref[1], jnp.int32) > 0

    def build(o, carry):
        for k in range(per_owner):
            block = o * per_owner + k
            for c in range(3):
                at = c * per_owner + k
                table[block, c : c + 1, :] = jnp.where(has_below, below_ref[o, at : at + 1, :] * scale, far_away)
                table[blocks + block, c : c + 1, :] = own_ref[o, at : at + 1, :] * scale
                table[2 * blocks + block, c : c + 1, :] = jnp.where(
                    has_above, above_ref[o, at : at + 1, :] * scale, far_away
                )
        return carry

    lax.fori_loop(0, devices, build, 0)
    total[...] = jnp.zeros_like(total)
    down = iota((8, lanes), 0)

    def group(g, carry):
        same = jnp.zeros((8, lanes), jnp.int32)
        for i in range(8):
            r, q = rows_ref[g * 8 + i], cols_ref[g * 8 + i]
            near[4 * i : 4 * i + 4, :] = table[blocks + r]
            far[4 * i : 4 * i + 4, :] = table[q]
            same = jnp.where(down == i, (q == r + blocks).astype(jnp.int32), same)
        px, py, pz = [near[pl.ds(c, 8, stride=4), :] for c in range(3)]
        fx, fy, fz = [far[pl.ds(c, 8, stride=4), :] for c in range(3)]
        ax = ay = az = jnp.zeros((8, lanes), f32)
        for s in range(lanes):
            if s == 0:
                dx, dy, dz = px - fx, py - fy, pz - fz
            else:
                dx = px - pltpu.roll(fx, s, 1)
                dy = py - pltpu.roll(fy, s, 1)
                dz = pz - pltpu.roll(fz, s, 1)
            w = jnp.maximum(1.0 - (dx * dx + dy * dy + dz * dz), 0.0)
            if s == 0:
                w = jnp.where(same > 0, 0.0, w)
            ax = ax + w * dx
            ay = ay + w * dy
            az = az + w * dz
        pulled[pl.ds(0, 8, stride=4), :] = ax
        pulled[pl.ds(1, 8, stride=4), :] = ay
        pulled[pl.ds(2, 8, stride=4), :] = az
        for i in range(8):
            r = rows_ref[g * 8 + i]
            total[r] = total[r] + pulled[4 * i : 4 * i + 4, :]
        return carry

    lax.fori_loop(0, rows_ref.shape[0] // 8, group, 0)
    back = contact_coef * math.sqrt(cutoff_sq)

    def finish(o, carry):
        for k in range(per_owner):
            for c in range(3):
                at = c * per_owner + k
                out_ref[o, at : at + 1, :] = total[o * per_owner + k, c : c + 1, :] * back
        return carry

    lax.fori_loop(0, devices, finish, 0)


def gather_kernel(slot_ref, source_ref, base_ref, out_ref):
    per_owner = source_ref.shape[1] // 3

    def one(group, carry):
        held = take_slots(slot_ref, source_ref, group, per_owner)
        for i in range(8):
            at = pl.ds(pl.multiple_of((group * 8 + i) * lanes, lanes), lanes)
            for c in range(3):
                out_ref[c : c + 1, at] = base_ref[c : c + 1, at] + time_step * held[c][i : i + 1, :]
        return carry

    lax.fori_loop(0, slot_ref.shape[0] // 8, one, 0)


def shifted(value, axis, steps):
    count = lax.axis_size(axis)
    first, last = (max(0, -steps), min(count, count - steps))
    return lax.ppermute(value, axis, [(source, source + steps) for source in range(first, last)])


def local(positions, noise, cell_owner, tile_rows, tile_cols, loop_left, loop_span):
    both = ("chain", "space")
    devices = lax.axis_size(both)
    mono_dev = positions.shape[1]
    capacity = 2 * mono_dev // devices
    per_owner = capacity // lanes
    rows = mono_dev // lanes
    blocks = devices * per_owner
    extruders = loop_left.shape[0]
    device_id = lax.axis_index(both)
    space_id = lax.axis_index("space")

    left = loop_left - device_id * mono_dev
    anchors = jnp.stack([left, left + loop_span])
    anchors_before = shifted(anchors, both, 1)
    edge = jnp.zeros((1, extruders), jnp.int32)
    edge = edge.at[0, 0].set((device_id > 0).astype(jnp.int32))
    edge = edge.at[0, 1].set((device_id < devices - 1).astype(jnp.int32))
    ends = jnp.concatenate([edge, anchors, anchors_before], axis=0)
    slabs = jnp.stack([space_id > 0, space_id < lax.axis_size("space") - 1]).astype(jnp.int32)
    noise_t = noise.transpose(1, 0, 2)

    sent = jax.ShapeDtypeStruct((devices, 3 * per_owner, lanes), f32)
    chain = jax.ShapeDtypeStruct((3, mono_dev), f32)
    chain_scratch = [
        pltpu.VMEM((8, lanes + mono_dev + longest_loop), f32),
        pltpu.VMEM((8, mono_dev), f32),
    ]

    before = shifted(positions, both, 1)
    after = shifted(positions[:, :longest_loop], both, -1)
    x_out, index, slot = call(
        functools.partial(index_kernel, capacity),
        [
            sent,
            jax.ShapeDtypeStruct((blocks, lanes), jnp.int32),
            jax.ShapeDtypeStruct((rows, lanes), jnp.int32),
        ],
        [vmem, vmem],
        (cell_owner.reshape(rows, lanes), positions),
        [pltpu.VMEM((blocks, lanes), f32)],
    )

    def exchange(value):
        return lax.all_to_all(value, both, split_axis=0, concat_axis=0, tiled=True)

    def contact(cells):
        below = shifted(cells, "space", 1)
        above = shifted(cells, "space", -1)
        return call(
            contact_kernel,
            sent,
            [smem, smem, smem, vmem, vmem, vmem],
            (slabs, tile_rows, tile_cols, cells, below, above),
            [
                pltpu.VMEM((3 * blocks, 4, lanes), f32),
                pltpu.VMEM((32, lanes), f32),
                pltpu.VMEM((32, lanes), f32),
                pltpu.VMEM((32, lanes), f32),
                pltpu.VMEM((blocks, 4, lanes), f32),
            ],
            flops=16 * tile_rows.shape[0] * lanes * lanes,
        )

    x_cells = exchange(x_out)
    y_chain, y_out = call(
        first_kernel,
        [chain, sent],
        [smem] + [vmem] * 5,
        (ends, positions, after, before, noise_t, index),
        chain_scratch,
    )
    y_cells = exchange(y_out)
    contact0 = contact(x_cells)
    back0 = exchange(contact0)
    x1_cells = y_cells + time_step * contact0
    contact1 = contact(x1_cells)
    back1 = exchange(contact1)

    x1 = call(gather_kernel, chain, [vmem] * 3, (slot, back0, y_chain))
    before1 = shifted(x1, both, 1)
    after1 = shifted(x1[:, :longest_loop], both, -1)
    z = call(
        functools.partial(chain_step, 1),
        chain,
        [smem] + [vmem] * 4,
        (ends, x1, after1, before1, noise_t),
        chain_scratch,
    )
    return call(gather_kernel, chain, [vmem] * 3, (slot, back1, z))


def solution(mesh):
    in_specs = (
        P(None, ("chain", "space")),
        P(None, None, ("chain", "space")),
        P(("chain", "space"), None),
        P(("chain", "space")),
        P(("chain", "space")),
        P(("chain", "space")),
        P(("chain", "space")),
    )
    out_specs = P(None, ("chain", "space"))
    return jax.shard_map(local, mesh=mesh, in_specs=in_specs, out_specs=out_specs, check_vma=False)
```

time: 832 us -> 185 us (0.22)
  local copies, waits for them, and re-layouts: 467 us -> 3.72 us
  other arithmetic: 268 us -> 4.27 us
  Pallas kernels: 0 us -> 106 us
  matrix products: 32.4 us -> 0 us
    gather x25 -> x0, local copies, waits for them, and re-layouts: 313 us -> none  [the longest x4 243 us: local(): excluded = returned[:, owners, ranks]]
    reduce_sum x64 -> x0, other arithmetic: 184 us -> none  [the longest x32 118 us: tile_force(): return jnp.sum(weight[None] * difference, axis=2)]
    pallas_call x0 -> x7, Pallas kernels: none -> 106 us  [call(): pl.pallas_call(body, out_shape=outs, in_specs=in_specs, out_specs=[vmem]...]
    unnamed x31 -> x16, local copies, waits for them, and re-layouts: 58.3 us -> 1.69 us
    scatter x3 -> x2, local copies, waits for them, and re-layouts: 42.3 us -> 1.37 us  [the longest x1 1.36 us: local(): edge = edge.at[0, 1].set((device_id < devices - 1).astype(jnp.int32))]
    dot_general x96 -> x0, matrix products: 32.4 us -> none  [the longest x64 20 us: pick_blocks(): jnp.dot(selector, table, precision=lax.Precision.HIGHEST, preferred_eleme...]
    select_n x48 -> x0, other arithmetic: 26.4 us -> none  [the longest x32 26.1 us: tile_force(): weight = jnp.where(jnp.logical_and(same_block, diagonal), 0.0, weight)]
    scatter-add x4 -> x0, other arithmetic: 23.4 us -> none  [local(): spread = jnp.zeros((3, 2 * mono_dev), jnp.float32).at[:, anchor_a].add(te...]
  transfers between devices with their start and end apart: 12 -> 13, of which waited for: 2 -> 3; matrix products, arithmetic and copies ran while one was open for 92% -> 3% of each run, Pallas kernels for 0% -> 55%
where the time goes in v1:
time: 185 us; the launch traced here: 184 us
  Pallas kernels  106 us (57%)
  starting transfers between devices  49.9 us (27%)
  waiting for transfers between devices  19.4 us (10%)
  other arithmetic  4.27 us (2%)
  local copies, waits for them, and re-layouts  3.72 us (2%)
    pallas_call x7, Pallas kernels, call(): pl.pallas_call(body, out_shape=outs, in_specs=in_specs, out_specs=[vmem]...  106 us
    ppermute x9, starting transfers between devices, shifted(): lax.ppermute(value, axis, [(source, source + steps) for source in range(f...  26.7 us
    all_to_all x4, starting transfers between devices, exchange(): return lax.all_to_all(value, both, split_axis=0, concat_axis=0, tiled=True)  23.2 us
    ppermute x9, waiting for transfers between devices, shifted(): lax.ppermute(value, axis, [(source, source + steps) for source in range(f...  19.4 us
  transfers between devices with their start and end apart: 13, of which 3 were waited for; matrix products, arithmetic and copies ran while one was open for 3% of the time, Pallas kernels for 55%

profile of v1, /device:TPU:0, one launch (start us, length us, event | category | flops | bytes accessed | tf_op | source)
XLA Modules:
  0.0 184.2 jit_solution(12064543071329092526)
XLA Ops:
  0.0 4.9 %collective-permute-start.2 = (f32[3,8192]{1,0:T(4,128)}, f32[3,8192]{1,0:T(4,128)S(1)}, u32[]{:S(2)}, u32[]{:S(2)}) collective-permute-start(f32[3,8192]{1,0:T(4,128)} %x_ref.3), channel_id=1, source_target_pairs={{0,1},{1,2},{2,3},{3,4},{4,5},{5,6},{6,7},{7,8},{8,9},{9,10},{10,1... | collective-permute-start | bytes 294920 | tf_op jit(solution)/shard_map/ppermute | solution.py:291
  6.6 17.5 %shard_map.73 = (f32[32,12,128]{2,1,0:T(8,128)}, s32[128,128]{1,0:T(8,128)S(1)}, s32[64,128]{1,0:T(8,128)S(1)}) custom-call(s32[64,128]{1,0:T(8,128)S(1)} %bitcast.14, f32[3,8192]{1,0:T(4,128)S(1)} %copy-done), custom_call_target="tpu_custom_call" | custom-call | bytes 2000000 | tf_op jit(solution)/shard_map/pallas_call | solution.py:29
  24.2 4.8 %all-to-all-start.1 = ((f32[32,12,128]{2,1,0:T(8,128)}), f32[32,12,128]{2,1,0:T(8,128)S(1)}, u32[]{:S(2)}, u32[]{:S(2)}) async-start(f32[32,12,128]{2,1,0:T(8,128)} %get-tuple-element.37), calls=%async_computation.1 | async-start | bytes 524288 | tf_op jit(solution)/shard_map/all_to_all | solution.py:338
  29.1 3.8 %collective-permute-start = (s32[2,16]{1,0:T(2,128)S(1)}, s32[2,16]{1,0:T(2,128)S(1)}, u32[]{:S(2)}, u32[]{:S(2)}) collective-permute-start(s32[2,16]{1,0:T(2,128)S(1)} %pad_add_fusion.1), channel_id=1, source_target_pairs={{0,1},{1,2},{2,3},{3,4},{4,5},{5,6},{6,7},{7,8},{8,9},{9,10},{10,1... | collective-permute-start | bytes 392 | tf_op jit(solution)/shard_map/ppermute | solution.py:291
  32.9 1.3 collective-permute-start.1
  36.8 1.9 %fusion = s32[1,1]{1,0:T(1,128)} fusion(pred[1,1]{1,0:T(4,128)(4,1)} %bitcast.4, s32[1,1]{1,0:T(1,128)} %bitcast.5, s32[]{:T(128)} %bitcast.6, s32[1,1]{1,0:T(1,128)} %bitcast.3), kind=kLoop, calls=%fused_computation.10 | loop fusion | flops 1 | bytes 17 | tf_op jit(solution)/shard_map/select.3
  38.7 1.4 scatter.9
  40.1 6.3 %shard_map.74 = (f32[3,8192]{1,0:T(4,128)S(1)}, f32[32,12,128]{2,1,0:T(8,128)}) custom-call(s32[5,16]{1,0:T(8,128)S(1)} %pad_add_fusion.ends_ref, f32[3,8192]{1,0:T(4,128)S(1)} %copy-done.1, f32[3,4096]{1,0:T(4,128)S(1)} %collective-permute-done.1.after_ref, f32[3,8192]{1,0:T(4,128)S(1)} %collective-permute-done.2.before_ref, f32[3,2,8192]{2,1,0:T(2,128)S(1)} %bitcast.12, ...), custom_call_target="tpu_custom_call" | custom-call | bytes 2000000 | tf_op jit(solution)/shard_map/pallas_call | solution.py:29
  46.4 6.7 %all-to-all-start = ((f32[32,12,128]{2,1,0:T(8,128)}), f32[32,12,128]{2,1,0:T(8,128)S(1)}, u32[]{:S(2)}, u32[]{:S(2)}) async-start(f32[32,12,128]{2,1,0:T(8,128)} %get-tuple-element.36), calls=%async_computation | async-start | bytes 524288 | tf_op jit(solution)/shard_map/all_to_all | solution.py:338
  53.1 1.3 collective-permute-start.4
  54.4 4.6 %collective-permute-start.3 = (f32[32,12,128]{2,1,0:T(8,128)S(1)}, f32[32,12,128]{2,1,0:T(8,128)S(1)}, u32[]{:S(2)}, u32[]{:S(2)}) collective-permute-start(f32[32,12,128]{2,1,0:T(8,128)S(1)} %all-to-all-done.1.own_ref), channel_id=1, source_target_pairs={{0,1},{1,2},{2,3},{4,5},{5,6},{6,7},{8,9},{9,10},{10,11},{12,13},{... | collective-permute-start | bytes 589832 | tf_op jit(solution)/shard_map/ppermute | solution.py:291
  59.1 6.7 %collective-permute-done.4.above_ref = f32[32,12,128]{2,1,0:T(8,128)S(1)} collective-permute-done((f32[32,12,128]{2,1,0:T(8,128)S(1)}, f32[32,12,128]{2,1,0:T(8,128)S(1)}, u32[]{:S(2)}, u32[]{:S(2)}) %collective-permute-start.4) | collective-permute-done | bytes 196640 | tf_op jit(solution)/shard_map/ppermute | solution.py:291
  65.8 36.2 %shard_map.75 = f32[32,12,128]{2,1,0:T(8,128)} custom-call(s32[2]{0:T(128)S(1)} %add_convert_fusion.ends_ref, s32[512]{0:T(512)S(1)} %copy-done.4, s32[512]{0:T(512)S(1)} %copy-done.5, f32[32,12,128]{2,1,0:T(8,128)S(1)} %all-to-all-done.1.own_ref, f32[32,12,128]{2,1,0:T(8,128)S(1)} %collective-permute-done.3.below_ref, ...), custom_call_target="tpu_custom_call" | custom-call | flops 134217728 | bytes 2000000 | tf_op jit(solution)/shard_map/pallas_call | solution.py:29
  102.0 5.6 %all-to-all-start.3 = ((f32[32,12,128]{2,1,0:T(8,128)}), f32[32,12,128]{2,1,0:T(8,128)S(1)}, u32[]{:S(2)}, u32[]{:S(2)}) async-start(f32[32,12,128]{2,1,0:T(8,128)} %shard_map.75), calls=%async_computation.3 | async-start | bytes 524288 | tf_op jit(solution)/shard_map/all_to_all | solution.py:338
  108.7 1.3 collective-permute-start.6
  110.0 4.6 %collective-permute-start.5 = (f32[32,12,128]{2,1,0:T(8,128)S(1)}, f32[32,12,128]{2,1,0:T(8,128)S(1)}, u32[]{:S(2)}, u32[]{:S(2)}) collective-permute-start(f32[32,12,128]{2,1,0:T(8,128)S(1)} %multiply_add_fusion.own_ref), channel_id=1, source_target_pairs={{0,1},{1,2},{2,3},{4,5},{5,6},{6,7},{8,9},{9,10},{10,11},{12,13},{... | collective-permute-start | bytes 589832 | tf_op jit(solution)/shard_map/ppermute | solution.py:291
  114.6 6.3 %collective-permute-done.6.above_ref = f32[32,12,128]{2,1,0:T(8,128)S(1)} collective-permute-done((f32[32,12,128]{2,1,0:T(8,128)S(1)}, f32[32,12,128]{2,1,0:T(8,128)S(1)}, u32[]{:S(2)}, u32[]{:S(2)}) %collective-permute-start.6) | collective-permute-done | bytes 196640 | tf_op jit(solution)/shard_map/ppermute | solution.py:291
  120.9 36.2 %shard_map.76 = f32[32,12,128]{2,1,0:T(8,128)} custom-call(s32[2]{0:T(128)S(1)} %add_convert_fusion.ends_ref, s32[512]{0:T(512)S(1)} %copy-done.4, s32[512]{0:T(512)S(1)} %copy-done.5, f32[32,12,128]{2,1,0:T(8,128)S(1)} %multiply_add_fusion.own_ref, f32[32,12,128]{2,1,0:T(8,128)S(1)} %collective-permute-done.5.below_ref, ...), custom_call_target="tpu_custom_call" | custom-call | flops 134217728 | bytes 2000000 | tf_op jit(solution)/shard_map/pallas_call | solution.py:29
  157.1 6.0 %all-to-all-start.2 = ((f32[32,12,128]{2,1,0:T(8,128)}), f32[32,12,128]{2,1,0:T(8,128)S(1)}, u32[]{:S(2)}, u32[]{:S(2)}) async-start(f32[32,12,128]{2,1,0:T(8,128)} %shard_map.76), calls=%async_computation.2 | async-start | bytes 524288 | tf_op jit(solution)/shard_map/all_to_all | solution.py:338
  163.2 3.9 %shard_map.77.x_ref = f32[3,8192]{1,0:T(4,128)S(1)} custom-call(s32[64,128]{1,0:T(8,128)S(1)} %get-tuple-element.34.slot_ref, f32[32,12,128]{2,1,0:T(8,128)S(1)} %all-to-all-done.3.source_ref, f32[3,8192]{1,0:T(4,128)S(1)} %get-tuple-element.38.base_ref), custom_call_target="tpu_custom_call" | custom-call | bytes 2000000 | tf_op jit(solution)/shard_map/pallas_call | solution.py:29
  167.1 3.7 %collective-permute-start.8 = (f32[3,8192]{1,0:T(4,128)S(1)}, f32[3,8192]{1,0:T(4,128)S(1)}, u32[]{:S(2)}, u32[]{:S(2)}) collective-permute-start(f32[3,8192]{1,0:T(4,128)S(1)} %shard_map.77.x_ref), channel_id=1, source_target_pairs={{0,1},{1,2},{2,3},{3,4},{4,5},{5,6},{6,7},{7,8},{8,9},{9,10},{10,1... | collective-permute-start | bytes 294920 | tf_op jit(solution)/shard_map/ppermute | solution.py:291
  170.8 1.3 collective-permute-start.7
  172.1 6.3 %collective-permute-done.7.after_ref = f32[3,4096]{1,0:T(4,128)S(1)} collective-permute-done((f32[3,4096]{1,0:T(4,128)S(1)}, f32[3,4096]{1,0:T(4,128)S(1)}, u32[]{:S(2)}, u32[]{:S(2)}) %collective-permute-start.7) | collective-permute-done | bytes 49184 | tf_op jit(solution)/shard_map/ppermute | solution.py:291
  179.6 4.6 %shard_map.79 = f32[3,8192]{1,0:T(4,128)} custom-call(s32[64,128]{1,0:T(8,128)S(1)} %get-tuple-element.34.slot_ref, f32[32,12,128]{2,1,0:T(8,128)S(1)} %all-to-all-done.2.source_ref, f32[3,8192]{1,0:T(4,128)S(1)} %shard_map.78.base_ref), custom_call_target="tpu_custom_call" | custom-call | bytes 2000000 | tf_op jit(solution)/shard_map/pallas_call | solution.py:29
  (39 shorter events, 6.0 us)
Async XLA Ops:
  0.0 40.1 %collective-permute-start.2 = (f32[3,8192]{1,0:T(4,128)}, f32[3,8192]{1,0:T(4,128)S(1)}, u32[]{:S(2)}, u32[]{:S(2)}) collective-permute-start(f32[3,8192]{1,0:T(4,128)} %x_ref.3), channel_id=1, source_target_pairs={{0,1},{1,2},{2,3},{3,4},{4,5},{5,6},{6,7},{7,8},{8,9},{9,10},{10,1... | collective-permute-start | bytes 294920 | tf_op jit(solution)/shard_map/ppermute | solution.py:291
  4.9 0.9 copy-start
  5.8 0.8 copy-start.3
  24.1 4.9 %copy-start.6 = (s32[16]{0:T(128)S(1)}, s32[16]{0:T(128)}, u32[]{:S(2)}) copy-start(s32[16]{0:T(128)} %param.16) | copy-start | bytes 196
  24.1 4.9 %copy-start.7 = (s32[16]{0:T(128)S(1)}, s32[16]{0:T(128)}, u32[]{:S(2)}) copy-start(s32[16]{0:T(128)} %param.17) | copy-start | bytes 196
  24.1 8.7 %copy-start.1 = (f32[3,8192]{1,0:T(4,128)S(1)}, f32[3,8192]{1,0:T(4,128)}, u32[]{:S(2)}) copy-start(f32[3,8192]{1,0:T(4,128)} %x_ref.3) | copy-start | bytes 294916
  24.2 22.3 %all-to-all-start.1 = ((f32[32,12,128]{2,1,0:T(8,128)}), f32[32,12,128]{2,1,0:T(8,128)S(1)}, u32[]{:S(2)}, u32[]{:S(2)}) async-start(f32[32,12,128]{2,1,0:T(8,128)} %get-tuple-element.37), calls=%async_computation.1 | async-start | bytes 524288 | tf_op jit(solution)/shard_map/all_to_all | solution.py:338
  29.0 11.1 %copy-start.2 = (f32[2,3,8192]{2,0,1:T(2,128)S(1)}, f32[2,3,8192]{2,0,1:T(2,128)}, u32[]{:S(2)}) copy-start(f32[2,3,8192]{2,0,1:T(2,128)} %param.12) | copy-start | bytes 589828
  29.1 11.0 %collective-permute-start = (s32[2,16]{1,0:T(2,128)S(1)}, s32[2,16]{1,0:T(2,128)S(1)}, u32[]{:S(2)}, u32[]{:S(2)}) collective-permute-start(s32[2,16]{1,0:T(2,128)S(1)} %pad_add_fusion.1), channel_id=1, source_target_pairs={{0,1},{1,2},{2,3},{3,4},{4,5},{5,6},{6,7},{7,8},{8,9},{9,10},{10,1... | collective-permute-start | bytes 392 | tf_op jit(solution)/shard_map/ppermute | solution.py:291
  32.9 7.2 %collective-permute-start.1 = (f32[3,4096]{1,0:T(4,128)S(1)}, f32[3,4096]{1,0:T(4,128)S(1)}, u32[]{:S(2)}, u32[]{:S(2)}) collective-permute-start(f32[3,4096]{1,0:T(4,128)S(1)} %slice.42), channel_id=1, source_target_pairs={{1,0},{2,1},{3,2},{4,3},{5,4},{6,5},{7,6},{8,7},{9,8},{10,9},{11,1... | collective-permute-start | bytes 147464 | tf_op jit(solution)/shard_map/ppermute | solution.py:291
  46.4 55.6 %all-to-all-start = ((f32[32,12,128]{2,1,0:T(8,128)}), f32[32,12,128]{2,1,0:T(8,128)S(1)}, u32[]{:S(2)}, u32[]{:S(2)}) async-start(f32[32,12,128]{2,1,0:T(8,128)} %get-tuple-element.36), calls=%async_computation | async-start | bytes 524288 | tf_op jit(solution)/shard_map/all_to_all | solution.py:338
  53.1 12.7 %collective-permute-start.4 = (f32[32,12,128]{2,1,0:T(8,128)S(1)}, f32[32,12,128]{2,1,0:T(8,128)S(1)}, u32[]{:S(2)}, u32[]{:S(2)}) collective-permute-start(f32[32,12,128]{2,1,0:T(8,128)S(1)} %all-to-all-done.1.own_ref), channel_id=1, source_target_pairs={{1,0},{2,1},{3,2},{5,4},{6,5},{7,6},{9,8},{10,9},{11,10},{13,12},{... | collective-permute-start | bytes 589832 | tf_op jit(solution)/shard_map/ppermute | solution.py:291
  54.4 11.4 %collective-permute-start.3 = (f32[32,12,128]{2,1,0:T(8,128)S(1)}, f32[32,12,128]{2,1,0:T(8,128)S(1)}, u32[]{:S(2)}, u32[]{:S(2)}) collective-permute-start(f32[32,12,128]{2,1,0:T(8,128)S(1)} %all-to-all-done.1.own_ref), channel_id=1, source_target_pairs={{0,1},{1,2},{2,3},{4,5},{5,6},{6,7},{8,9},{9,10},{10,11},{12,13},{... | collective-permute-start | bytes 589832 | tf_op jit(solution)/shard_map/ppermute | solution.py:291
  59.0 6.8 %copy-start.5 = (s32[512]{0:T(512)S(1)}, s32[512]{0:T(512)}, u32[]{:S(2)}) copy-start(s32[512]{0:T(512)} %cols_ref.3) | copy-start | bytes 6148
  59.0 6.8 %copy-start.4 = (s32[512]{0:T(512)S(1)}, s32[512]{0:T(512)}, u32[]{:S(2)}) copy-start(s32[512]{0:T(512)} %rows_ref.3) | copy-start | bytes 6148
  102.0 55.1 %all-to-all-start.3 = ((f32[32,12,128]{2,1,0:T(8,128)}), f32[32,12,128]{2,1,0:T(8,128)S(1)}, u32[]{:S(2)}, u32[]{:S(2)}) async-start(f32[32,12,128]{2,1,0:T(8,128)} %shard_map.75), calls=%async_computation.3 | async-start | bytes 524288 | tf_op jit(solution)/shard_map/all_to_all | solution.py:338
  108.7 12.2 %collective-permute-start.6 = (f32[32,12,128]{2,1,0:T(8,128)S(1)}, f32[32,12,128]{2,1,0:T(8,128)S(1)}, u32[]{:S(2)}, u32[]{:S(2)}) collective-permute-start(f32[32,12,128]{2,1,0:T(8,128)S(1)} %multiply_add_fusion.own_ref), channel_id=1, source_target_pairs={{1,0},{2,1},{3,2},{5,4},{6,5},{7,6},{9,8},{10,9},{11,10},{13,12},{... | collective-permute-start | bytes 589832 | tf_op jit(solution)/shard_map/ppermute | solution.py:291
  110.0 10.9 %collective-permute-start.5 = (f32[32,12,128]{2,1,0:T(8,128)S(1)}, f32[32,12,128]{2,1,0:T(8,128)S(1)}, u32[]{:S(2)}, u32[]{:S(2)}) collective-permute-start(f32[32,12,128]{2,1,0:T(8,128)S(1)} %multiply_add_fusion.own_ref), channel_id=1, source_target_pairs={{0,1},{1,2},{2,3},{4,5},{5,6},{6,7},{8,9},{9,10},{10,11},{12,13},{... | collective-permute-start | bytes 589832 | tf_op jit(solution)/shard_map/ppermute | solution.py:291
  157.1 22.5 %all-to-all-start.2 = ((f32[32,12,128]{2,1,0:T(8,128)}), f32[32,12,128]{2,1,0:T(8,128)S(1)}, u32[]{:S(2)}, u32[]{:S(2)}) async-start(f32[32,12,128]{2,1,0:T(8,128)} %shard_map.76), calls=%async_computation.2 | async-start | bytes 524288 | tf_op jit(solution)/shard_map/all_to_all | solution.py:338
  167.1 11.3 %collective-permute-start.8 = (f32[3,8192]{1,0:T(4,128)S(1)}, f32[3,8192]{1,0:T(4,128)S(1)}, u32[]{:S(2)}, u32[]{:S(2)}) collective-permute-start(f32[3,8192]{1,0:T(4,128)S(1)} %shard_map.77.x_ref), channel_id=1, source_target_pairs={{0,1},{1,2},{2,3},{3,4},{4,5},{5,6},{6,7},{7,8},{8,9},{9,10},{10,1... | collective-permute-start | bytes 294920 | tf_op jit(solution)/shard_map/ppermute | solution.py:291
  170.8 7.6 %collective-permute-start.7 = (f32[3,4096]{1,0:T(4,128)S(1)}, f32[3,4096]{1,0:T(4,128)S(1)}, u32[]{:S(2)}, u32[]{:S(2)}) collective-permute-start(f32[3,4096]{1,0:T(4,128)S(1)} %slice.44), channel_id=1, source_target_pairs={{1,0},{2,1},{3,2},{4,3},{5,4},{6,5},{7,6},{8,7},{9,8},{10,9},{11,1... | collective-permute-start | bytes 147464 | tf_op jit(solution)/shard_map/ppermute | solution.py:291

commit v2 on v1

v2 whole, which is shorter than its diff:
```python
import functools
import math

import jax
import jax.numpy as jnp
from jax import lax
from jax.experimental import pallas as pl
from jax.experimental.pallas import tpu as pltpu
from jax.sharding import PartitionSpec as P

time_step = 0.05
bond_stiff = 1.0
loop_stiff = 2.0
cutoff_sq = 2.25
contact_coef = 0.4 / 2.25
noise_gain = math.sqrt(0.1)
longest_loop = 4096
lanes = 128
far_away = 1e15
pairs_at_once = 32

vmem = pl.BlockSpec(memory_space=pltpu.VMEM)
smem = pl.BlockSpec(memory_space=pltpu.SMEM)
both = ("chain", "space")
f32 = jnp.float32
bf16 = jnp.bfloat16


def call(body, outs, in_specs, args, scratch=(), flops=0, moved=2_000_000):
    many = isinstance(outs, list)
    return pl.pallas_call(
        body,
        out_shape=outs,
        in_specs=in_specs,
        out_specs=[vmem] * len(outs) if many else vmem,
        scratch_shapes=list(scratch),
        compiler_params=pltpu.CompilerParams(vmem_limit_bytes=32 * 1024 * 1024),
        cost_estimate=pl.CostEstimate(flops=flops, bytes_accessed=moved, transcendentals=0),
    )(*args)


def iota(shape, dim):
    return lax.broadcasted_iota(jnp.int32, shape, dim)


def pick(row, where_to):
    return jnp.take_along_axis(
        jnp.broadcast_to(row, where_to.shape), where_to, axis=1, mode="promise_in_bounds"
    )


def fill_slots(index_ref, source_ref, per_owner, store):
    rows = source_ref.shape[1] // lanes
    fields = source_ref.shape[0]
    owners_here = 8 // per_owner

    def one(group, carry):
        code = index_ref[pl.ds(pl.multiple_of(group * 8, 8), 8), :]
        row_of = (code >> 7) - 1
        lane_of = code & 127
        held = [jnp.full((8, lanes), far_away, f32) for _ in range(fields)]
        for j in range(rows):
            here = row_of == j
            for c in range(fields):
                row = source_ref[c : c + 1, j * lanes : (j + 1) * lanes]
                held[c] = jnp.where(here, pick(row, lane_of), held[c])
        for i in range(owners_here):
            for c in range(fields):
                store(group * owners_here + i, c, held[c][i * per_owner : (i + 1) * per_owner, :])
        return carry

    lax.fori_loop(0, index_ref.shape[0] // 8, one, 0)


def index_kernel(slabs, owner_ref, x_ref, out_ref, index_ref, slot_ref, turned_ref, total_ref):
    rows = owner_ref.shape[0]
    devices = out_ref.shape[0]
    per_owner = out_ref.shape[1] // 9
    own = owner_ref[...]
    lane = iota((rows, lanes), 1)
    tri = jnp.where(
        iota((lanes, 2 * lanes), 1) >= lanes,
        1.0,
        jnp.where(iota((lanes, 2 * lanes), 0) < iota((lanes, 2 * lanes), 1), 1.0, 0.0),
    ).astype(bf16)

    def count(chunk, carry):
        prefix, total = carry
        masks = jnp.concatenate(
            [jnp.where(own == chunk * 8 + i, 1.0, 0.0) for i in range(8)], axis=0
        ).astype(bf16)
        sums = jnp.dot(masks, tri, preferred_element_type=f32)
        for i in range(8):
            o = chunk * 8 + i
            part = sums[i * rows : (i + 1) * rows]
            prefix = jnp.where(own == o, part[:, :lanes], prefix)
            total = jnp.where(lane == o, part[:, lanes:], total)
        return prefix, total

    zero = jnp.zeros((rows, lanes), f32)
    prefix, total = lax.fori_loop(0, devices // 8, count, (zero, zero))
    lower = jnp.where(iota((rows, rows), 1) < iota((rows, rows), 0), 1.0, 0.0).astype(bf16)
    above = jnp.dot(lower, total.astype(bf16), preferred_element_type=f32)
    offset = jnp.take_along_axis(above, own, axis=1, mode="promise_in_bounds")
    slot = own * (per_owner * lanes) + (prefix + offset).astype(jnp.int32)
    slot_ref[...] = slot

    turned_ref[...] = jnp.concatenate([slot & 127] * (lanes // rows), axis=0).T
    down = iota((lanes, lanes), 0)
    across = iota((lanes, lanes), 1)
    lane_code = across.astype(f32)
    total_ref[...] = jnp.zeros_like(total_ref)
    at_once = 8

    def spread(chunk, carry):
        left, right = [], []
        low = turned_ref[...]
        low = jnp.where(chunk > 0, pltpu.roll(low, lanes - chunk * at_once, 1), low)
        for i in range(at_once):
            j = chunk * at_once + i
            high = (slot_ref[pl.ds(j, 1), :] >> 7) == down
            row_code = (j + 1).astype(f32)
            left.append(
                jnp.concatenate(
                    [jnp.where(high, lane_code, 0.0), jnp.where(high, row_code, 0.0)], axis=0
                ).astype(bf16)
            )
            right.append(jnp.where(low[:, i : i + 1] == across, 1.0, 0.0).astype(bf16))
        total_ref[...] += jnp.dot(
            jnp.concatenate(left, axis=1),
            jnp.concatenate(right, axis=0),
            preferred_element_type=f32,
        )
        return carry

    lax.fori_loop(0, rows // at_once, spread, 0)
    blocks = index_ref.shape[0]
    index_ref[...] = (total_ref[0:blocks, :] + lanes * total_ref[blocks:, :]).astype(jnp.int32)

    def store(owner, c, values):
        place = lax.rem(owner, slabs)
        width = 3 * per_owner
        at = c * per_owner
        up = lax.rem(owner + 1, devices)
        below = lax.rem(owner + devices - 1, devices)
        out_ref[owner, width + at : width + at + per_owner, :] = values
        out_ref[up, at : at + per_owner, :] = jnp.where(place < slabs - 1, values, far_away)
        out_ref[below, 2 * width + at : 2 * width + at + per_owner, :] = jnp.where(
            place > 0, values, far_away
        )

    fill_slots(index_ref, x_ref, per_owner, store)


def chain_forces(left_ref, span_ref, x_ref, after_ref, before_ref, anchors_ref, wide_ref, force_ref):
    mono_dev = x_ref.shape[1]
    blocks = mono_dev // lanes
    extruders = left_ref.shape[0]
    count = lax.axis_size("chain") * lax.axis_size("space")
    me = lax.axis_index("chain") * lax.axis_size("space") + lax.axis_index("space")
    wide_ref[...] = jnp.zeros_like(wide_ref)
    wide_ref[0:3, 0:lanes] = before_ref[0:3, mono_dev - lanes :]
    wide_ref[0:3, lanes : lanes + mono_dev] = x_ref[...]
    wide_ref[0:3, lanes + mono_dev :] = after_ref[...]
    lane = iota((8, lanes), 1)
    has_before = (me > 0).astype(f32)
    has_after = (me < count - 1).astype(f32)
    for j in range(blocks):
        here = wide_ref[:, (j + 1) * lanes : (j + 2) * lanes]
        left = wide_ref[:, j * lanes : (j + 1) * lanes]
        right = wide_ref[:, (j + 2) * lanes : (j + 3) * lanes]
        down = pltpu.roll(jnp.where(lane == lanes - 1, left, here), 1, 1) - here
        up = pltpu.roll(jnp.where(lane == 0, right, here), lanes - 1, 1) - here
        if j == 0:
            down = jnp.where(lane == 0, down * has_before, down)
        if j == blocks - 1:
            up = jnp.where(lane == lanes - 1, up * has_after, up)
        force_ref[:, j * lanes : (j + 1) * lanes] = bond_stiff * down + bond_stiff * up

    def window(ref, at):
        return ref.at[:, pl.ds(pl.multiple_of((at >> 7) * lanes, lanes), lanes)]

    def value(block, at):
        there = iota(block.shape, 1) == (at & 127)
        return jnp.sum(jnp.where(there, block, 0.0), axis=1, keepdims=True)

    todo = []
    for e in range(extruders):
        a = left_ref[e] - me * mono_dev
        b = a + span_ref[e]
        pull = loop_stiff * (
            value(window(wide_ref, b + lanes)[...], b) - value(window(wide_ref, a + lanes)[...], a)
        )
        todo.append((a, pull))
        todo.append((jnp.minimum(b, mono_dev - 1), jnp.where(b < mono_dev, -pull, 0.0)))
    for e in range(extruders):
        a = anchors_ref[0, e] - (me - 1) * mono_dev
        b = a + anchors_ref[1, e] - mono_dev
        wanted = jnp.logical_and(b >= 0, me > 0)
        a = jnp.where(wanted, a, 0)
        b = jnp.where(wanted, b, 0)
        far_end = value(window(before_ref, a)[0:3, :], a)
        pull = loop_stiff * (value(window(wide_ref, b + lanes)[...], b)[0:3] - far_end)
        pull = jnp.where(wanted, -pull, 0.0)
        todo.append((b, jnp.concatenate([pull, jnp.zeros((5, 1), f32)], axis=0)))
    for at, pull in todo:
        spot = window(force_ref, at)
        spot[...] = spot[...] + jnp.where(lane == (at & 127), pull, 0.0)


def chain_kernel(
    step, left_ref, span_ref, anchors_ref, x_ref, after_ref, before_ref, noise_ref, base_ref, out_ref, wide_ref, force_ref
):
    chain_forces(left_ref, span_ref, x_ref, after_ref, before_ref, anchors_ref, wide_ref, force_ref)
    for c in range(3):
        out_ref[c : c + 1, :] = (
            base_ref[c : c + 1, :]
            + time_step * force_ref[c : c + 1, :]
            + noise_gain * noise_ref[c, step : step + 1, :]
        )


def first_kernel(
    left_ref, span_ref, anchors_ref, x_ref, after_ref, before_ref, noise_ref, index_ref, out_ref, y_ref, wide_ref, force_ref
):
    chain_kernel(
        0, left_ref, span_ref, anchors_ref, x_ref, after_ref, before_ref, noise_ref, x_ref, y_ref, wide_ref, force_ref
    )
    per_owner = out_ref.shape[1] // 3

    def store(owner, c, values):
        out_ref[owner, c * per_owner : (c + 1) * per_owner, :] = values

    fill_slots(index_ref, y_ref, per_owner, store)


def pieces(x):
    high = x.astype(bf16).astype(f32)
    middle = (x - high).astype(bf16).astype(f32)
    return high, middle, x - high - middle


def contact_kernel(merged, rows_ref, cols_ref, *refs):
    if merged:
        cells_ref, refs = refs[0], refs[1:]
        width = cells_ref.shape[1] // 3
        sides = [(cells_ref, 0), (cells_ref, width), (cells_ref, 2 * width)]
    else:
        sides = [(refs[0], 0), (refs[1], 0), (refs[2], 0)]
        width = refs[0].shape[1]
        refs = refs[3:]
    out_ref, refs = refs[0], refs[1:]
    far_t, far_x, near_t, stage, cap, total = refs
    devices = out_ref.shape[0]
    per_owner = width // 3
    blocks = devices * per_owner
    owners = 8 // per_owner
    scale = 1.0 / math.sqrt(cutoff_sq)
    place = lax.axis_index("space")
    has_below = place > 0
    has_above = place < lax.axis_size("space") - 1
    cap[0:lanes, :] = jnp.full((lanes, lanes), 1e30, f32)
    cap[lanes:, :] = jnp.where(iota((lanes, lanes), 0) == iota((lanes, lanes), 1), 0.0, 1e30)
    stage[...] = jnp.zeros_like(stage)
    total[...] = jnp.zeros_like(total)

    def eight(ref, first, group, c):
        at = first + c * per_owner
        return jnp.concatenate(
            [ref[group * owners + i, at : at + per_owner, :] for i in range(owners)], axis=0
        )

    def build(group, carry):
        for side, valid in enumerate((has_below, None, has_above)):
            ref, first = sides[side]
            xs = [eight(ref, first, group, c) for c in range(3)]
            live = xs[0] < 0.5 * far_away
            if valid is not None:
                live = jnp.logical_and(live, jnp.full((8, lanes), valid.astype(jnp.int32)) > 0)
            xs = [jnp.where(live, x, 0.0) * scale for x in xs]
            square = xs[0] * xs[0] + xs[1] * xs[1] + xs[2] * xs[2]
            high, middle, low = [list(part) for part in zip(*[pieces(x) for x in xs])]
            one = [jnp.ones((8, lanes), f32)] * 3
            spot = stage.at[side]
            far = high + middle + high + list(pieces(jnp.where(live, -square, -1e9))) + one
            for f, v in enumerate(far):
                spot[pl.ds(f, 8, stride=16), :] = v
            at = pl.ds(pl.multiple_of((side * blocks + group * 8) * 16, lanes), lanes)
            far_t[at, :] = spot[...].astype(bf16).T
            for f in range(3):
                spot[pl.ds(6 + f, 8, stride=16), :] = low[f]
            far_x[at, :] = spot[...].astype(bf16)
            if side == 1:
                spot = stage.at[3]
                near = [2.0 * v for v in high + high + middle] + one
                near += list(pieces(jnp.where(live, 1.0 - square, -1e9)))
                for f, v in enumerate(near):
                    spot[pl.ds(f, 8, stride=16), :] = v
                near_t[pl.ds(pl.multiple_of(group * lanes, lanes), lanes), :] = spot[...].astype(bf16)
        return carry

    lax.fori_loop(0, blocks // 8, build, 0)
    zero = jnp.zeros((lanes, lanes), bf16)

    def sixteen(ref, block):
        return ref[pl.ds(pl.multiple_of(block * 16, 16), 16), :]

    pairs = min(pairs_at_once, rows_ref.shape[0] // 2)

    def tiles(step, carry):
        results = []
        for pair in range(pairs):
            first = (step * pairs + pair) * 2
            ids = [(rows_ref[first + i], cols_ref[first + i]) for i in range(2)]
            left, right = [], []
            for r, q in ids:
                near = sixteen(near_t, r)
                right.append(
                    jnp.concatenate(
                        [jnp.where((q & 7) == k, near, jnp.zeros_like(near)) for k in range(8)], axis=0
                    )
                )
                left.append(far_t[pl.ds(pl.multiple_of((q >> 3) * lanes, lanes), lanes), :])
            right = jnp.concatenate(
                [jnp.concatenate([right[0], zero], axis=1), jnp.concatenate([zero, right[1]], axis=1)],
                axis=0,
            )
            reach = jnp.dot(jnp.concatenate(left, axis=1), right, preferred_element_type=f32)
            for i, (r, q) in enumerate(ids):
                same = (q == r + blocks).astype(jnp.int32)
                most = cap[pl.ds(pl.multiple_of(same * lanes, lanes), lanes), :]
                w = jnp.maximum(jnp.minimum(reach[:, i * lanes : (i + 1) * lanes], most), 0.0).astype(bf16)
                results.append((r, jnp.dot(sixteen(far_x, q), w, preferred_element_type=f32)))
        for r, v in results:
            spot = total.at[pl.ds(pl.multiple_of(r * 16, 16), 16), :]
            spot[...] = spot[...] + v
        return carry

    lax.fori_loop(0, rows_ref.shape[0] // (2 * pairs), tiles, 0)
    back = contact_coef * math.sqrt(cutoff_sq)

    def finish(group, carry):
        sums = [total[pl.ds(group * lanes + f, 8, stride=16), :] for f in range(13)]
        for c in range(3):
            place = eight(sides[1][0], sides[1][1], group, c)
            here = jnp.where(place < 0.5 * far_away, place, 0.0) * scale
            force = (here * sums[12] - (sums[c] + sums[3 + c] + sums[6 + c])) * back
            for i in range(owners):
                out_ref[group * owners + i, c * per_owner : (c + 1) * per_owner, :] = force[
                    i * per_owner : (i + 1) * per_owner
                ]
        return carry

    lax.fori_loop(0, blocks // 8, finish, 0)


def gather_kernel(slot_ref, source_ref, *refs):
    base_ref, out_ref = refs if len(refs) == 2 else (None, refs[0])
    per_owner = source_ref.shape[1] // 3

    def one(group, carry):
        slot = slot_ref[pl.ds(pl.multiple_of(group * 8, 8), 8), :]
        row_of = slot >> 7
        lane_of = slot & 127
        held = [jnp.zeros((8, lanes), f32) for _ in range(3)]
        for s in range(source_ref.shape[0] * per_owner):
            here = row_of == s
            for c in range(3):
                at = c * per_owner + s % per_owner
                row = source_ref[s // per_owner, at : at + 1, :]
                held[c] = jnp.where(here, pick(row, lane_of), held[c])
        for i in range(8):
            at = pl.ds(pl.multiple_of((group * 8 + i) * lanes, lanes), lanes)
            for c in range(3):
                value = held[c][i : i + 1, :]
                if base_ref is not None:
                    value = base_ref[c : c + 1, at] + time_step * value
                out_ref[c : c + 1, at] = value
        return carry

    lax.fori_loop(0, slot_ref.shape[0] // 8, one, 0)


def shifted(value, axis, steps):
    count = lax.axis_size(axis)
    first, last = (max(0, -steps), min(count, count - steps))
    return lax.ppermute(value, axis, [(source, source + steps) for source in range(first, last)])


def local(positions, noise, cell_owner, tile_rows, tile_cols, loop_left, loop_span):
    devices = lax.axis_size(both)
    mono_dev = positions.shape[1]
    per_owner = 2 * mono_dev // devices // lanes
    rows = mono_dev // lanes
    blocks = devices * per_owner
    noise_t = noise.transpose(1, 0, 2)

    sent = jax.ShapeDtypeStruct((devices, 3 * per_owner, lanes), f32)
    chain = jax.ShapeDtypeStruct((3, mono_dev), f32)
    chain_scratch = [
        pltpu.VMEM((8, lanes + mono_dev + longest_loop), f32),
        pltpu.VMEM((8, mono_dev), f32),
    ]

    def exchange(value):
        return lax.all_to_all(value, both, split_axis=0, concat_axis=0, tiled=True)

    def contact(merged, cells):
        return call(
            functools.partial(contact_kernel, merged),
            sent,
            [smem, smem] + [vmem] * len(cells),
            (tile_rows, tile_cols, *cells),
            [
                pltpu.VMEM((3 * blocks * 16, lanes), bf16),
                pltpu.VMEM((3 * blocks * 16, lanes), bf16),
                pltpu.VMEM((blocks * 16, lanes), bf16),
                pltpu.VMEM((4, lanes, lanes), f32),
                pltpu.VMEM((2 * lanes, lanes), f32),
                pltpu.VMEM((blocks * 16, lanes), f32),
            ],
            flops=16 * tile_rows.shape[0] * lanes * lanes,
        )

    anchors_before = shifted(jnp.stack([loop_left, loop_span]), both, 1)
    before = shifted(positions, both, 1)
    after = shifted(positions[:, :longest_loop], both, -1)
    x_out, index, slot = call(
        functools.partial(index_kernel, lax.axis_size("space")),
        [
            jax.ShapeDtypeStruct((devices, 9 * per_owner, lanes), f32),
            jax.ShapeDtypeStruct((blocks, lanes), jnp.int32),
            jax.ShapeDtypeStruct((rows, lanes), jnp.int32),
        ],
        [vmem, vmem],
        (cell_owner.reshape(rows, lanes), positions),
        [pltpu.VMEM((lanes, lanes), jnp.int32), pltpu.VMEM((2 * blocks, lanes), f32)],
    )
    x_cells = exchange(x_out)
    y_out = call(
        first_kernel,
        sent,
        [smem] * 3 + [vmem] * 5,
        (loop_left, loop_span, anchors_before, positions, after, before, noise_t, index),
        [pltpu.VMEM((3, mono_dev), f32)] + chain_scratch,
    )
    y_cells = exchange(y_out)
    contact0 = contact(True, (x_cells,))
    x1_cells = y_cells + time_step * contact0
    below = shifted(x1_cells, "space", 1)
    above = shifted(x1_cells, "space", -1)
    x1_back = exchange(x1_cells)
    contact1 = contact(False, (below, x1_cells, above))
    back1 = exchange(contact1)

    x1 = call(gather_kernel, chain, [vmem] * 2, (slot, x1_back))
    before1 = shifted(x1, both, 1)
    after1 = shifted(x1[:, :longest_loop], both, -1)
    pushed = call(gather_kernel, chain, [vmem] * 3, (slot, back1, x1))
    return call(
        functools.partial(chain_kernel, 1),
        chain,
        [smem] * 3 + [vmem] * 5,
        (loop_left, loop_span, anchors_before, x1, after1, before1, noise_t, pushed),
        chain_scratch,
    )


def solution(mesh):
    in_specs = (
        P(None, ("chain", "space")),
        P(None, None, ("chain", "space")),
        P(("chain", "space"), None),
        P(("chain", "space")),
        P(("chain", "space")),
        P(("chain", "space")),
        P(("chain", "space")),
    )
    out_specs = P(None, ("chain", "space"))
    return jax.shard_map(local, mesh=mesh, in_specs=in_specs, out_specs=out_specs, check_vma=False)
```

time: 185 us -> 126 us (0.68)
  Pallas kernels: 106 us -> 58 us
  waiting for transfers between devices: 19.4 us -> 13.5 us
  other arithmetic: 4.27 us -> 0.75 us
    pallas_call x7, Pallas kernels: 106 us -> 58 us  [call(): pl.pallas_call(body, out_shape=outs, in_specs=in_specs, out_specs=[vmem]...]
    ppermute x9 -> x7, waiting for transfers between devices: 19.4 us -> 12.2 us  [shifted(): lax.ppermute(value, axis, [(source, source + steps) for source in range(f...]
    ppermute x9 -> x7, starting transfers between devices: 26.7 us -> 20.3 us  [shifted(): lax.ppermute(value, axis, [(source, source + steps) for source in range(f...]
    all_to_all x4, starting transfers between devices: 23.2 us -> 29.3 us  [exchange(): return lax.all_to_all(value, both, split_axis=0, concat_axis=0, tiled=True)]
    another operation x5 -> x1, other arithmetic: 3.17 us -> 0.01 us  [local(): anchors_before = shifted(jnp.stack([loop_left, loop_span]), both, 1)]
  transfers between devices with their start and end apart: 13 -> 11, of which waited for: 3 -> 4; matrix products, arithmetic and copies ran while one was open for 3% -> 0% of each run, Pallas kernels for 55% -> 36%
where the time goes in v2:
time: 126 us; the launch traced here: 124 us
  Pallas kernels  58 us (46%)
  starting transfers between devices  49.6 us (39%)
  waiting for transfers between devices  13.5 us (11%)
  local copies, waits for them, and re-layouts  2.36 us (2%)
    pallas_call x7, Pallas kernels, call(): pl.pallas_call(body, out_shape=outs, in_specs=in_specs, out_specs=[vmem]...  58 us
    all_to_all x4, starting transfers between devices, exchange(): return lax.all_to_all(value, both, split_axis=0, concat_axis=0, tiled=True)  29.3 us
    ppermute x7, starting transfers between devices, shifted(): lax.ppermute(value, axis, [(source, source + steps) for source in range(f...  20.3 us
    ppermute x7, waiting for transfers between devices, shifted(): lax.ppermute(value, axis, [(source, source + steps) for source in range(f...  12.2 us
  transfers between devices with their start and end apart: 11, of which 4 were waited for; matrix products, arithmetic and copies ran while one was open for 0% of the time, Pallas kernels for 36%

profile of v2, /device:TPU:0, one launch (start us, length us, event | category | flops | bytes accessed | tf_op | source)
XLA Modules:
  0.0 124.4 jit_solution(10208589980764951067)
XLA Ops:
  0.0 0.9 copy-done
  0.9 0.8 copy-done.3
  1.7 11.3 %shard_map.73 = (f32[32,36,128]{2,1,0:T(8,128)}, s32[128,128]{1,0:T(8,128)S(1)}, s32[64,128]{1,0:T(8,128)S(1)}) custom-call(s32[64,128]{1,0:T(8,128)S(1)} %bitcast.6, f32[3,8192]{1,0:T(4,128)S(1)} %copy-done), custom_call_target="tpu_custom_call" | custom-call | bytes 2000000 | tf_op jit(solution)/shard_map/pallas_call | solution.py:31
  12.9 7.3 %all-to-all-start.1 = ((f32[32,36,128]{2,1,0:T(8,128)}), f32[32,36,128]{2,1,0:T(8,128)S(1)}, u32[]{:S(2)}, u32[]{:S(2)}) async-start(f32[32,36,128]{2,1,0:T(8,128)} %get-tuple-element.10), calls=%async_computation.1 | async-start | bytes 1310720 | tf_op jit(solution)/shard_map/all_to_all | solution.py:406
  20.2 3.7 %collective-permute-start.2 = (f32[3,8192]{1,0:T(4,128)S(1)}, f32[3,8192]{1,0:T(4,128)S(1)}, u32[]{:S(2)}, u32[]{:S(2)}) collective-permute-start(f32[3,8192]{1,0:T(4,128)S(1)} %copy-done.1), channel_id=1, source_target_pairs={{0,1},{1,2},{2,3},{3,4},{4,5},{5,6},{6,7},{7,8},{8,9},{9,10},{10,1... | collective-permute-start | bytes 294920 | tf_op jit(solution)/shard_map/ppermute | solution.py:387
  23.9 1.3 %collective-permute-start.1 = (f32[3,4096]{1,0:T(4,128)S(1)}, f32[3,4096]{1,0:T(4,128)S(1)}, u32[]{:S(2)}, u32[]{:S(2)}) collective-permute-start(f32[3,4096]{1,0:T(4,128)S(1)} %slice.6), channel_id=1, source_target_pairs={{1,0},{2,1},{3,2},{4,3},{5,4},{6,5},{7,6},{8,7},{9,8},{10,9},{11,1... | collective-permute-start | bytes 147464 | tf_op jit(solution)/shard_map/ppermute | solution.py:387
  25.9 4.5 %collective-permute-start = (s32[2,16]{1,0:T(2,128)S(1)}, s32[2,16]{1,0:T(2,128)S(1)}, u32[]{:S(2)}, u32[]{:S(2)}) collective-permute-start(s32[2,16]{1,0:T(2,128)S(1)} %pad_add_fusion), channel_id=1, source_target_pairs={{0,1},{1,2},{2,3},{3,4},{4,5},{5,6},{6,7},{7,8},{8,9},{9,10},{10,1... | collective-permute-start | bytes 392 | tf_op jit(solution)/shard_map/ppermute | solution.py:387
  30.5 4.2 %collective-permute-done.anchors_ref = s32[2,16]{1,0:T(2,128)S(1)} collective-permute-done((s32[2,16]{1,0:T(2,128)S(1)}, s32[2,16]{1,0:T(2,128)S(1)}, u32[]{:S(2)}, u32[]{:S(2)}) %collective-permute-start) | collective-permute-done | bytes 160 | tf_op jit(solution)/shard_map/ppermute | solution.py:387
  34.6 6.4 %shard_map.74 = f32[32,12,128]{2,1,0:T(8,128)} custom-call(s32[16]{0:T(128)S(1)} %copy-done.6, s32[16]{0:T(128)S(1)} %copy-done.7, s32[2,16]{1,0:T(2,128)S(1)} %collective-permute-done.anchors_ref, f32[3,8192]{1,0:T(4,128)S(1)} %copy-done.1, f32[3,4096]{1,0:T(4,128)S(1)} %collective-permute-done.1.after_ref, ...), custom_call_target="tpu_custom_call" | custom-call | bytes 2000000 | tf_op jit(solution)/shard_map/pallas_call | solution.py:31
  41.0 10.4 %all-to-all-start = ((f32[32,12,128]{2,1,0:T(8,128)}), f32[32,12,128]{2,1,0:T(8,128)S(1)}, u32[]{:S(2)}, u32[]{:S(2)}) async-start(f32[32,12,128]{2,1,0:T(8,128)} %shard_map.74), calls=%async_computation | async-start | bytes 524288 | tf_op jit(solution)/shard_map/all_to_all | solution.py:406
  51.4 14.8 %shard_map.75 = f32[32,12,128]{2,1,0:T(8,128)S(1)} custom-call(s32[512]{0:T(512)S(1)} %copy-done.4, s32[512]{0:T(512)S(1)} %copy-done.5, f32[32,36,128]{2,1,0:T(8,128)S(1)} %all-to-all-done.1.refs_0_), custom_call_target="tpu_custom_call" | custom-call | flops 134217728 | bytes 2000000 | tf_op jit(solution)/shard_map/pallas_call | solution.py:31
  67.0 5.8 %all-to-all-start.2 = ((f32[32,12,128]{2,1,0:T(8,128)}), f32[32,12,128]{2,1,0:T(8,128)S(1)}, u32[]{:S(2)}, u32[]{:S(2)}) async-start(f32[32,12,128]{2,1,0:T(8,128)} %multiply_add_fusion.refs_1_), calls=%async_computation.2 | async-start | bytes 524288 | tf_op jit(solution)/shard_map/all_to_all | solution.py:406
  72.9 1.3 %collective-permute-start.6 = (f32[32,12,128]{2,1,0:T(8,128)}, f32[32,12,128]{2,1,0:T(8,128)S(1)}, u32[]{:S(2)}, u32[]{:S(2)}) collective-permute-start(f32[32,12,128]{2,1,0:T(8,128)} %multiply_add_fusion.refs_1_), channel_id=1, source_target_pairs={{1,0},{2,1},{3,2},{5,4},{6,5},{7,6},{9,8},{10,9},{11,10},{13,12},{... | collective-permute-start | bytes 589832 | tf_op jit(solution)/shard_map/ppermute | solution.py:387
  74.2 4.6 %collective-permute-start.5 = (f32[32,12,128]{2,1,0:T(8,128)}, f32[32,12,128]{2,1,0:T(8,128)S(1)}, u32[]{:S(2)}, u32[]{:S(2)}) collective-permute-start(f32[32,12,128]{2,1,0:T(8,128)} %multiply_add_fusion.refs_1_), channel_id=1, source_target_pairs={{0,1},{1,2},{2,3},{4,5},{5,6},{6,7},{8,9},{9,10},{10,11},{12,13},{... | collective-permute-start | bytes 589832 | tf_op jit(solution)/shard_map/ppermute | solution.py:387
  78.8 6.9 %collective-permute-done.6.refs_2_ = f32[32,12,128]{2,1,0:T(8,128)S(1)} collective-permute-done((f32[32,12,128]{2,1,0:T(8,128)}, f32[32,12,128]{2,1,0:T(8,128)S(1)}, u32[]{:S(2)}, u32[]{:S(2)}) %collective-permute-start.6) | collective-permute-done | bytes 196640 | tf_op jit(solution)/shard_map/ppermute | solution.py:387
  85.7 15.9 %shard_map.77 = f32[32,12,128]{2,1,0:T(8,128)} custom-call(s32[512]{0:T(512)S(1)} %copy-done.4, s32[512]{0:T(512)S(1)} %copy-done.5, f32[32,12,128]{2,1,0:T(8,128)S(1)} %collective-permute-done.5.refs_0_, f32[32,12,128]{2,1,0:T(8,128)} %multiply_add_fusion.refs_1_, f32[32,12,128]{2,1,0:T(8,128)S(1)} %collective-permute-done.6.refs_2_), custom_call_target="tpu_custom_call" | custom-call | flops 134217728 | bytes 2000000 | tf_op jit(solution)/shard_map/pallas_call | solution.py:31
  101.6 5.8 %all-to-all-start.3 = ((f32[32,12,128]{2,1,0:T(8,128)}), f32[32,12,128]{2,1,0:T(8,128)S(1)}, u32[]{:S(2)}, u32[]{:S(2)}) async-start(f32[32,12,128]{2,1,0:T(8,128)} %shard_map.77), calls=%async_computation.3 | async-start | bytes 524288 | tf_op jit(solution)/shard_map/all_to_all | solution.py:406
  107.4 3.9 %shard_map.76.refs_0_.x_ref = f32[3,8192]{1,0:T(4,128)S(1)} custom-call(s32[64,128]{1,0:T(8,128)S(1)} %get-tuple-element.8.slot_ref, f32[32,12,128]{2,1,0:T(8,128)S(1)} %all-to-all-done.2.source_ref), custom_call_target="tpu_custom_call" | custom-call | bytes 2000000 | tf_op jit(solution)/shard_map/pallas_call | solution.py:31
  111.2 3.7 %collective-permute-start.4 = (f32[3,8192]{1,0:T(4,128)S(1)}, f32[3,8192]{1,0:T(4,128)S(1)}, u32[]{:S(2)}, u32[]{:S(2)}) collective-permute-start(f32[3,8192]{1,0:T(4,128)S(1)} %shard_map.76.refs_0_.x_ref), channel_id=1, source_target_pairs={{0,1},{1,2},{2,3},{3,4},{4,5},{5,6},{6,7},{7,8},{8,9},{9,10},{10,1... | collective-permute-start | bytes 294920 | tf_op jit(solution)/shard_map/ppermute | solution.py:387
  115.0 1.3 %collective-permute-start.3 = (f32[3,4096]{1,0:T(4,128)S(1)}, f32[3,4096]{1,0:T(4,128)S(1)}, u32[]{:S(2)}, u32[]{:S(2)}) collective-permute-start(f32[3,4096]{1,0:T(4,128)S(1)} %slice.8), channel_id=1, source_target_pairs={{1,0},{2,1},{3,2},{4,3},{5,4},{6,5},{7,6},{8,7},{9,8},{10,9},{11,1... | collective-permute-start | bytes 147464 | tf_op jit(solution)/shard_map/ppermute | solution.py:387
  116.3 1.3 %all-to-all-done.3.source_ref = f32[32,12,128]{2,1,0:T(8,128)S(1)} async-done(((f32[32,12,128]{2,1,0:T(8,128)}), f32[32,12,128]{2,1,0:T(8,128)S(1)}, u32[]{:S(2)}, u32[]{:S(2)}) %all-to-all-start.3) | async-done | bytes 196640 | tf_op jit(solution)/shard_map/all_to_all | solution.py:406
  117.6 3.9 %shard_map.78.base_ref = f32[3,8192]{1,0:T(4,128)S(1)} custom-call(s32[64,128]{1,0:T(8,128)S(1)} %get-tuple-element.8.slot_ref, f32[32,12,128]{2,1,0:T(8,128)S(1)} %all-to-all-done.3.source_ref, f32[3,8192]{1,0:T(4,128)S(1)} %shard_map.76.refs_0_.x_ref), custom_call_target="tpu_custom_call" | custom-call | bytes 2000000 | tf_op jit(solution)/shard_map/pallas_call | solution.py:31
  121.5 1.1 collective-permute-done.3.after_ref
  122.6 1.9 %shard_map.79 = f32[3,8192]{1,0:T(4,128)} custom-call(s32[16]{0:T(128)S(1)} %copy-done.6, s32[16]{0:T(128)S(1)} %copy-done.7, s32[2,16]{1,0:T(2,128)S(1)} %collective-permute-done.anchors_ref, f32[3,8192]{1,0:T(4,128)S(1)} %shard_map.76.refs_0_.x_ref, f32[3,4096]{1,0:T(4,128)S(1)} %collective-permute-done.3.after_ref, ...), custom_call_target="tpu_custom_call" | custom-call | bytes 2000000 | tf_op jit(solution)/shard_map/pallas_call | solution.py:31
  (25 shorter events, 1.5 us)
Async XLA Ops:
  0.0 0.9 copy-start
  0.9 0.8 copy-start.3
  12.9 7.3 %copy-start.1 = (f32[3,8192]{1,0:T(4,128)S(1)}, f32[3,8192]{1,0:T(4,128)}, u32[]{:S(2)}) copy-start(f32[3,8192]{1,0:T(4,128)} %x_ref.3) | copy-start | bytes 294916
  12.9 21.7 %copy-start.2 = (f32[2,3,8192]{2,0,1:T(2,128)S(1)}, f32[2,3,8192]{2,0,1:T(2,128)}, u32[]{:S(2)}) copy-start(f32[2,3,8192]{2,0,1:T(2,128)} %param.8) | copy-start | bytes 589828
  12.9 28.1 %all-to-all-start.1 = ((f32[32,36,128]{2,1,0:T(8,128)}), f32[32,36,128]{2,1,0:T(8,128)S(1)}, u32[]{:S(2)}, u32[]{:S(2)}) async-start(f32[32,36,128]{2,1,0:T(8,128)} %get-tuple-element.10), calls=%async_computation.1 | async-start | bytes 1310720 | tf_op jit(solution)/shard_map/all_to_all | solution.py:406
  20.2 14.4 %collective-permute-start.2 = (f32[3,8192]{1,0:T(4,128)S(1)}, f32[3,8192]{1,0:T(4,128)S(1)}, u32[]{:S(2)}, u32[]{:S(2)}) collective-permute-start(f32[3,8192]{1,0:T(4,128)S(1)} %copy-done.1), channel_id=1, source_target_pairs={{0,1},{1,2},{2,3},{3,4},{4,5},{5,6},{6,7},{7,8},{8,9},{9,10},{10,1... | collective-permute-start | bytes 294920 | tf_op jit(solution)/shard_map/ppermute | solution.py:387
  23.9 10.7 %collective-permute-start.1 = (f32[3,4096]{1,0:T(4,128)S(1)}, f32[3,4096]{1,0:T(4,128)S(1)}, u32[]{:S(2)}, u32[]{:S(2)}) collective-permute-start(f32[3,4096]{1,0:T(4,128)S(1)} %slice.6), channel_id=1, source_target_pairs={{1,0},{2,1},{3,2},{4,3},{5,4},{6,5},{7,6},{8,7},{9,8},{10,9},{11,1... | collective-permute-start | bytes 147464 | tf_op jit(solution)/shard_map/ppermute | solution.py:387
  25.2 0.7 copy-start.6
  25.3 0.7 copy-start.7
  25.9 8.7 %collective-permute-start = (s32[2,16]{1,0:T(2,128)S(1)}, s32[2,16]{1,0:T(2,128)S(1)}, u32[]{:S(2)}, u32[]{:S(2)}) collective-permute-start(s32[2,16]{1,0:T(2,128)S(1)} %pad_add_fusion), channel_id=1, source_target_pairs={{0,1},{1,2},{2,3},{3,4},{4,5},{5,6},{6,7},{7,8},{8,9},{9,10},{10,1... | collective-permute-start | bytes 392 | tf_op jit(solution)/shard_map/ppermute | solution.py:387
  41.0 10.4 %copy-start.4 = (s32[512]{0:T(512)S(1)}, s32[512]{0:T(512)}, u32[]{:S(2)}) copy-start(s32[512]{0:T(512)} %rows_ref.3) | copy-start | bytes 6148
  41.0 10.4 %copy-start.5 = (s32[512]{0:T(512)S(1)}, s32[512]{0:T(512)}, u32[]{:S(2)}) copy-start(s32[512]{0:T(512)} %cols_ref.3) | copy-start | bytes 6148
  41.0 25.3 %all-to-all-start = ((f32[32,12,128]{2,1,0:T(8,128)}), f32[32,12,128]{2,1,0:T(8,128)S(1)}, u32[]{:S(2)}, u32[]{:S(2)}) async-start(f32[32,12,128]{2,1,0:T(8,128)} %shard_map.74), calls=%async_computation | async-start | bytes 524288 | tf_op jit(solution)/shard_map/all_to_all | solution.py:406
  67.0 34.5 %all-to-all-start.2 = ((f32[32,12,128]{2,1,0:T(8,128)}), f32[32,12,128]{2,1,0:T(8,128)S(1)}, u32[]{:S(2)}, u32[]{:S(2)}) async-start(f32[32,12,128]{2,1,0:T(8,128)} %multiply_add_fusion.refs_1_), calls=%async_computation.2 | async-start | bytes 524288 | tf_op jit(solution)/shard_map/all_to_all | solution.py:406
  72.9 12.8 %collective-permute-start.6 = (f32[32,12,128]{2,1,0:T(8,128)}, f32[32,12,128]{2,1,0:T(8,128)S(1)}, u32[]{:S(2)}, u32[]{:S(2)}) collective-permute-start(f32[32,12,128]{2,1,0:T(8,128)} %multiply_add_fusion.refs_1_), channel_id=1, source_target_pairs={{1,0},{2,1},{3,2},{5,4},{6,5},{7,6},{9,8},{10,9},{11,10},{13,12},{... | collective-permute-start | bytes 589832 | tf_op jit(solution)/shard_map/ppermute | solution.py:387
  74.2 11.5 %collective-permute-start.5 = (f32[32,12,128]{2,1,0:T(8,128)}, f32[32,12,128]{2,1,0:T(8,128)S(1)}, u32[]{:S(2)}, u32[]{:S(2)}) collective-permute-start(f32[32,12,128]{2,1,0:T(8,128)} %multiply_add_fusion.refs_1_), channel_id=1, source_target_pairs={{0,1},{1,2},{2,3},{4,5},{5,6},{6,7},{8,9},{9,10},{10,11},{12,13},{... | collective-permute-start | bytes 589832 | tf_op jit(solution)/shard_map/ppermute | solution.py:387
  101.6 16.0 %all-to-all-start.3 = ((f32[32,12,128]{2,1,0:T(8,128)}), f32[32,12,128]{2,1,0:T(8,128)S(1)}, u32[]{:S(2)}, u32[]{:S(2)}) async-start(f32[32,12,128]{2,1,0:T(8,128)} %shard_map.77), calls=%async_computation.3 | async-start | bytes 524288 | tf_op jit(solution)/shard_map/all_to_all | solution.py:406
  111.2 11.3 %collective-permute-start.4 = (f32[3,8192]{1,0:T(4,128)S(1)}, f32[3,8192]{1,0:T(4,128)S(1)}, u32[]{:S(2)}, u32[]{:S(2)}) collective-permute-start(f32[3,8192]{1,0:T(4,128)S(1)} %shard_map.76.refs_0_.x_ref), channel_id=1, source_target_pairs={{0,1},{1,2},{2,3},{3,4},{4,5},{5,6},{6,7},{7,8},{8,9},{9,10},{10,1... | collective-permute-start | bytes 294920 | tf_op jit(solution)/shard_map/ppermute | solution.py:387
  115.0 7.6 %collective-permute-start.3 = (f32[3,4096]{1,0:T(4,128)S(1)}, f32[3,4096]{1,0:T(4,128)S(1)}, u32[]{:S(2)}, u32[]{:S(2)}) collective-permute-start(f32[3,4096]{1,0:T(4,128)S(1)} %slice.8), channel_id=1, source_target_pairs={{1,0},{2,1},{3,2},{4,3},{5,4},{6,5},{7,6},{8,7},{9,8},{10,9},{11,1... | collective-permute-start | bytes 147464 | tf_op jit(solution)/shard_map/ppermute | solution.py:387

commit v3 on v2

--- a/solution.py
+++ b/solution.py
@@ -17,7 +17,7 @@
 longest_loop = 4096
 lanes = 128
 far_away = 1e15
-pairs_at_once = 32
+pairs_at_once = 64
 
 vmem = pl.BlockSpec(memory_space=pltpu.VMEM)
 smem = pl.BlockSpec(memory_space=pltpu.SMEM)
@@ -72,10 +72,9 @@
     lax.fori_loop(0, index_ref.shape[0] // 8, one, 0)
 
 
-def index_kernel(slabs, owner_ref, x_ref, out_ref, index_ref, slot_ref, turned_ref, total_ref):
+def index_kernel(devices, owner_ref, index_ref, slot_ref, turned_ref, total_ref):
     rows = owner_ref.shape[0]
-    devices = out_ref.shape[0]
-    per_owner = out_ref.shape[1] // 9
+    per_owner = index_ref.shape[0] // devices
     own = owner_ref[...]
     lane = iota((rows, lanes), 1)
     tri = jnp.where(
@@ -136,6 +135,11 @@
     lax.fori_loop(0, rows // at_once, spread, 0)
     blocks = index_ref.shape[0]
     index_ref[...] = (total_ref[0:blocks, :] + lanes * total_ref[blocks:, :]).astype(jnp.int32)
+
+
+def send_kernel(slabs, index_ref, x_ref, after_ref, before_ref, out_ref):
+    devices = out_ref.shape[0]
+    per_owner = out_ref.shape[1] // 9
 
     def store(owner, c, values):
         place = lax.rem(owner, slabs)
@@ -419,23 +423,31 @@
                 pltpu.VMEM((2 * lanes, lanes), f32),
                 pltpu.VMEM((blocks * 16, lanes), f32),
             ],
-            flops=16 * tile_rows.shape[0] * lanes * lanes,
-        )
-
-    anchors_before = shifted(jnp.stack([loop_left, loop_span]), both, 1)
-    before = shifted(positions, both, 1)
+            flops=1600 * tile_rows.shape[0] * lanes * lanes,
+        )
+
+    extruders = loop_left.shape[0]
+    anchors = jnp.concatenate([loop_left, loop_span]).astype(f32)
+    anchors = jnp.pad(anchors, (0, mono_dev - 2 * extruders))
+    before = shifted(jnp.concatenate([positions, anchors[None]], axis=0), both, 1)
     after = shifted(positions[:, :longest_loop], both, -1)
-    x_out, index, slot = call(
-        functools.partial(index_kernel, lax.axis_size("space")),
+    index, slot = call(
+        functools.partial(index_kernel, devices),
         [
-            jax.ShapeDtypeStruct((devices, 9 * per_owner, lanes), f32),
             jax.ShapeDtypeStruct((blocks, lanes), jnp.int32),
             jax.ShapeDtypeStruct((rows, lanes), jnp.int32),
         ],
-        [vmem, vmem],
-        (cell_owner.reshape(rows, lanes), positions),
+        [vmem],
+        (cell_owner.reshape(rows, lanes),),
         [pltpu.VMEM((lanes, lanes), jnp.int32), pltpu.VMEM((2 * blocks, lanes), f32)],
     )
+    x_out = call(
+        functools.partial(send_kernel, lax.axis_size("space")),
+        jax.ShapeDtypeStruct((devices, 9 * per_owner, lanes), f32),
+        [vmem] * 4,
+        (index, positions, after, before),
+    )
+    anchors_before = before[3, : 2 * extruders].astype(jnp.int32).reshape(2, extruders)
     x_cells = exchange(x_out)
     y_out = call(
         first_kernel,

time: 126 us -> 114 us (0.905)
  starting transfers between devices: 49.6 us -> 39.5 us
  Pallas kernels: 58 us -> 55.6 us
  other arithmetic: 0.75 us -> 2.55 us
  local copies, waits for them, and re-layouts: 2.36 us -> 0.8 us
    all_to_all x4, waiting for transfers between devices: 1.31 us -> 11.1 us  [exchange(): return lax.all_to_all(value, both, split_axis=0, concat_axis=0, tiled=True)]
    ppermute x7 -> x6, waiting for transfers between devices: 12.2 us -> 2.93 us  [shifted(): lax.ppermute(value, axis, [(source, source + steps) for source in range(f...]
    all_to_all x4, starting transfers between devices: 29.3 us -> 22.4 us  [exchange(): return lax.all_to_all(value, both, split_axis=0, concat_axis=0, tiled=True)]
    ppermute x7 -> x6, starting transfers between devices: 20.3 us -> 17 us  [shifted(): lax.ppermute(value, axis, [(source, source + steps) for source in range(f...]
    pallas_call x7 -> x8, Pallas kernels: 58 us -> 55.6 us  [call(): pl.pallas_call(body, out_shape=outs, in_specs=in_specs, out_specs=[vmem]...]
    unnamed x16 -> x14, local copies, waits for them, and re-layouts: 2.33 us -> 0.69 us
  transfers between devices with their start and end apart: 11 -> 10, of which waited for: 4 -> 5; matrix products, arithmetic and copies ran while one was open for 0% -> 0% of each run, Pallas kernels for 36% -> 43%
where the time goes in v3:
time: 114 us; the launch traced here: 113 us
  Pallas kernels  55.6 us (49%)
  starting transfers between devices  39.5 us (35%)
  waiting for transfers between devices  14 us (12%)
  other arithmetic  2.55 us (2%)
    pallas_call x8, Pallas kernels, call(): pl.pallas_call(body, out_shape=outs, in_specs=in_specs, out_specs=[vmem]...  55.6 us
    all_to_all x4, starting transfers between devices, exchange(): return lax.all_to_all(value, both, split_axis=0, concat_axis=0, tiled=True)  22.4 us
    ppermute x6, starting transfers between devices, shifted(): lax.ppermute(value, axis, [(source, source + steps) for source in range(f...  17 us
    all_to_all x4, waiting for transfers between devices, exchange(): return lax.all_to_all(value, both, split_axis=0, concat_axis=0, tiled=True)  11.1 us
    ppermute x6, waiting for transfers between devices, shifted(): lax.ppermute(value, axis, [(source, source + steps) for source in range(f...  2.93 us
  transfers between devices with their start and end apart: 10, of which 5 were waited for; matrix products, arithmetic and copies ran while one was open for 0% of the time, Pallas kernels for 43%

profile of v3, /device:TPU:0, one launch (start us, length us, event | category | flops | bytes accessed | tf_op | source)
XLA Modules:
  0.0 112.7 jit_solution(11032227977992793250)
XLA Ops:
  0.0 0.7 add_convert_fusion
  0.8 1.0 pad_maximum_fusion
  1.8 4.9 %collective-permute-start = (f32[4,8192]{1,0:T(4,128)S(1)}, f32[4,8192]{1,0:T(4,128)S(1)}, u32[]{:S(2)}, u32[]{:S(2)}) collective-permute-start(f32[4,8192]{1,0:T(4,128)S(1)} %pad_maximum_fusion), channel_id=1, source_target_pairs={{0,1},{1,2},{2,3},{3,4},{4,5},{5,6},{6,7},{7,8},{8,9},{9,10},{10,1... | collective-permute-start | bytes 393224 | tf_op jit(solution)/shard_map/ppermute | solution.py:391
  6.8 1.3 %collective-permute-start.1 = (f32[3,4096]{1,0:T(4,128)S(1)}, f32[3,4096]{1,0:T(4,128)S(1)}, u32[]{:S(2)}, u32[]{:S(2)}) collective-permute-start(f32[3,4096]{1,0:T(4,128)S(1)} %slice.10), channel_id=1, source_target_pairs={{1,0},{2,1},{3,2},{4,3},{5,4},{6,5},{7,6},{8,7},{9,8},{10,9},{11,1... | collective-permute-start | bytes 147464 | tf_op jit(solution)/shard_map/ppermute | solution.py:391
  8.1 5.8 %shard_map.73 = (s32[128,128]{1,0:T(8,128)S(1)}, s32[64,128]{1,0:T(8,128)S(1)}) custom-call(s32[64,128]{1,0:T(8,128)S(1)} %bitcast.5), custom_call_target="tpu_custom_call" | custom-call | bytes 2000000 | tf_op jit(solution)/shard_map/pallas_call | solution.py:31
  14.5 5.4 %shard_map.75 = f32[32,36,128]{2,1,0:T(8,128)} custom-call(s32[128,128]{1,0:T(8,128)S(1)} %get-tuple-element.8.index_ref, f32[3,8192]{1,0:T(4,128)S(1)} %copy-done, f32[3,4096]{1,0:T(4,128)S(1)} %collective-permute-done.1.after_ref, f32[4,8192]{1,0:T(4,128)S(1)} %collective-permute-done.before_ref), custom_call_target="tpu_custom_call" | custom-call | bytes 2000000 | tf_op jit(solution)/shard_map/pallas_call | solution.py:31
  19.9 6.4 %all-to-all-start.1 = ((f32[32,36,128]{2,1,0:T(8,128)}), f32[32,36,128]{2,1,0:T(8,128)S(1)}, u32[]{:S(2)}, u32[]{:S(2)}) async-start(f32[32,36,128]{2,1,0:T(8,128)} %shard_map.75), calls=%async_computation.1 | async-start | bytes 1310720 | tf_op jit(solution)/shard_map/all_to_all | solution.py:410
  27.0 6.3 %shard_map.74 = f32[32,12,128]{2,1,0:T(8,128)} custom-call(s32[16]{0:T(128)S(1)} %copy-done.3, s32[16]{0:T(128)S(1)} %copy-done.4, s32[2,16]{1,0:T(2,128)S(1)} %convert_element_type.14.anchors_ref, f32[3,8192]{1,0:T(4,128)S(1)} %copy-done, f32[3,4096]{1,0:T(4,128)S(1)} %collective-permute-done.1.after_ref, f32[4,8192]{1,0:T(4,128)S(1)} %collective-permute-done.before_ref, ...), custom_call_target="tpu_custom_call" | custom-call | bytes 2000000 | tf_op jit(solution)/shard_map/pallas_call | solution.py:31
  33.4 9.8 %all-to-all-done.1.refs_0_ = f32[32,36,128]{2,1,0:T(8,128)S(1)} async-done(((f32[32,36,128]{2,1,0:T(8,128)}), f32[32,36,128]{2,1,0:T(8,128)S(1)}, u32[]{:S(2)}, u32[]{:S(2)}) %all-to-all-start.1) | async-done | bytes 589856 | tf_op jit(solution)/shard_map/all_to_all | solution.py:410
  43.2 4.3 %all-to-all-start = ((f32[32,12,128]{2,1,0:T(8,128)}), f32[32,12,128]{2,1,0:T(8,128)S(1)}, u32[]{:S(2)}, u32[]{:S(2)}) async-start(f32[32,12,128]{2,1,0:T(8,128)} %shard_map.74), calls=%async_computation | async-start | bytes 524288 | tf_op jit(solution)/shard_map/all_to_all | solution.py:410
  47.5 13.7 %shard_map.76 = f32[32,12,128]{2,1,0:T(8,128)S(1)} custom-call(s32[512]{0:T(512)S(1)} %copy-done.5, s32[512]{0:T(512)S(1)} %copy-done.6, f32[32,36,128]{2,1,0:T(8,128)S(1)} %all-to-all-done.1.refs_0_), custom_call_target="tpu_custom_call" | custom-call | flops 13421772800 | bytes 2000000 | tf_op jit(solution)/shard_map/pallas_call | solution.py:31
  61.9 1.3 %collective-permute-start.5 = (f32[32,12,128]{2,1,0:T(8,128)}, f32[32,12,128]{2,1,0:T(8,128)S(1)}, u32[]{:S(2)}, u32[]{:S(2)}) collective-permute-start(f32[32,12,128]{2,1,0:T(8,128)} %multiply_add_fusion.refs_1_), channel_id=1, source_target_pairs={{1,0},{2,1},{3,2},{5,4},{6,5},{7,6},{9,8},{10,9},{11,10},{13,12},{... | collective-permute-start | bytes 589832 | tf_op jit(solution)/shard_map/ppermute | solution.py:391
  63.2 4.6 %collective-permute-start.4 = (f32[32,12,128]{2,1,0:T(8,128)}, f32[32,12,128]{2,1,0:T(8,128)S(1)}, u32[]{:S(2)}, u32[]{:S(2)}) collective-permute-start(f32[32,12,128]{2,1,0:T(8,128)} %multiply_add_fusion.refs_1_), channel_id=1, source_target_pairs={{0,1},{1,2},{2,3},{4,5},{5,6},{6,7},{8,9},{9,10},{10,11},{12,13},{... | collective-permute-start | bytes 589832 | tf_op jit(solution)/shard_map/ppermute | solution.py:391
  67.8 4.9 %all-to-all-start.2 = ((f32[32,12,128]{2,1,0:T(8,128)}), f32[32,12,128]{2,1,0:T(8,128)S(1)}, u32[]{:S(2)}, u32[]{:S(2)}) async-start(f32[32,12,128]{2,1,0:T(8,128)} %multiply_add_fusion.refs_1_), calls=%async_computation.2 | async-start | bytes 524288 | tf_op jit(solution)/shard_map/all_to_all | solution.py:410
  72.7 1.3 %collective-permute-done.4.refs_0_ = f32[32,12,128]{2,1,0:T(8,128)S(1)} collective-permute-done((f32[32,12,128]{2,1,0:T(8,128)}, f32[32,12,128]{2,1,0:T(8,128)S(1)}, u32[]{:S(2)}, u32[]{:S(2)}) %collective-permute-start.4) | collective-permute-done | bytes 196640 | tf_op jit(solution)/shard_map/ppermute | solution.py:391
  74.0 14.8 %shard_map.78 = f32[32,12,128]{2,1,0:T(8,128)} custom-call(s32[512]{0:T(512)S(1)} %copy-done.5, s32[512]{0:T(512)S(1)} %copy-done.6, f32[32,12,128]{2,1,0:T(8,128)S(1)} %collective-permute-done.4.refs_0_, f32[32,12,128]{2,1,0:T(8,128)} %multiply_add_fusion.refs_1_, f32[32,12,128]{2,1,0:T(8,128)S(1)} %collective-permute-done.5.refs_2_), custom_call_target="tpu_custom_call" | custom-call | flops 13421772800 | bytes 2000000 | tf_op jit(solution)/shard_map/pallas_call | solution.py:31
  88.7 6.9 %all-to-all-start.3 = ((f32[32,12,128]{2,1,0:T(8,128)}), f32[32,12,128]{2,1,0:T(8,128)S(1)}, u32[]{:S(2)}, u32[]{:S(2)}) async-start(f32[32,12,128]{2,1,0:T(8,128)} %shard_map.78), calls=%async_computation.3 | async-start | bytes 524288 | tf_op jit(solution)/shard_map/all_to_all | solution.py:410
  95.6 3.9 %shard_map.77.refs_0_.x_ref = f32[3,8192]{1,0:T(4,128)S(1)} custom-call(s32[64,128]{1,0:T(8,128)S(1)} %get-tuple-element.7.slot_ref, f32[32,12,128]{2,1,0:T(8,128)S(1)} %all-to-all-done.2.source_ref), custom_call_target="tpu_custom_call" | custom-call | bytes 2000000 | tf_op jit(solution)/shard_map/pallas_call | solution.py:31
  99.5 3.7 %collective-permute-start.3 = (f32[3,8192]{1,0:T(4,128)S(1)}, f32[3,8192]{1,0:T(4,128)S(1)}, u32[]{:S(2)}, u32[]{:S(2)}) collective-permute-start(f32[3,8192]{1,0:T(4,128)S(1)} %shard_map.77.refs_0_.x_ref), channel_id=1, source_target_pairs={{0,1},{1,2},{2,3},{3,4},{4,5},{5,6},{6,7},{7,8},{8,9},{9,10},{10,1... | collective-permute-start | bytes 294920 | tf_op jit(solution)/shard_map/ppermute | solution.py:391
  103.2 1.3 %collective-permute-start.2 = (f32[3,4096]{1,0:T(4,128)S(1)}, f32[3,4096]{1,0:T(4,128)S(1)}, u32[]{:S(2)}, u32[]{:S(2)}) collective-permute-start(f32[3,4096]{1,0:T(4,128)S(1)} %slice.13), channel_id=1, source_target_pairs={{1,0},{2,1},{3,2},{4,3},{5,4},{6,5},{7,6},{8,7},{9,8},{10,9},{11,1... | collective-permute-start | bytes 147464 | tf_op jit(solution)/shard_map/ppermute | solution.py:391
  104.5 1.3 %all-to-all-done.3.source_ref = f32[32,12,128]{2,1,0:T(8,128)S(1)} async-done(((f32[32,12,128]{2,1,0:T(8,128)}), f32[32,12,128]{2,1,0:T(8,128)S(1)}, u32[]{:S(2)}, u32[]{:S(2)}) %all-to-all-start.3) | async-done | bytes 196640 | tf_op jit(solution)/shard_map/all_to_all | solution.py:410
  105.8 3.9 %shard_map.79.base_ref = f32[3,8192]{1,0:T(4,128)S(1)} custom-call(s32[64,128]{1,0:T(8,128)S(1)} %get-tuple-element.7.slot_ref, f32[32,12,128]{2,1,0:T(8,128)S(1)} %all-to-all-done.3.source_ref, f32[3,8192]{1,0:T(4,128)S(1)} %shard_map.77.refs_0_.x_ref), custom_call_target="tpu_custom_call" | custom-call | bytes 2000000 | tf_op jit(solution)/shard_map/pallas_call | solution.py:31
  109.7 1.1 collective-permute-done.2.after_ref
  110.8 1.9 %shard_map.80 = f32[3,8192]{1,0:T(4,128)} custom-call(s32[16]{0:T(128)S(1)} %copy-done.3, s32[16]{0:T(128)S(1)} %copy-done.4, s32[2,16]{1,0:T(2,128)S(1)} %convert_element_type.14.anchors_ref, f32[3,8192]{1,0:T(4,128)S(1)} %shard_map.77.refs_0_.x_ref, f32[3,4096]{1,0:T(4,128)S(1)} %collective-permute-done.2.after_ref, ...), custom_call_target="tpu_custom_call" | custom-call | bytes 2000000 | tf_op jit(solution)/shard_map/pallas_call | solution.py:31
  (26 shorter events, 2.1 us)
Async XLA Ops:
  0.8 6.0 %copy-start = (f32[3,8192]{1,0:T(4,128)S(1)}, f32[3,8192]{1,0:T(4,128)}, u32[]{:S(2)}) copy-start(f32[3,8192]{1,0:T(4,128)} %x_ref.3) | copy-start | bytes 294916
  1.8 6.3 %copy-start.2 = (s32[8192,1]{0,1:T(1,128)S(1)}, s32[8192,1]{0,1:T(1,128)}, u32[]{:S(2)}) copy-start(s32[8192,1]{0,1:T(1,128)} %param.9) | copy-start | bytes 98308
  1.8 12.7 %collective-permute-start = (f32[4,8192]{1,0:T(4,128)S(1)}, f32[4,8192]{1,0:T(4,128)S(1)}, u32[]{:S(2)}, u32[]{:S(2)}) collective-permute-start(f32[4,8192]{1,0:T(4,128)S(1)} %pad_maximum_fusion), channel_id=1, source_target_pairs={{0,1},{1,2},{2,3},{3,4},{4,5},{5,6},{6,7},{7,8},{8,9},{9,10},{10,1... | collective-permute-start | bytes 393224 | tf_op jit(solution)/shard_map/ppermute | solution.py:391
  6.8 7.7 %collective-permute-start.1 = (f32[3,4096]{1,0:T(4,128)S(1)}, f32[3,4096]{1,0:T(4,128)S(1)}, u32[]{:S(2)}, u32[]{:S(2)}) collective-permute-start(f32[3,4096]{1,0:T(4,128)S(1)} %slice.10), channel_id=1, source_target_pairs={{1,0},{2,1},{3,2},{4,3},{5,4},{6,5},{7,6},{8,7},{9,8},{10,9},{11,1... | collective-permute-start | bytes 147464 | tf_op jit(solution)/shard_map/ppermute | solution.py:391
  19.9 6.5 %copy-start.1 = (f32[2,3,8192]{2,0,1:T(2,128)S(1)}, f32[2,3,8192]{2,0,1:T(2,128)}, u32[]{:S(2)}) copy-start(f32[2,3,8192]{2,0,1:T(2,128)} %param.8) | copy-start | bytes 589828
  19.9 23.3 %all-to-all-start.1 = ((f32[32,36,128]{2,1,0:T(8,128)}), f32[32,36,128]{2,1,0:T(8,128)S(1)}, u32[]{:S(2)}, u32[]{:S(2)}) async-start(f32[32,36,128]{2,1,0:T(8,128)} %shard_map.75), calls=%async_computation.1 | async-start | bytes 1310720 | tf_op jit(solution)/shard_map/all_to_all | solution.py:410
  26.4 0.7 copy-start.3
  26.4 0.7 copy-start.4
  33.4 14.1 %copy-start.5 = (s32[512]{0:T(512)S(1)}, s32[512]{0:T(512)}, u32[]{:S(2)}) copy-start(s32[512]{0:T(512)} %rows_ref.3) | copy-start | bytes 6148
  33.4 14.1 %copy-start.6 = (s32[512]{0:T(512)S(1)}, s32[512]{0:T(512)}, u32[]{:S(2)}) copy-start(s32[512]{0:T(512)} %cols_ref.3) | copy-start | bytes 6148
  43.2 18.0 %all-to-all-start = ((f32[32,12,128]{2,1,0:T(8,128)}), f32[32,12,128]{2,1,0:T(8,128)S(1)}, u32[]{:S(2)}, u32[]{:S(2)}) async-start(f32[32,12,128]{2,1,0:T(8,128)} %shard_map.74), calls=%async_computation | async-start | bytes 524288 | tf_op jit(solution)/shard_map/all_to_all | solution.py:410
  61.9 10.8 %collective-permute-start.5 = (f32[32,12,128]{2,1,0:T(8,128)}, f32[32,12,128]{2,1,0:T(8,128)S(1)}, u32[]{:S(2)}, u32[]{:S(2)}) collective-permute-start(f32[32,12,128]{2,1,0:T(8,128)} %multiply_add_fusion.refs_1_), channel_id=1, source_target_pairs={{1,0},{2,1},{3,2},{5,4},{6,5},{7,6},{9,8},{10,9},{11,10},{13,12},{... | collective-permute-start | bytes 589832 | tf_op jit(solution)/shard_map/ppermute | solution.py:391
  63.2 10.7 %collective-permute-start.4 = (f32[32,12,128]{2,1,0:T(8,128)}, f32[32,12,128]{2,1,0:T(8,128)S(1)}, u32[]{:S(2)}, u32[]{:S(2)}) collective-permute-start(f32[32,12,128]{2,1,0:T(8,128)} %multiply_add_fusion.refs_1_), channel_id=1, source_target_pairs={{0,1},{1,2},{2,3},{4,5},{5,6},{6,7},{8,9},{9,10},{10,11},{12,13},{... | collective-permute-start | bytes 589832 | tf_op jit(solution)/shard_map/ppermute | solution.py:391
  67.8 20.9 %all-to-all-start.2 = ((f32[32,12,128]{2,1,0:T(8,128)}), f32[32,12,128]{2,1,0:T(8,128)S(1)}, u32[]{:S(2)}, u32[]{:S(2)}) async-start(f32[32,12,128]{2,1,0:T(8,128)} %multiply_add_fusion.refs_1_), calls=%async_computation.2 | async-start | bytes 524288 | tf_op jit(solution)/shard_map/all_to_all | solution.py:410
  88.7 17.1 %all-to-all-start.3 = ((f32[32,12,128]{2,1,0:T(8,128)}), f32[32,12,128]{2,1,0:T(8,128)S(1)}, u32[]{:S(2)}, u32[]{:S(2)}) async-start(f32[32,12,128]{2,1,0:T(8,128)} %shard_map.78), calls=%async_computation.3 | async-start | bytes 524288 | tf_op jit(solution)/shard_map/all_to_all | solution.py:410
  99.5 11.3 %collective-permute-start.3 = (f32[3,8192]{1,0:T(4,128)S(1)}, f32[3,8192]{1,0:T(4,128)S(1)}, u32[]{:S(2)}, u32[]{:S(2)}) collective-permute-start(f32[3,8192]{1,0:T(4,128)S(1)} %shard_map.77.refs_0_.x_ref), channel_id=1, source_target_pairs={{0,1},{1,2},{2,3},{3,4},{4,5},{5,6},{6,7},{7,8},{8,9},{9,10},{10,1... | collective-permute-start | bytes 294920 | tf_op jit(solution)/shard_map/ppermute | solution.py:391
  103.2 7.6 %collective-permute-start.2 = (f32[3,4096]{1,0:T(4,128)S(1)}, f32[3,4096]{1,0:T(4,128)S(1)}, u32[]{:S(2)}, u32[]{:S(2)}) collective-permute-start(f32[3,4096]{1,0:T(4,128)S(1)} %slice.13), channel_id=1, source_target_pairs={{1,0},{2,1},{3,2},{4,3},{5,4},{6,5},{7,6},{8,7},{9,8},{10,9},{11,1... | collective-permute-start | bytes 147464 | tf_op jit(solution)/shard_map/ppermute | solution.py:391

commit v4 on v3

--- a/solution.py
+++ b/solution.py
@@ -26,7 +26,7 @@
 bf16 = jnp.bfloat16
 
 
-def call(body, outs, in_specs, args, scratch=(), flops=0, moved=2_000_000):
+def call(body, outs, in_specs, args, scratch=(), micros=1):
     many = isinstance(outs, list)
     return pl.pallas_call(
         body,
@@ -35,7 +35,9 @@
         out_specs=[vmem] * len(outs) if many else vmem,
         scratch_shapes=list(scratch),
         compiler_params=pltpu.CompilerParams(vmem_limit_bytes=32 * 1024 * 1024),
-        cost_estimate=pl.CostEstimate(flops=flops, bytes_accessed=moved, transcendentals=0),
+        cost_estimate=pl.CostEstimate(
+            flops=int(micros * 1e9), bytes_accessed=1_000_000, transcendentals=0
+        ),
     )(*args)
 
 
@@ -137,21 +139,11 @@
     index_ref[...] = (total_ref[0:blocks, :] + lanes * total_ref[blocks:, :]).astype(jnp.int32)
 
 
-def send_kernel(slabs, index_ref, x_ref, after_ref, before_ref, out_ref):
-    devices = out_ref.shape[0]
-    per_owner = out_ref.shape[1] // 9
+def send_kernel(index_ref, x_ref, after_ref, before_ref, out_ref):
+    per_owner = out_ref.shape[1] // 3
 
     def store(owner, c, values):
-        place = lax.rem(owner, slabs)
-        width = 3 * per_owner
-        at = c * per_owner
-        up = lax.rem(owner + 1, devices)
-        below = lax.rem(owner + devices - 1, devices)
-        out_ref[owner, width + at : width + at + per_owner, :] = values
-        out_ref[up, at : at + per_owner, :] = jnp.where(place < slabs - 1, values, far_away)
-        out_ref[below, 2 * width + at : 2 * width + at + per_owner, :] = jnp.where(
-            place > 0, values, far_away
-        )
+        out_ref[owner, c * per_owner : (c + 1) * per_owner, :] = values
 
     fill_slots(index_ref, x_ref, per_owner, store)
 
@@ -244,19 +236,11 @@
     return high, middle, x - high - middle
 
 
-def contact_kernel(merged, rows_ref, cols_ref, *refs):
-    if merged:
-        cells_ref, refs = refs[0], refs[1:]
-        width = cells_ref.shape[1] // 3
-        sides = [(cells_ref, 0), (cells_ref, width), (cells_ref, 2 * width)]
-    else:
-        sides = [(refs[0], 0), (refs[1], 0), (refs[2], 0)]
-        width = refs[0].shape[1]
-        refs = refs[3:]
-    out_ref, refs = refs[0], refs[1:]
-    far_t, far_x, near_t, stage, cap, total = refs
+def contact_kernel(
+    rows_ref, cols_ref, below_ref, own_ref, above_ref, out_ref, far_t, far_x, near_t, stage, cap, total
+):
     devices = out_ref.shape[0]
-    per_owner = width // 3
+    per_owner = out_ref.shape[1] // 3
     blocks = devices * per_owner
     owners = 8 // per_owner
     scale = 1.0 / math.sqrt(cutoff_sq)
@@ -268,16 +252,13 @@
     stage[...] = jnp.zeros_like(stage)
     total[...] = jnp.zeros_like(total)
 
-    def eight(ref, first, group, c):
-        at = first + c * per_owner
-        return jnp.concatenate(
-            [ref[group * owners + i, at : at + per_owner, :] for i in range(owners)], axis=0
-        )
+    def eight(ref, group, c):
+        return ref[c, pl.ds(pl.multiple_of(group * 8, 8), 8), :]
 
     def build(group, carry):
-        for side, valid in enumerate((has_below, None, has_above)):
-            ref, first = sides[side]
-            xs = [eight(ref, first, group, c) for c in range(3)]
+        sides = ((below_ref, has_below), (own_ref, None), (above_ref, has_above))
+        for side, (ref, valid) in enumerate(sides):
+            xs = [eight(ref, group, c) for c in range(3)]
             live = xs[0] < 0.5 * far_away
             if valid is not None:
                 live = jnp.logical_and(live, jnp.full((8, lanes), valid.astype(jnp.int32)) > 0)
@@ -346,7 +327,7 @@
     def finish(group, carry):
         sums = [total[pl.ds(group * lanes + f, 8, stride=16), :] for f in range(13)]
         for c in range(3):
-            place = eight(sides[1][0], sides[1][1], group, c)
+            place = eight(own_ref, group, c)
             here = jnp.where(place < 0.5 * far_away, place, 0.0) * scale
             force = (here * sums[12] - (sums[c] + sums[3 + c] + sums[6 + c])) * back
             for i in range(owners):
@@ -385,6 +366,25 @@
     lax.fori_loop(0, slot_ref.shape[0] // 8, one, 0)
 
 
+def turn_kernel(cells_ref, later_ref, out_ref):
+    per_owner = cells_ref.shape[1] // 3
+    for o in range(cells_ref.shape[0]):
+        for c in range(3):
+            out_ref[c, o * per_owner : (o + 1) * per_owner, :] = cells_ref[
+                o, c * per_owner : (c + 1) * per_owner, :
+            ]
+
+
+def advance_kernel(y_ref, force_ref, plain_ref, turned_ref):
+    per_owner = y_ref.shape[1] // 3
+    for o in range(y_ref.shape[0]):
+        for c in range(3):
+            at = slice(c * per_owner, (c + 1) * per_owner)
+            value = y_ref[o, at, :] + time_step * force_ref[o, at, :]
+            plain_ref[o, at, :] = value
+            turned_ref[c, o * per_owner : (o + 1) * per_owner, :] = value
+
+
 def shifted(value, axis, steps):
     count = lax.axis_size(axis)
     first, last = (max(0, -steps), min(count, count - steps))
@@ -409,12 +409,14 @@
     def exchange(value):
         return lax.all_to_all(value, both, split_axis=0, concat_axis=0, tiled=True)
 
-    def contact(merged, cells):
+    def contact(cells):
+        below = shifted(cells, "space", 1)
+        above = shifted(cells, "space", -1)
         return call(
-            functools.partial(contact_kernel, merged),
+            contact_kernel,
             sent,
-            [smem, smem] + [vmem] * len(cells),
-            (tile_rows, tile_cols, *cells),
+            [smem, smem] + [vmem] * 3,
+            (tile_rows, tile_cols, below, cells, above),
             [
                 pltpu.VMEM((3 * blocks * 16, lanes), bf16),
                 pltpu.VMEM((3 * blocks * 16, lanes), bf16),
@@ -423,7 +425,7 @@
                 pltpu.VMEM((2 * lanes, lanes), f32),
                 pltpu.VMEM((blocks * 16, lanes), f32),
             ],
-            flops=1600 * tile_rows.shape[0] * lanes * lanes,
+            micros=14,
         )
 
     extruders = loop_left.shape[0]
@@ -440,12 +442,14 @@
         [vmem],
         (cell_owner.reshape(rows, lanes),),
         [pltpu.VMEM((lanes, lanes), jnp.int32), pltpu.VMEM((2 * blocks, lanes), f32)],
+        micros=6,
     )
     x_out = call(
-        functools.partial(send_kernel, lax.axis_size("space")),
-        jax.ShapeDtypeStruct((devices, 9 * per_owner, lanes), f32),
+        send_kernel,
+        sent,
         [vmem] * 4,
         (index, positions, after, before),
+        micros=4,
     )
     anchors_before = before[3, : 2 * extruders].astype(jnp.int32).reshape(2, extruders)
     x_cells = exchange(x_out)
@@ -455,20 +459,21 @@
         [smem] * 3 + [vmem] * 5,
         (loop_left, loop_span, anchors_before, positions, after, before, noise_t, index),
         [pltpu.VMEM((3, mono_dev), f32)] + chain_scratch,
+        micros=6,
     )
     y_cells = exchange(y_out)
-    contact0 = contact(True, (x_cells,))
-    x1_cells = y_cells + time_step * contact0
-    below = shifted(x1_cells, "space", 1)
-    above = shifted(x1_cells, "space", -1)
+    turned = jax.ShapeDtypeStruct((3, blocks, lanes), f32)
+    hbm = pl.BlockSpec(memory_space=pl.ANY)
+    contact0 = contact(call(turn_kernel, turned, [vmem, hbm], (x_cells, y_out)))
+    x1_cells, x1_turned = call(advance_kernel, [sent, turned], [vmem] * 2, (y_cells, contact0))
     x1_back = exchange(x1_cells)
-    contact1 = contact(False, (below, x1_cells, above))
+    contact1 = contact(x1_turned)
     back1 = exchange(contact1)
 
-    x1 = call(gather_kernel, chain, [vmem] * 2, (slot, x1_back))
+    x1 = call(gather_kernel, chain, [vmem] * 2, (slot, x1_back), micros=4)
     before1 = shifted(x1, both, 1)
     after1 = shifted(x1[:, :longest_loop], both, -1)
-    pushed = call(gather_kernel, chain, [vmem] * 3, (slot, back1, x1))
+    pushed = call(gather_kernel, chain, [vmem] * 3, (slot, back1, x1), micros=4)
     return call(
         functools.partial(chain_kernel, 1),
         chain,

time: 114 us -> 110 us (0.965)
  waiting for transfers between devices: 14 us -> 9.46 us
    all_to_all x4, waiting for transfers between devices: 11.1 us -> 4.49 us  [exchange(): return lax.all_to_all(value, both, split_axis=0, concat_axis=0, tiled=True)]
    ppermute x6 -> x8, starting transfers between devices: 17 us -> 20.2 us  [shifted(): lax.ppermute(value, axis, [(source, source + steps) for source in range(f...]
    all_to_all x4, starting transfers between devices: 22.4 us -> 20.2 us  [exchange(): return lax.all_to_all(value, both, split_axis=0, concat_axis=0, tiled=True)]
    ppermute x6 -> x8, waiting for transfers between devices: 2.93 us -> 4.96 us  [shifted(): lax.ppermute(value, axis, [(source, source + steps) for source in range(f...]
    pallas_call x8 -> x10, Pallas kernels: 55.6 us -> 55.7 us  [call(): pl.pallas_call(body, out_shape=outs, in_specs=in_specs, out_specs=[vmem]...]
  transfers between devices with their start and end apart: 10 -> 12, of which waited for: 5 -> 6; matrix products, arithmetic and copies ran while one was open for 0% -> 0% of each run, Pallas kernels for 43% -> 44%
where the time goes in v4:
time: 110 us; the launch traced here: 108 us
  Pallas kernels  55.7 us (51%)
  starting transfers between devices  40.4 us (37%)
  waiting for transfers between devices  9.46 us (9%)
  other arithmetic  1.81 us (2%)
    pallas_call x10, Pallas kernels, call(): pl.pallas_call(body, out_shape=outs, in_specs=in_specs, out_specs=[vmem]...  55.7 us
    all_to_all x4, starting transfers between devices, exchange(): return lax.all_to_all(value, both, split_axis=0, concat_axis=0, tiled=True)  20.2 us
    ppermute x8, starting transfers between devices, shifted(): lax.ppermute(value, axis, [(source, source + steps) for source in range(f...  20.2 us
    ppermute x8, waiting for transfers between devices, shifted(): lax.ppermute(value, axis, [(source, source + steps) for source in range(f...  4.96 us
    all_to_all x4, waiting for transfers between devices, exchange(): return lax.all_to_all(value, both, split_axis=0, concat_axis=0, tiled=True)  4.49 us
  transfers between devices with their start and end apart: 12, of which 6 were waited for; matrix products, arithmetic and copies ran while one was open for 0% of the time, Pallas kernels for 44%

profile of v4, /device:TPU:0, one launch (start us, length us, event | category | flops | bytes accessed | tf_op | source)
XLA Modules:
  0.0 108.5 jit_solution(8337266293496827365)
XLA Ops:
  1.8 4.9 %collective-permute-start = (f32[4,8192]{1,0:T(4,128)S(1)}, f32[4,8192]{1,0:T(4,128)S(1)}, u32[]{:S(2)}, u32[]{:S(2)}) collective-permute-start(f32[4,8192]{1,0:T(4,128)S(1)} %pad_maximum_fusion), channel_id=1, source_target_pairs={{0,1},{1,2},{2,3},{3,4},{4,5},{5,6},{6,7},{7,8},{8,9},{9,10},{10,1... | collective-permute-start | bytes 393224 | tf_op jit(solution)/shard_map/ppermute | solution.py:391
  6.8 1.3 %collective-permute-start.1 = (f32[3,4096]{1,0:T(4,128)S(1)}, f32[3,4096]{1,0:T(4,128)S(1)}, u32[]{:S(2)}, u32[]{:S(2)}) collective-permute-start(f32[3,4096]{1,0:T(4,128)S(1)} %slice.10), channel_id=1, source_target_pairs={{1,0},{2,1},{3,2},{4,3},{5,4},{6,5},{7,6},{8,7},{9,8},{10,9},{11,1... | collective-permute-start | bytes 147464 | tf_op jit(solution)/shard_map/ppermute | solution.py:391
  8.1 5.8 %shard_map.73 = (s32[128,128]{1,0:T(8,128)S(1)}, s32[64,128]{1,0:T(8,128)S(1)}) custom-call(s32[64,128]{1,0:T(8,128)S(1)} %bitcast.5), custom_call_target="tpu_custom_call" | custom-call | flops 6000000000 | bytes 1000000 | tf_op jit(solution)/shard_map/pallas_call | solution.py:31
  14.5 5.1 %shard_map.75 = f32[32,12,128]{2,1,0:T(8,128)} custom-call(s32[128,128]{1,0:T(8,128)S(1)} %get-tuple-element.10.index_ref, f32[3,8192]{1,0:T(4,128)S(1)} %copy-done, f32[3,4096]{1,0:T(4,128)S(1)} %collective-permute-done.1.after_ref, f32[4,8192]{1,0:T(4,128)S(1)} %collective-permute-done.before_ref), custom_call_target="tpu_custom_call" | custom-call | flops 4000000000 | bytes 1000000 | tf_op jit(solution)/shard_map/pallas_call | solution.py:31
  19.6 6.5 %all-to-all-start.1 = ((f32[32,12,128]{2,1,0:T(8,128)}), f32[32,12,128]{2,1,0:T(8,128)S(1)}, u32[]{:S(2)}, u32[]{:S(2)}) async-start(f32[32,12,128]{2,1,0:T(8,128)} %shard_map.75), calls=%async_computation.1 | async-start | bytes 524288 | tf_op jit(solution)/shard_map/all_to_all | solution.py:410
  26.8 6.3 %shard_map.74.later_ref = f32[32,12,128]{2,1,0:T(8,128)} custom-call(s32[16]{0:T(128)S(1)} %copy-done.5, s32[16]{0:T(128)S(1)} %copy-done.6, s32[2,16]{1,0:T(2,128)S(1)} %convert_element_type.14.anchors_ref, f32[3,8192]{1,0:T(4,128)S(1)} %copy-done, f32[3,4096]{1,0:T(4,128)S(1)} %collective-permute-done.1.after_ref, ...), custom_call_target="tpu_custom_call" | custom-call | flops 6000000000 | bytes 1000000 | tf_op jit(solution)/shard_map/pallas_call | solution.py:31
  33.1 3.2 %all-to-all-done.1.cells_ref = f32[32,12,128]{2,1,0:T(8,128)S(1)} async-done(((f32[32,12,128]{2,1,0:T(8,128)}), f32[32,12,128]{2,1,0:T(8,128)S(1)}, u32[]{:S(2)}, u32[]{:S(2)}) %all-to-all-start.1) | async-done | bytes 196640 | tf_op jit(solution)/shard_map/all_to_all | solution.py:410
  36.4 3.0 %collective-permute-start.2 = (f32[3,128,128]{2,1,0:T(8,128)S(1)}, f32[3,128,128]{2,1,0:T(8,128)S(1)}, u32[]{:S(2)}, u32[]{:S(2)}) collective-permute-start(f32[3,128,128]{2,1,0:T(8,128)S(1)} %shard_map.76.own_ref), channel_id=1, source_target_pairs={{0,1},{1,2},{2,3},{4,5},{5,6},{6,7},{8,9},{9,10},{10,11},{12,13},{... | collective-permute-start | bytes 589832 | tf_op jit(solution)/shard_map/ppermute | solution.py:391
  39.4 1.3 %collective-permute-start.3 = (f32[3,128,128]{2,1,0:T(8,128)S(1)}, f32[3,128,128]{2,1,0:T(8,128)S(1)}, u32[]{:S(2)}, u32[]{:S(2)}) collective-permute-start(f32[3,128,128]{2,1,0:T(8,128)S(1)} %shard_map.76.own_ref), channel_id=1, source_target_pairs={{1,0},{2,1},{3,2},{5,4},{6,5},{7,6},{9,8},{10,9},{11,10},{13,12},{... | collective-permute-start | bytes 589832 | tf_op jit(solution)/shard_map/ppermute | solution.py:391
  40.7 4.3 %all-to-all-start = ((f32[32,12,128]{2,1,0:T(8,128)}), f32[32,12,128]{2,1,0:T(8,128)S(1)}, u32[]{:S(2)}, u32[]{:S(2)}) async-start(f32[32,12,128]{2,1,0:T(8,128)} %shard_map.74.later_ref), calls=%async_computation | async-start | bytes 524288 | tf_op jit(solution)/shard_map/all_to_all | solution.py:410
  45.0 2.0 %collective-permute-done.3.above_ref = f32[3,128,128]{2,1,0:T(8,128)S(1)} collective-permute-done((f32[3,128,128]{2,1,0:T(8,128)S(1)}, f32[3,128,128]{2,1,0:T(8,128)S(1)}, u32[]{:S(2)}, u32[]{:S(2)}) %collective-permute-start.3) | collective-permute-done | bytes 196640 | tf_op jit(solution)/shard_map/ppermute | solution.py:391
  47.0 13.6 %shard_map.77.force_ref = f32[32,12,128]{2,1,0:T(8,128)S(1)} custom-call(s32[512]{0:T(512)S(1)} %copy-done.3, s32[512]{0:T(512)S(1)} %copy-done.4, f32[3,128,128]{2,1,0:T(8,128)S(1)} %collective-permute-done.2.below_ref, f32[3,128,128]{2,1,0:T(8,128)S(1)} %shard_map.76.own_ref, f32[3,128,128]{2,1,0:T(8,128)S(1)} %collective-permute-done.3.above_ref), custom_call_target="tpu_custom_call" | custom-call | flops 14000000000 | bytes 1000000 | tf_op jit(solution)/shard_map/pallas_call | solution.py:31
  61.4 3.4 %collective-permute-start.6 = (f32[3,128,128]{2,1,0:T(8,128)S(1)}, f32[3,128,128]{2,1,0:T(8,128)S(1)}, u32[]{:S(2)}, u32[]{:S(2)}) collective-permute-start(f32[3,128,128]{2,1,0:T(8,128)S(1)} %get-tuple-element.12.own_ref), channel_id=1, source_target_pairs={{0,1},{1,2},{2,3},{4,5},{5,6},{6,7},{8,9},{9,10},{10,11},{12,13},{... | collective-permute-start | bytes 589832 | tf_op jit(solution)/shard_map/ppermute | solution.py:391
  64.8 1.3 %collective-permute-start.7 = (f32[3,128,128]{2,1,0:T(8,128)S(1)}, f32[3,128,128]{2,1,0:T(8,128)S(1)}, u32[]{:S(2)}, u32[]{:S(2)}) collective-permute-start(f32[3,128,128]{2,1,0:T(8,128)S(1)} %get-tuple-element.12.own_ref), channel_id=1, source_target_pairs={{1,0},{2,1},{3,2},{5,4},{6,5},{7,6},{9,8},{10,9},{11,10},{13,12},{... | collective-permute-start | bytes 589832 | tf_op jit(solution)/shard_map/ppermute | solution.py:391
  66.1 5.0 %all-to-all-start.2 = ((f32[32,12,128]{2,1,0:T(8,128)}), f32[32,12,128]{2,1,0:T(8,128)S(1)}, u32[]{:S(2)}, u32[]{:S(2)}) async-start(f32[32,12,128]{2,1,0:T(8,128)} %get-tuple-element.11), calls=%async_computation.2 | async-start | bytes 524288 | tf_op jit(solution)/shard_map/all_to_all | solution.py:410
  71.2 1.4 %collective-permute-done.7.above_ref = f32[3,128,128]{2,1,0:T(8,128)S(1)} collective-permute-done((f32[3,128,128]{2,1,0:T(8,128)S(1)}, f32[3,128,128]{2,1,0:T(8,128)S(1)}, u32[]{:S(2)}, u32[]{:S(2)}) %collective-permute-start.7) | collective-permute-done | bytes 196640 | tf_op jit(solution)/shard_map/ppermute | solution.py:391
  72.6 14.3 %shard_map.80 = f32[32,12,128]{2,1,0:T(8,128)} custom-call(s32[512]{0:T(512)S(1)} %copy-done.3, s32[512]{0:T(512)S(1)} %copy-done.4, f32[3,128,128]{2,1,0:T(8,128)S(1)} %collective-permute-done.6.below_ref, f32[3,128,128]{2,1,0:T(8,128)S(1)} %get-tuple-element.12.own_ref, f32[3,128,128]{2,1,0:T(8,128)S(1)} %collective-permute-done.7.above_ref), custom_call_target="tpu_custom_call" | custom-call | flops 14000000000 | bytes 1000000 | tf_op jit(solution)/shard_map/pallas_call | solution.py:31
  86.9 4.4 %all-to-all-start.3 = ((f32[32,12,128]{2,1,0:T(8,128)}), f32[32,12,128]{2,1,0:T(8,128)S(1)}, u32[]{:S(2)}, u32[]{:S(2)}) async-start(f32[32,12,128]{2,1,0:T(8,128)} %shard_map.80), calls=%async_computation.3 | async-start | bytes 524288 | tf_op jit(solution)/shard_map/all_to_all | solution.py:410
  91.4 3.9 %shard_map.79.refs_0_.x_ref = f32[3,8192]{1,0:T(4,128)S(1)} custom-call(s32[64,128]{1,0:T(8,128)S(1)} %get-tuple-element.9.slot_ref, f32[32,12,128]{2,1,0:T(8,128)S(1)} %all-to-all-done.2.source_ref), custom_call_target="tpu_custom_call" | custom-call | flops 4000000000 | bytes 1000000 | tf_op jit(solution)/shard_map/pallas_call | solution.py:31
  95.3 3.7 %collective-permute-start.5 = (f32[3,8192]{1,0:T(4,128)S(1)}, f32[3,8192]{1,0:T(4,128)S(1)}, u32[]{:S(2)}, u32[]{:S(2)}) collective-permute-start(f32[3,8192]{1,0:T(4,128)S(1)} %shard_map.79.refs_0_.x_ref), channel_id=1, source_target_pairs={{0,1},{1,2},{2,3},{3,4},{4,5},{5,6},{6,7},{7,8},{8,9},{9,10},{10,1... | collective-permute-start | bytes 294920 | tf_op jit(solution)/shard_map/ppermute | solution.py:391
  99.0 1.3 %collective-permute-start.4 = (f32[3,4096]{1,0:T(4,128)S(1)}, f32[3,4096]{1,0:T(4,128)S(1)}, u32[]{:S(2)}, u32[]{:S(2)}) collective-permute-start(f32[3,4096]{1,0:T(4,128)S(1)} %slice.13), channel_id=1, source_target_pairs={{1,0},{2,1},{3,2},{4,3},{5,4},{6,5},{7,6},{8,7},{9,8},{10,9},{11,1... | collective-permute-start | bytes 147464 | tf_op jit(solution)/shard_map/ppermute | solution.py:391
  100.3 1.3 %all-to-all-done.3.source_ref = f32[32,12,128]{2,1,0:T(8,128)S(1)} async-done(((f32[32,12,128]{2,1,0:T(8,128)}), f32[32,12,128]{2,1,0:T(8,128)S(1)}, u32[]{:S(2)}, u32[]{:S(2)}) %all-to-all-start.3) | async-done | bytes 196640 | tf_op jit(solution)/shard_map/all_to_all | solution.py:410
  101.6 3.9 %shard_map.81.base_ref = f32[3,8192]{1,0:T(4,128)S(1)} custom-call(s32[64,128]{1,0:T(8,128)S(1)} %get-tuple-element.9.slot_ref, f32[32,12,128]{2,1,0:T(8,128)S(1)} %all-to-all-done.3.source_ref, f32[3,8192]{1,0:T(4,128)S(1)} %shard_map.79.refs_0_.x_ref), custom_call_target="tpu_custom_call" | custom-call | flops 4000000000 | bytes 1000000 | tf_op jit(solution)/shard_map/pallas_call | solution.py:31
  106.6 1.9 %shard_map.82 = f32[3,8192]{1,0:T(4,128)} custom-call(s32[16]{0:T(128)S(1)} %copy-done.5, s32[16]{0:T(128)S(1)} %copy-done.6, s32[2,16]{1,0:T(2,128)S(1)} %convert_element_type.14.anchors_ref, f32[3,8192]{1,0:T(4,128)S(1)} %shard_map.79.refs_0_.x_ref, f32[3,4096]{1,0:T(4,128)S(1)} %collective-permute-done.4.after_ref, ...), custom_call_target="tpu_custom_call" | custom-call | flops 1000000000 | bytes 1000000 | tf_op jit(solution)/shard_map/pallas_call | solution.py:31
  (31 shorter events, 5.0 us)
Async XLA Ops:
  0.8 6.0 %copy-start = (f32[3,8192]{1,0:T(4,128)S(1)}, f32[3,8192]{1,0:T(4,128)}, u32[]{:S(2)}) copy-start(f32[3,8192]{1,0:T(4,128)} %x_ref.3) | copy-start | bytes 294916
  1.8 6.3 %copy-start.2 = (s32[8192,1]{0,1:T(1,128)S(1)}, s32[8192,1]{0,1:T(1,128)}, u32[]{:S(2)}) copy-start(s32[8192,1]{0,1:T(1,128)} %param.9) | copy-start | bytes 98308
  1.8 12.1 %collective-permute-start = (f32[4,8192]{1,0:T(4,128)S(1)}, f32[4,8192]{1,0:T(4,128)S(1)}, u32[]{:S(2)}, u32[]{:S(2)}) collective-permute-start(f32[4,8192]{1,0:T(4,128)S(1)} %pad_maximum_fusion), channel_id=1, source_target_pairs={{0,1},{1,2},{2,3},{3,4},{4,5},{5,6},{6,7},{7,8},{8,9},{9,10},{10,1... | collective-permute-start | bytes 393224 | tf_op jit(solution)/shard_map/ppermute | solution.py:391
  6.8 7.7 %collective-permute-start.1 = (f32[3,4096]{1,0:T(4,128)S(1)}, f32[3,4096]{1,0:T(4,128)S(1)}, u32[]{:S(2)}, u32[]{:S(2)}) collective-permute-start(f32[3,4096]{1,0:T(4,128)S(1)} %slice.10), channel_id=1, source_target_pairs={{1,0},{2,1},{3,2},{4,3},{5,4},{6,5},{7,6},{8,7},{9,8},{10,9},{11,1... | collective-permute-start | bytes 147464 | tf_op jit(solution)/shard_map/ppermute | solution.py:391
  19.6 6.5 %copy-start.1 = (f32[2,3,8192]{2,0,1:T(2,128)S(1)}, f32[2,3,8192]{2,0,1:T(2,128)}, u32[]{:S(2)}) copy-start(f32[2,3,8192]{2,0,1:T(2,128)} %param.8) | copy-start | bytes 589828
  19.6 16.7 %all-to-all-start.1 = ((f32[32,12,128]{2,1,0:T(8,128)}), f32[32,12,128]{2,1,0:T(8,128)S(1)}, u32[]{:S(2)}, u32[]{:S(2)}) async-start(f32[32,12,128]{2,1,0:T(8,128)} %shard_map.75), calls=%async_computation.1 | async-start | bytes 524288 | tf_op jit(solution)/shard_map/all_to_all | solution.py:410
  26.1 0.7 copy-start.5
  26.1 0.7 copy-start.6
  36.3 10.6 %copy-start.3 = (s32[512]{0:T(512)S(1)}, s32[512]{0:T(512)}, u32[]{:S(2)}) copy-start(s32[512]{0:T(512)} %rows_ref.3) | copy-start | bytes 6148
  36.3 10.6 %copy-start.4 = (s32[512]{0:T(512)S(1)}, s32[512]{0:T(512)}, u32[]{:S(2)}) copy-start(s32[512]{0:T(512)} %cols_ref.3) | copy-start | bytes 6148
  36.4 8.6 %collective-permute-start.2 = (f32[3,128,128]{2,1,0:T(8,128)S(1)}, f32[3,128,128]{2,1,0:T(8,128)S(1)}, u32[]{:S(2)}, u32[]{:S(2)}) collective-permute-start(f32[3,128,128]{2,1,0:T(8,128)S(1)} %shard_map.76.own_ref), channel_id=1, source_target_pairs={{0,1},{1,2},{2,3},{4,5},{5,6},{6,7},{8,9},{9,10},{10,11},{12,13},{... | collective-permute-start | bytes 589832 | tf_op jit(solution)/shard_map/ppermute | solution.py:391
  39.4 7.6 %collective-permute-start.3 = (f32[3,128,128]{2,1,0:T(8,128)S(1)}, f32[3,128,128]{2,1,0:T(8,128)S(1)}, u32[]{:S(2)}, u32[]{:S(2)}) collective-permute-start(f32[3,128,128]{2,1,0:T(8,128)S(1)} %shard_map.76.own_ref), channel_id=1, source_target_pairs={{1,0},{2,1},{3,2},{5,4},{6,5},{7,6},{9,8},{10,9},{11,10},{13,12},{... | collective-permute-start | bytes 589832 | tf_op jit(solution)/shard_map/ppermute | solution.py:391
  40.7 19.9 %all-to-all-start = ((f32[32,12,128]{2,1,0:T(8,128)}), f32[32,12,128]{2,1,0:T(8,128)S(1)}, u32[]{:S(2)}, u32[]{:S(2)}) async-start(f32[32,12,128]{2,1,0:T(8,128)} %shard_map.74.later_ref), calls=%async_computation | async-start | bytes 524288 | tf_op jit(solution)/shard_map/all_to_all | solution.py:410
  61.4 9.8 %collective-permute-start.6 = (f32[3,128,128]{2,1,0:T(8,128)S(1)}, f32[3,128,128]{2,1,0:T(8,128)S(1)}, u32[]{:S(2)}, u32[]{:S(2)}) collective-permute-start(f32[3,128,128]{2,1,0:T(8,128)S(1)} %get-tuple-element.12.own_ref), channel_id=1, source_target_pairs={{0,1},{1,2},{2,3},{4,5},{5,6},{6,7},{8,9},{9,10},{10,11},{12,13},{... | collective-permute-start | bytes 589832 | tf_op jit(solution)/shard_map/ppermute | solution.py:391
  64.8 7.8 %collective-permute-start.7 = (f32[3,128,128]{2,1,0:T(8,128)S(1)}, f32[3,128,128]{2,1,0:T(8,128)S(1)}, u32[]{:S(2)}, u32[]{:S(2)}) collective-permute-start(f32[3,128,128]{2,1,0:T(8,128)S(1)} %get-tuple-element.12.own_ref), channel_id=1, source_target_pairs={{1,0},{2,1},{3,2},{5,4},{6,5},{7,6},{9,8},{10,9},{11,10},{13,12},{... | collective-permute-start | bytes 589832 | tf_op jit(solution)/shard_map/ppermute | solution.py:391
  66.1 20.8 %all-to-all-start.2 = ((f32[32,12,128]{2,1,0:T(8,128)}), f32[32,12,128]{2,1,0:T(8,128)S(1)}, u32[]{:S(2)}, u32[]{:S(2)}) async-start(f32[32,12,128]{2,1,0:T(8,128)} %get-tuple-element.11), calls=%async_computation.2 | async-start | bytes 524288 | tf_op jit(solution)/shard_map/all_to_all | solution.py:410
  86.9 14.6 %all-to-all-start.3 = ((f32[32,12,128]{2,1,0:T(8,128)}), f32[32,12,128]{2,1,0:T(8,128)S(1)}, u32[]{:S(2)}, u32[]{:S(2)}) async-start(f32[32,12,128]{2,1,0:T(8,128)} %shard_map.80), calls=%async_computation.3 | async-start | bytes 524288 | tf_op jit(solution)/shard_map/all_to_all | solution.py:410
  95.3 11.3 %collective-permute-start.5 = (f32[3,8192]{1,0:T(4,128)S(1)}, f32[3,8192]{1,0:T(4,128)S(1)}, u32[]{:S(2)}, u32[]{:S(2)}) collective-permute-start(f32[3,8192]{1,0:T(4,128)S(1)} %shard_map.79.refs_0_.x_ref), channel_id=1, source_target_pairs={{0,1},{1,2},{2,3},{3,4},{4,5},{5,6},{6,7},{7,8},{8,9},{9,10},{10,1... | collective-permute-start | bytes 294920 | tf_op jit(solution)/shard_map/ppermute | solution.py:391
  99.0 7.6 %collective-permute-start.4 = (f32[3,4096]{1,0:T(4,128)S(1)}, f32[3,4096]{1,0:T(4,128)S(1)}, u32[]{:S(2)}, u32[]{:S(2)}) collective-permute-start(f32[3,4096]{1,0:T(4,128)S(1)} %slice.13), channel_id=1, source_target_pairs={{1,0},{2,1},{3,2},{4,3},{5,4},{6,5},{7,6},{8,7},{9,8},{10,9},{11,1... | collective-permute-start | bytes 147464 | tf_op jit(solution)/shard_map/ppermute | solution.py:391

commit v5 on v4

--- a/solution.py
+++ b/solution.py
@@ -148,23 +148,54 @@
     fill_slots(index_ref, x_ref, per_owner, store)
 
 
-def chain_forces(left_ref, span_ref, x_ref, after_ref, before_ref, anchors_ref, wide_ref, force_ref):
+def column(block, at):
+    there = iota(block.shape, 1) == at
+    return jnp.sum(jnp.where(there, block, 0.0), axis=1, keepdims=True)
+
+
+def window(ref, at):
+    return ref.at[:, pl.ds(pl.multiple_of((at >> 7) * lanes, lanes), lanes)]
+
+
+def value(ref, at):
+    return column(window(ref, at)[...], at & 127)
+
+
+def my_place():
+    return lax.axis_index("chain") * lax.axis_size("space") + lax.axis_index("space")
+
+
+def loops_before(anchors_ref, mono_dev):
+    me = my_place()
+    found = []
+    for e in range(anchors_ref.shape[1]):
+        a = anchors_ref[0, e] - (me - 1) * mono_dev
+        b = a + anchors_ref[1, e] - mono_dev
+        wanted = jnp.logical_and(b >= 0, me > 0)
+        found.append((jnp.where(wanted, a, 0), jnp.where(wanted, b, 0), wanted))
+    return found
+
+
+def chain_forces(left_ref, span_ref, anchors_ref, x_ref, ghost, wide_ref, force_ref):
     mono_dev = x_ref.shape[1]
     blocks = mono_dev // lanes
     extruders = left_ref.shape[0]
     count = lax.axis_size("chain") * lax.axis_size("space")
-    me = lax.axis_index("chain") * lax.axis_size("space") + lax.axis_index("space")
+    me = my_place()
     wide_ref[...] = jnp.zeros_like(wide_ref)
-    wide_ref[0:3, 0:lanes] = before_ref[0:3, mono_dev - lanes :]
-    wide_ref[0:3, lanes : lanes + mono_dev] = x_ref[...]
-    wide_ref[0:3, lanes + mono_dev :] = after_ref[...]
+    wide_ref[0:3, :] = x_ref[...]
+    ghost = jnp.concatenate([ghost, jnp.zeros((5, lanes), f32)], axis=0)
+
+    def ghost_at(k):
+        return jnp.broadcast_to(ghost[:, k : k + 1], (8, lanes))
+
     lane = iota((8, lanes), 1)
     has_before = (me > 0).astype(f32)
     has_after = (me < count - 1).astype(f32)
     for j in range(blocks):
-        here = wide_ref[:, (j + 1) * lanes : (j + 2) * lanes]
-        left = wide_ref[:, j * lanes : (j + 1) * lanes]
-        right = wide_ref[:, (j + 2) * lanes : (j + 3) * lanes]
+        here = wide_ref[:, j * lanes : (j + 1) * lanes]
+        left = wide_ref[:, (j - 1) * lanes : j * lanes] if j > 0 else ghost_at(2 * extruders)
+        right = wide_ref[:, (j + 1) * lanes : (j + 2) * lanes] if j < blocks - 1 else ghost_at(2 * extruders + 1)
         down = pltpu.roll(jnp.where(lane == lanes - 1, left, here), 1, 1) - here
         up = pltpu.roll(jnp.where(lane == 0, right, here), lanes - 1, 1) - here
         if j == 0:
@@ -173,61 +204,83 @@
             up = jnp.where(lane == lanes - 1, up * has_after, up)
         force_ref[:, j * lanes : (j + 1) * lanes] = bond_stiff * down + bond_stiff * up
 
-    def window(ref, at):
-        return ref.at[:, pl.ds(pl.multiple_of((at >> 7) * lanes, lanes), lanes)]
-
-    def value(block, at):
-        there = iota(block.shape, 1) == (at & 127)
-        return jnp.sum(jnp.where(there, block, 0.0), axis=1, keepdims=True)
-
     todo = []
     for e in range(extruders):
         a = left_ref[e] - me * mono_dev
         b = a + span_ref[e]
-        pull = loop_stiff * (
-            value(window(wide_ref, b + lanes)[...], b) - value(window(wide_ref, a + lanes)[...], a)
-        )
+        b_here = jnp.minimum(b, mono_dev - 1)
+        right = jnp.where(b < mono_dev, value(wide_ref, b_here), ghost[:, extruders + e : extruders + e + 1])
+        pull = loop_stiff * (right - value(wide_ref, a))
         todo.append((a, pull))
-        todo.append((jnp.minimum(b, mono_dev - 1), jnp.where(b < mono_dev, -pull, 0.0)))
-    for e in range(extruders):
-        a = anchors_ref[0, e] - (me - 1) * mono_dev
-        b = a + anchors_ref[1, e] - mono_dev
-        wanted = jnp.logical_and(b >= 0, me > 0)
-        a = jnp.where(wanted, a, 0)
-        b = jnp.where(wanted, b, 0)
-        far_end = value(window(before_ref, a)[0:3, :], a)
-        pull = loop_stiff * (value(window(wide_ref, b + lanes)[...], b)[0:3] - far_end)
-        pull = jnp.where(wanted, -pull, 0.0)
-        todo.append((b, jnp.concatenate([pull, jnp.zeros((5, 1), f32)], axis=0)))
+        todo.append((b_here, jnp.where(b < mono_dev, -pull, 0.0)))
+    for e, (a, b, wanted) in enumerate(loops_before(anchors_ref, mono_dev)):
+        pull = loop_stiff * (value(wide_ref, b) - ghost[:, e : e + 1])
+        todo.append((b, jnp.where(wanted, -pull, 0.0)))
     for at, pull in todo:
         spot = window(force_ref, at)
         spot[...] = spot[...] + jnp.where(lane == (at & 127), pull, 0.0)
 
 
-def chain_kernel(
-    step, left_ref, span_ref, anchors_ref, x_ref, after_ref, before_ref, noise_ref, base_ref, out_ref, wide_ref, force_ref
-):
-    chain_forces(left_ref, span_ref, x_ref, after_ref, before_ref, anchors_ref, wide_ref, force_ref)
+def chain_step(step, x_ref, noise_ref, out_ref, force_ref):
     for c in range(3):
         out_ref[c : c + 1, :] = (
-            base_ref[c : c + 1, :]
+            x_ref[c : c + 1, :]
             + time_step * force_ref[c : c + 1, :]
             + noise_gain * noise_ref[c, step : step + 1, :]
         )
 
 
 def first_kernel(
-    left_ref, span_ref, anchors_ref, x_ref, after_ref, before_ref, noise_ref, index_ref, out_ref, y_ref, wide_ref, force_ref
+    left_ref,
+    span_ref,
+    anchors_ref,
+    x_ref,
+    after_ref,
+    before_ref,
+    noise_ref,
+    index_ref,
+    slot_ref,
+    out_ref,
+    y_ref,
+    wide_ref,
+    force_ref,
 ):
-    chain_kernel(
-        0, left_ref, span_ref, anchors_ref, x_ref, after_ref, before_ref, noise_ref, x_ref, y_ref, wide_ref, force_ref
-    )
+    mono_dev = x_ref.shape[1]
+    extruders = left_ref.shape[0]
     per_owner = out_ref.shape[1] // 3
+    me = my_place()
+    lane = iota((3, lanes), 1)
+    found = loops_before(anchors_ref, mono_dev)
+    ghost = jnp.zeros((3, lanes), f32)
+    for e in range(extruders):
+        a, b, wanted = found[e]
+        ghost = jnp.where(lane == e, column(window(before_ref, a)[0:3, :], a & 127), ghost)
+        far_end = left_ref[e] - me * mono_dev + span_ref[e] - mono_dev
+        ghost = jnp.where(lane == extruders + e, value(after_ref, jnp.maximum(far_end, 0)), ghost)
+    ghost = jnp.where(lane == 2 * extruders, before_ref[0:3, mono_dev - 1 : mono_dev], ghost)
+    ghost = jnp.where(lane == 2 * extruders + 1, after_ref[:, 0:1], ghost)
+    chain_forces(left_ref, span_ref, anchors_ref, x_ref, ghost, wide_ref, force_ref)
+    chain_step(0, x_ref, noise_ref, y_ref, force_ref)
 
     def store(owner, c, values):
         out_ref[owner, c * per_owner : (c + 1) * per_owner, :] = values
 
     fill_slots(index_ref, y_ref, per_owner, store)
+
+    asked = [(left_ref[e] - me * mono_dev, True) for e in range(extruders)]
+    asked += [(b, wanted) for _, b, wanted in found]
+    asked += [(mono_dev - 1, True), (0, True)]
+    lane = iota((1, lanes), 1)
+    slots = jnp.full((1, lanes), -1.0, f32)
+    for k, (at, wanted) in enumerate(asked):
+        slot = column(slot_ref[pl.ds(at >> 7, 1), :].astype(f32), at & 127)
+        slots = jnp.where(jnp.logical_and(lane == k, wanted), slot, slots)
+    slots = slots.astype(jnp.int32)
+    width = per_owner * lanes
+    for o in range(out_ref.shape[0]):
+        local_slot = slots - o * width
+        here = jnp.logical_and(local_slot >= 0, local_slot < width)
+        out_ref[o, 3 * per_owner : 3 * per_owner + 1, :] = jnp.where(here, local_slot + 1, 0).astype(f32)
 
 
 def pieces(x):
@@ -339,10 +392,7 @@
     lax.fori_loop(0, blocks // 8, finish, 0)
 
 
-def gather_kernel(slot_ref, source_ref, *refs):
-    base_ref, out_ref = refs if len(refs) == 2 else (None, refs[0])
-    per_owner = source_ref.shape[1] // 3
-
+def take_slots(slot_ref, source_ref, per_owner, emit):
     def one(group, carry):
         slot = slot_ref[pl.ds(pl.multiple_of(group * 8, 8), 8), :]
         row_of = slot >> 7
@@ -357,13 +407,34 @@
         for i in range(8):
             at = pl.ds(pl.multiple_of((group * 8 + i) * lanes, lanes), lanes)
             for c in range(3):
-                value = held[c][i : i + 1, :]
-                if base_ref is not None:
-                    value = base_ref[c : c + 1, at] + time_step * value
-                out_ref[c : c + 1, at] = value
+                emit(c, at, held[c][i : i + 1, :])
         return carry
 
     lax.fori_loop(0, slot_ref.shape[0] // 8, one, 0)
+
+
+def second_kernel(
+    per_owner, left_ref, span_ref, anchors_ref, slot_ref, back_ref, noise_ref, out_ref, x_ref, wide_ref, force_ref
+):
+    def emit(c, at, values):
+        x_ref[c : c + 1, at] = values
+
+    take_slots(slot_ref, back_ref, per_owner, emit)
+    ghost = [jnp.zeros((1, lanes), f32) for _ in range(3)]
+    for o in range(back_ref.shape[0]):
+        for c in range(3):
+            at = 3 * per_owner + c
+            ghost[c] = ghost[c] + back_ref[o, at : at + 1, :]
+    ghost = jnp.concatenate(ghost, axis=0)
+    chain_forces(left_ref, span_ref, anchors_ref, x_ref, ghost, wide_ref, force_ref)
+    chain_step(1, x_ref, noise_ref, out_ref, force_ref)
+
+
+def last_kernel(slot_ref, back_ref, base_ref, out_ref):
+    def emit(c, at, values):
+        out_ref[c : c + 1, at] = base_ref[c : c + 1, at] + time_step * values
+
+    take_slots(slot_ref, back_ref, back_ref.shape[1] // 3, emit)
 
 
 def turn_kernel(cells_ref, later_ref, out_ref):
@@ -375,14 +446,36 @@
             ]
 
 
-def advance_kernel(y_ref, force_ref, plain_ref, turned_ref):
-    per_owner = y_ref.shape[1] // 3
-    for o in range(y_ref.shape[0]):
+def advance_kernel(extruders, y_ref, force_ref, plain_ref, turned_ref, answer_ref):
+    devices = y_ref.shape[0]
+    per_owner = force_ref.shape[1] // 3
+    for o in range(devices):
         for c in range(3):
             at = slice(c * per_owner, (c + 1) * per_owner)
-            value = y_ref[o, at, :] + time_step * force_ref[o, at, :]
-            plain_ref[o, at, :] = value
-            turned_ref[c, o * per_owner : (o + 1) * per_owner, :] = value
+            result = y_ref[o, at, :] + time_step * force_ref[o, at, :]
+            plain_ref[o, at, :] = result
+            turned_ref[c, o * per_owner : (o + 1) * per_owner, :] = result
+    answer_ref[...] = jnp.zeros_like(answer_ref)
+    row = 3 * per_owner
+    for group in range(devices // 8):
+        asked = jnp.concatenate([y_ref[group * 8 + i, row : row + 1, :] for i in range(8)], axis=0)
+        asked = asked.astype(jnp.int32) - 1
+        row_of = asked >> 7
+        lane_of = asked & 127
+        for c in range(3):
+            held = jnp.zeros((8, lanes), f32)
+            for k in range(per_owner):
+                source = turned_ref[c, pl.ds(group * 8 * per_owner + k, 8, stride=per_owner), :]
+                picked = jnp.take_along_axis(source, lane_of, axis=1, mode="promise_in_bounds")
+                held = jnp.where(row_of == k, picked, held)
+            answer_ref[c, 8 + group * 8 : 16 + group * 8, :] = held
+    lane = iota((1, lanes), 1)
+    from_before = jnp.logical_or(lane < extruders, lane == 2 * extruders)
+    for d in range(devices):
+        for c in range(3):
+            plain_ref[d, row + c : row + c + 1, :] = jnp.where(
+                from_before, answer_ref[c, 7 + d : 8 + d, :], answer_ref[c, 9 + d : 10 + d, :]
+            )
 
 
 def shifted(value, axis, steps):
@@ -402,7 +495,8 @@
     sent = jax.ShapeDtypeStruct((devices, 3 * per_owner, lanes), f32)
     chain = jax.ShapeDtypeStruct((3, mono_dev), f32)
     chain_scratch = [
-        pltpu.VMEM((8, lanes + mono_dev + longest_loop), f32),
+        pltpu.VMEM((3, mono_dev), f32),
+        pltpu.VMEM((8, mono_dev), f32),
         pltpu.VMEM((8, mono_dev), f32),
     ]
 
@@ -455,32 +549,35 @@
     x_cells = exchange(x_out)
     y_out = call(
         first_kernel,
-        sent,
-        [smem] * 3 + [vmem] * 5,
-        (loop_left, loop_span, anchors_before, positions, after, before, noise_t, index),
-        [pltpu.VMEM((3, mono_dev), f32)] + chain_scratch,
+        jax.ShapeDtypeStruct((devices, 3 * per_owner + 1, lanes), f32),
+        [smem] * 3 + [vmem] * 6,
+        (loop_left, loop_span, anchors_before, positions, after, before, noise_t, index, slot),
+        chain_scratch,
         micros=6,
     )
     y_cells = exchange(y_out)
     turned = jax.ShapeDtypeStruct((3, blocks, lanes), f32)
     hbm = pl.BlockSpec(memory_space=pl.ANY)
     contact0 = contact(call(turn_kernel, turned, [vmem, hbm], (x_cells, y_out)))
-    x1_cells, x1_turned = call(advance_kernel, [sent, turned], [vmem] * 2, (y_cells, contact0))
+    x1_cells, x1_turned = call(
+        functools.partial(advance_kernel, extruders),
+        [jax.ShapeDtypeStruct((devices, 3 * per_owner + 3, lanes), f32), turned],
+        [vmem] * 2,
+        (y_cells, contact0),
+        [pltpu.VMEM((3, devices + 16, lanes), f32)],
+    )
     x1_back = exchange(x1_cells)
     contact1 = contact(x1_turned)
     back1 = exchange(contact1)
-
-    x1 = call(gather_kernel, chain, [vmem] * 2, (slot, x1_back), micros=4)
-    before1 = shifted(x1, both, 1)
-    after1 = shifted(x1[:, :longest_loop], both, -1)
-    pushed = call(gather_kernel, chain, [vmem] * 3, (slot, back1, x1), micros=4)
-    return call(
-        functools.partial(chain_kernel, 1),
+    z = call(
+        functools.partial(second_kernel, per_owner),
         chain,
-        [smem] * 3 + [vmem] * 5,
-        (loop_left, loop_span, anchors_before, x1, after1, before1, noise_t, pushed),
+        [smem] * 3 + [vmem] * 3,
+        (loop_left, loop_span, anchors_before, slot, x1_back, noise_t),
         chain_scratch,
-    )
+        micros=6,
+    )
+    return call(last_kernel, chain, [vmem] * 3, (slot, back1, z), micros=4)
 
 
 def solution(mesh):

time: 110 us -> 109 us (level)
  starting transfers between devices: 40.4 us -> 38.1 us
  waiting for transfers between devices: 9.46 us -> 10.7 us
    all_to_all x4, waiting for transfers between devices: 4.49 us -> 7.48 us  [exchange(): return lax.all_to_all(value, both, split_axis=0, concat_axis=0, tiled=True)]
    ppermute x8 -> x6, waiting for transfers between devices: 4.96 us -> 3.17 us  [shifted(): lax.ppermute(value, axis, [(source, source + steps) for source in range(f...]
    ppermute x8 -> x6, starting transfers between devices: 20.2 us -> 19 us  [shifted(): lax.ppermute(value, axis, [(source, source + steps) for source in range(f...]
    all_to_all x4, starting transfers between devices: 20.2 us -> 19.1 us  [exchange(): return lax.all_to_all(value, both, split_axis=0, concat_axis=0, tiled=True)]
    pallas_call x10 -> x9, Pallas kernels: 55.7 us -> 56.7 us  [call(): pl.pallas_call(body, out_shape=outs, in_specs=in_specs, out_specs=[vmem]...]
  transfers between devices with their start and end apart: 12 -> 10, of which waited for: 6 -> 5; matrix products, arithmetic and copies ran while one was open for 0% -> 1% of each run, Pallas kernels for 44% -> 43%
where the time goes in v5:
time: 109 us; the launch traced here: 108 us
  Pallas kernels  56.7 us (52%)
  starting transfers between devices  38.1 us (35%)
  waiting for transfers between devices  10.7 us (10%)
  local copies, waits for them, and re-layouts  1.69 us (2%)
    pallas_call x9, Pallas kernels, call(): pl.pallas_call(body, out_shape=outs, in_specs=in_specs, out_specs=[vmem]...  56.7 us
    all_to_all x4, starting transfers between devices, exchange(): return lax.all_to_all(value, both, split_axis=0, concat_axis=0, tiled=True)  19.1 us
    ppermute x6, starting transfers between devices, shifted(): lax.ppermute(value, axis, [(source, source + steps) for source in range(f...  19 us
    all_to_all x4, waiting for transfers between devices, exchange(): return lax.all_to_all(value, both, split_axis=0, concat_axis=0, tiled=True)  7.48 us
    ppermute x6, waiting for transfers between devices, shifted(): lax.ppermute(value, axis, [(source, source + steps) for source in range(f...  3.17 us
  transfers between devices with their start and end apart: 10, of which 5 were waited for; matrix products, arithmetic and copies ran while one was open for 1% of the time, Pallas kernels for 43%

profile of v5, /device:TPU:0, one launch (start us, length us, event | category | flops | bytes accessed | tf_op | source)
XLA Modules:
  0.0 108.2 jit_solution(2297663848692514561)
XLA Ops:
  0.0 0.9 slice.7
  0.9 1.3 %collective-permute-start.1 = (f32[3,4096]{1,0:T(4,128)S(1)}, f32[3,4096]{1,0:T(4,128)S(1)}, u32[]{:S(2)}, u32[]{:S(2)}) collective-permute-start(f32[3,4096]{1,0:T(4,128)S(1)} %slice.7), channel_id=1, source_target_pairs={{1,0},{2,1},{3,2},{4,3},{5,4},{6,5},{7,6},{8,7},{9,8},{10,9},{11,1... | collective-permute-start | bytes 147464 | tf_op jit(solution)/shard_map/ppermute | solution.py:484
  2.2 0.8 add_convert_fusion
  3.1 5.6 %collective-permute-start = (f32[4,8192]{1,0:T(4,128)S(1)}, f32[4,8192]{1,0:T(4,128)S(1)}, u32[]{:S(2)}, u32[]{:S(2)}) collective-permute-start(f32[4,8192]{1,0:T(4,128)S(1)} %pad_maximum_fusion), channel_id=1, source_target_pairs={{0,1},{1,2},{2,3},{3,4},{4,5},{5,6},{6,7},{7,8},{8,9},{9,10},{10,1... | collective-permute-start | bytes 393224 | tf_op jit(solution)/shard_map/ppermute | solution.py:484
  8.7 5.9 %shard_map.73 = (s32[128,128]{1,0:T(8,128)S(1)}, s32[64,128]{1,0:T(8,128)S(1)}) custom-call(s32[64,128]{1,0:T(8,128)S(1)} %bitcast.5), custom_call_target="tpu_custom_call" | custom-call | flops 6000000000 | bytes 1000000 | tf_op jit(solution)/shard_map/pallas_call | solution.py:31
  14.6 5.1 %shard_map.75 = f32[32,12,128]{2,1,0:T(8,128)} custom-call(s32[128,128]{1,0:T(8,128)S(1)} %get-tuple-element.10.index_ref, f32[3,8192]{1,0:T(4,128)S(1)} %copy-done, f32[3,4096]{1,0:T(4,128)S(1)} %collective-permute-done.1.after_ref, f32[4,8192]{1,0:T(4,128)S(1)} %collective-permute-done.before_ref), custom_call_target="tpu_custom_call" | custom-call | flops 4000000000 | bytes 1000000 | tf_op jit(solution)/shard_map/pallas_call | solution.py:31
  19.7 8.1 %all-to-all-start.1 = ((f32[32,12,128]{2,1,0:T(8,128)}), f32[32,12,128]{2,1,0:T(8,128)S(1)}, u32[]{:S(2)}, u32[]{:S(2)}) async-start(f32[32,12,128]{2,1,0:T(8,128)} %shard_map.75), calls=%async_computation.1 | async-start | bytes 524288 | tf_op jit(solution)/shard_map/all_to_all | solution.py:504
  28.5 6.9 %shard_map.74.later_ref = f32[32,13,128]{2,1,0:T(8,128)} custom-call(s32[16]{0:T(128)S(1)} %copy-done.5, s32[16]{0:T(128)S(1)} %copy-done.6, s32[2,16]{1,0:T(2,128)S(1)} %convert_element_type.14.anchors_ref, f32[3,8192]{1,0:T(4,128)S(1)} %copy-done, f32[3,4096]{1,0:T(4,128)S(1)} %collective-permute-done.1.after_ref, ...), custom_call_target="tpu_custom_call" | custom-call | flops 6000000000 | bytes 1000000 | tf_op jit(solution)/shard_map/pallas_call | solution.py:31
  35.4 2.6 %all-to-all-done.1.cells_ref = f32[32,12,128]{2,1,0:T(8,128)S(1)} async-done(((f32[32,12,128]{2,1,0:T(8,128)}), f32[32,12,128]{2,1,0:T(8,128)S(1)}, u32[]{:S(2)}, u32[]{:S(2)}) %all-to-all-start.1) | async-done | bytes 196640 | tf_op jit(solution)/shard_map/all_to_all | solution.py:504
  38.1 1.3 %collective-permute-start.3 = (f32[3,128,128]{2,1,0:T(8,128)S(1)}, f32[3,128,128]{2,1,0:T(8,128)S(1)}, u32[]{:S(2)}, u32[]{:S(2)}) collective-permute-start(f32[3,128,128]{2,1,0:T(8,128)S(1)} %shard_map.76.own_ref), channel_id=1, source_target_pairs={{1,0},{2,1},{3,2},{5,4},{6,5},{7,6},{9,8},{10,9},{11,10},{13,12},{... | collective-permute-start | bytes 589832 | tf_op jit(solution)/shard_map/ppermute | solution.py:484
  39.4 4.6 %collective-permute-start.2 = (f32[3,128,128]{2,1,0:T(8,128)S(1)}, f32[3,128,128]{2,1,0:T(8,128)S(1)}, u32[]{:S(2)}, u32[]{:S(2)}) collective-permute-start(f32[3,128,128]{2,1,0:T(8,128)S(1)} %shard_map.76.own_ref), channel_id=1, source_target_pairs={{0,1},{1,2},{2,3},{4,5},{5,6},{6,7},{8,9},{9,10},{10,11},{12,13},{... | collective-permute-start | bytes 589832 | tf_op jit(solution)/shard_map/ppermute | solution.py:484
  43.9 2.6 %all-to-all-start = ((f32[32,13,128]{2,1,0:T(8,128)}), f32[32,13,128]{2,1,0:T(8,128)S(1)}, u32[]{:S(2)}, u32[]{:S(2)}) async-start(f32[32,13,128]{2,1,0:T(8,128)} %shard_map.74.later_ref), calls=%async_computation | async-start | bytes 524288 | tf_op jit(solution)/shard_map/all_to_all | solution.py:504
  46.6 0.7 collective-permute-done.3.above_ref
  47.2 2.0 %collective-permute-done.2.below_ref = f32[3,128,128]{2,1,0:T(8,128)S(1)} collective-permute-done((f32[3,128,128]{2,1,0:T(8,128)S(1)}, f32[3,128,128]{2,1,0:T(8,128)S(1)}, u32[]{:S(2)}, u32[]{:S(2)}) %collective-permute-start.2) | collective-permute-done | bytes 196640 | tf_op jit(solution)/shard_map/ppermute | solution.py:484
  49.2 13.6 %shard_map.77.force_ref = f32[32,12,128]{2,1,0:T(8,128)S(1)} custom-call(s32[512]{0:T(512)S(1)} %copy-done.3, s32[512]{0:T(512)S(1)} %copy-done.4, f32[3,128,128]{2,1,0:T(8,128)S(1)} %collective-permute-done.2.below_ref, f32[3,128,128]{2,1,0:T(8,128)S(1)} %shard_map.76.own_ref, f32[3,128,128]{2,1,0:T(8,128)S(1)} %collective-permute-done.3.above_ref), custom_call_target="tpu_custom_call" | custom-call | flops 14000000000 | bytes 1000000 | tf_op jit(solution)/shard_map/pallas_call | solution.py:31
  62.8 0.9 shard_map.78
  63.8 1.3 %collective-permute-start.5 = (f32[3,128,128]{2,1,0:T(8,128)S(1)}, f32[3,128,128]{2,1,0:T(8,128)S(1)}, u32[]{:S(2)}, u32[]{:S(2)}) collective-permute-start(f32[3,128,128]{2,1,0:T(8,128)S(1)} %get-tuple-element.11.own_ref), channel_id=1, source_target_pairs={{1,0},{2,1},{3,2},{5,4},{6,5},{7,6},{9,8},{10,9},{11,10},{13,12},{... | collective-permute-start | bytes 589832 | tf_op jit(solution)/shard_map/ppermute | solution.py:484
  65.1 5.0 %collective-permute-start.4 = (f32[3,128,128]{2,1,0:T(8,128)S(1)}, f32[3,128,128]{2,1,0:T(8,128)S(1)}, u32[]{:S(2)}, u32[]{:S(2)}) collective-permute-start(f32[3,128,128]{2,1,0:T(8,128)S(1)} %get-tuple-element.11.own_ref), channel_id=1, source_target_pairs={{0,1},{1,2},{2,3},{4,5},{5,6},{6,7},{8,9},{9,10},{10,11},{12,13},{... | collective-permute-start | bytes 589832 | tf_op jit(solution)/shard_map/ppermute | solution.py:484
  70.1 2.6 %all-to-all-start.3 = ((f32[32,15,128]{2,1,0:T(8,128)}), f32[32,15,128]{2,1,0:T(8,128)S(1)}, u32[]{:S(2)}, u32[]{:S(2)}) async-start(f32[32,15,128]{2,1,0:T(8,128)} %get-tuple-element.12), calls=%async_computation.3 | async-start | bytes 524288 | tf_op jit(solution)/shard_map/all_to_all | solution.py:504
  73.3 14.3 %shard_map.79 = f32[32,12,128]{2,1,0:T(8,128)} custom-call(s32[512]{0:T(512)S(1)} %copy-done.3, s32[512]{0:T(512)S(1)} %copy-done.4, f32[3,128,128]{2,1,0:T(8,128)S(1)} %collective-permute-done.4.below_ref, f32[3,128,128]{2,1,0:T(8,128)S(1)} %get-tuple-element.11.own_ref, f32[3,128,128]{2,1,0:T(8,128)S(1)} %collective-permute-done.5.above_ref), custom_call_target="tpu_custom_call" | custom-call | flops 14000000000 | bytes 1000000 | tf_op jit(solution)/shard_map/pallas_call | solution.py:31
  87.6 5.8 %all-to-all-start.2 = ((f32[32,12,128]{2,1,0:T(8,128)}), f32[32,12,128]{2,1,0:T(8,128)S(1)}, u32[]{:S(2)}, u32[]{:S(2)}) async-start(f32[32,12,128]{2,1,0:T(8,128)} %shard_map.79), calls=%async_computation.2 | async-start | bytes 524288 | tf_op jit(solution)/shard_map/all_to_all | solution.py:504
  93.4 5.3 %shard_map.80.base_ref = f32[3,8192]{1,0:T(4,128)S(1)} custom-call(s32[16]{0:T(128)S(1)} %copy-done.5, s32[16]{0:T(128)S(1)} %copy-done.6, s32[2,16]{1,0:T(2,128)S(1)} %convert_element_type.14.anchors_ref, s32[64,128]{1,0:T(8,128)S(1)} %get-tuple-element.9.slot_ref, f32[32,15,128]{2,1,0:T(8,128)S(1)} %all-to-all-done.3.back_ref, f32[3,2,8192]{2,1,0:T(2,128)S(1)} %bitcast.4), custom_call_target="tpu_custom_call" | custom-call | flops 6000000000 | bytes 1000000 | tf_op jit(solution)/shard_map/pallas_call | solution.py:31
  98.8 4.9 %all-to-all-done.2.back_ref = f32[32,12,128]{2,1,0:T(8,128)S(1)} async-done(((f32[32,12,128]{2,1,0:T(8,128)}), f32[32,12,128]{2,1,0:T(8,128)S(1)}, u32[]{:S(2)}, u32[]{:S(2)}) %all-to-all-start.2) | async-done | bytes 196640 | tf_op jit(solution)/shard_map/all_to_all | solution.py:504
  103.6 4.6 %shard_map.81 = f32[3,8192]{1,0:T(4,128)} custom-call(s32[64,128]{1,0:T(8,128)S(1)} %get-tuple-element.9.slot_ref, f32[32,12,128]{2,1,0:T(8,128)S(1)} %all-to-all-done.2.back_ref, f32[3,8192]{1,0:T(4,128)S(1)} %shard_map.80.base_ref), custom_call_target="tpu_custom_call" | custom-call | flops 4000000000 | bytes 1000000 | tf_op jit(solution)/shard_map/pallas_call | solution.py:31
  (25 shorter events, 1.4 us)
Async XLA Ops:
  0.0 3.0 %copy-start = (f32[3,8192]{1,0:T(4,128)S(1)}, f32[3,8192]{1,0:T(4,128)}, u32[]{:S(2)}) copy-start(f32[3,8192]{1,0:T(4,128)} %x_ref.3) | copy-start | bytes 294916
  0.9 13.7 %collective-permute-start.1 = (f32[3,4096]{1,0:T(4,128)S(1)}, f32[3,4096]{1,0:T(4,128)S(1)}, u32[]{:S(2)}, u32[]{:S(2)}) collective-permute-start(f32[3,4096]{1,0:T(4,128)S(1)} %slice.7), channel_id=1, source_target_pairs={{1,0},{2,1},{3,2},{4,3},{5,4},{6,5},{7,6},{8,7},{9,8},{10,9},{11,1... | collective-permute-start | bytes 147464 | tf_op jit(solution)/shard_map/ppermute | solution.py:484
  3.0 5.7 %copy-start.2 = (s32[8192,1]{0,1:T(1,128)S(1)}, s32[8192,1]{0,1:T(1,128)}, u32[]{:S(2)}) copy-start(s32[8192,1]{0,1:T(1,128)} %param.9) | copy-start | bytes 98308
  3.1 11.4 %collective-permute-start = (f32[4,8192]{1,0:T(4,128)S(1)}, f32[4,8192]{1,0:T(4,128)S(1)}, u32[]{:S(2)}, u32[]{:S(2)}) collective-permute-start(f32[4,8192]{1,0:T(4,128)S(1)} %pad_maximum_fusion), channel_id=1, source_target_pairs={{0,1},{1,2},{2,3},{3,4},{4,5},{5,6},{6,7},{7,8},{8,9},{9,10},{10,1... | collective-permute-start | bytes 393224 | tf_op jit(solution)/shard_map/ppermute | solution.py:484
  19.7 8.1 %copy-start.1 = (f32[2,3,8192]{2,0,1:T(2,128)S(1)}, f32[2,3,8192]{2,0,1:T(2,128)}, u32[]{:S(2)}) copy-start(f32[2,3,8192]{2,0,1:T(2,128)} %param.8) | copy-start | bytes 589828
  19.7 18.3 %all-to-all-start.1 = ((f32[32,12,128]{2,1,0:T(8,128)}), f32[32,12,128]{2,1,0:T(8,128)S(1)}, u32[]{:S(2)}, u32[]{:S(2)}) async-start(f32[32,12,128]{2,1,0:T(8,128)} %shard_map.75), calls=%async_computation.1 | async-start | bytes 524288 | tf_op jit(solution)/shard_map/all_to_all | solution.py:504
  27.8 0.7 copy-start.5
  27.8 0.7 copy-start.6
  38.1 11.1 %copy-start.3 = (s32[512]{0:T(512)S(1)}, s32[512]{0:T(512)}, u32[]{:S(2)}) copy-start(s32[512]{0:T(512)} %rows_ref.3) | copy-start | bytes 6148
  38.1 11.1 %copy-start.4 = (s32[512]{0:T(512)S(1)}, s32[512]{0:T(512)}, u32[]{:S(2)}) copy-start(s32[512]{0:T(512)} %cols_ref.3) | copy-start | bytes 6148
  38.1 9.1 %collective-permute-start.3 = (f32[3,128,128]{2,1,0:T(8,128)S(1)}, f32[3,128,128]{2,1,0:T(8,128)S(1)}, u32[]{:S(2)}, u32[]{:S(2)}) collective-permute-start(f32[3,128,128]{2,1,0:T(8,128)S(1)} %shard_map.76.own_ref), channel_id=1, source_target_pairs={{1,0},{2,1},{3,2},{5,4},{6,5},{7,6},{9,8},{10,9},{11,10},{13,12},{... | collective-permute-start | bytes 589832 | tf_op jit(solution)/shard_map/ppermute | solution.py:484
  39.4 9.8 %collective-permute-start.2 = (f32[3,128,128]{2,1,0:T(8,128)S(1)}, f32[3,128,128]{2,1,0:T(8,128)S(1)}, u32[]{:S(2)}, u32[]{:S(2)}) collective-permute-start(f32[3,128,128]{2,1,0:T(8,128)S(1)} %shard_map.76.own_ref), channel_id=1, source_target_pairs={{0,1},{1,2},{2,3},{4,5},{5,6},{6,7},{8,9},{9,10},{10,11},{12,13},{... | collective-permute-start | bytes 589832 | tf_op jit(solution)/shard_map/ppermute | solution.py:484
  43.9 18.9 %all-to-all-start = ((f32[32,13,128]{2,1,0:T(8,128)}), f32[32,13,128]{2,1,0:T(8,128)S(1)}, u32[]{:S(2)}, u32[]{:S(2)}) async-start(f32[32,13,128]{2,1,0:T(8,128)} %shard_map.74.later_ref), calls=%async_computation | async-start | bytes 524288 | tf_op jit(solution)/shard_map/all_to_all | solution.py:504
  63.8 8.9 %collective-permute-start.5 = (f32[3,128,128]{2,1,0:T(8,128)S(1)}, f32[3,128,128]{2,1,0:T(8,128)S(1)}, u32[]{:S(2)}, u32[]{:S(2)}) collective-permute-start(f32[3,128,128]{2,1,0:T(8,128)S(1)} %get-tuple-element.11.own_ref), channel_id=1, source_target_pairs={{1,0},{2,1},{3,2},{5,4},{6,5},{7,6},{9,8},{10,9},{11,10},{13,12},{... | collective-permute-start | bytes 589832 | tf_op jit(solution)/shard_map/ppermute | solution.py:484
  65.1 8.2 %collective-permute-start.4 = (f32[3,128,128]{2,1,0:T(8,128)S(1)}, f32[3,128,128]{2,1,0:T(8,128)S(1)}, u32[]{:S(2)}, u32[]{:S(2)}) collective-permute-start(f32[3,128,128]{2,1,0:T(8,128)S(1)} %get-tuple-element.11.own_ref), channel_id=1, source_target_pairs={{0,1},{1,2},{2,3},{4,5},{5,6},{6,7},{8,9},{9,10},{10,11},{12,13},{... | collective-permute-start | bytes 589832 | tf_op jit(solution)/shard_map/ppermute | solution.py:484
  70.1 17.5 %all-to-all-start.3 = ((f32[32,15,128]{2,1,0:T(8,128)}), f32[32,15,128]{2,1,0:T(8,128)S(1)}, u32[]{:S(2)}, u32[]{:S(2)}) async-start(f32[32,15,128]{2,1,0:T(8,128)} %get-tuple-element.12), calls=%async_computation.3 | async-start | bytes 524288 | tf_op jit(solution)/shard_map/all_to_all | solution.py:504
  87.6 16.0 %all-to-all-start.2 = ((f32[32,12,128]{2,1,0:T(8,128)}), f32[32,12,128]{2,1,0:T(8,128)S(1)}, u32[]{:S(2)}, u32[]{:S(2)}) async-start(f32[32,12,128]{2,1,0:T(8,128)} %shard_map.79), calls=%async_computation.2 | async-start | bytes 524288 | tf_op jit(solution)/shard_map/all_to_all | solution.py:504

commit v6 on v5

--- a/solution.py
+++ b/solution.py
@@ -14,10 +14,9 @@
 cutoff_sq = 2.25
 contact_coef = 0.4 / 2.25
 noise_gain = math.sqrt(0.1)
-longest_loop = 4096
 lanes = 128
 far_away = 1e15
-pairs_at_once = 64
+pairs_at_once = 128
 
 vmem = pl.BlockSpec(memory_space=pltpu.VMEM)
 smem = pl.BlockSpec(memory_space=pltpu.SMEM)
@@ -51,30 +50,41 @@
     )
 
 
-def fill_slots(index_ref, source_ref, per_owner, store):
-    rows = source_ref.shape[1] // lanes
+def fill_slots(index_ref, ranges_ref, source_ref, out_ref, per_owner):
     fields = source_ref.shape[0]
-    owners_here = 8 // per_owner
+    at_once = 16
 
     def one(group, carry):
-        code = index_ref[pl.ds(pl.multiple_of(group * 8, 8), 8), :]
+        first_owner = lax.div(group, per_owner) * 8
+        k = lax.rem(group, per_owner)
+        code = index_ref[pl.ds(first_owner * per_owner + k, 8, stride=per_owner), :]
         row_of = (code >> 7) - 1
         lane_of = code & 127
-        held = [jnp.full((8, lanes), far_away, f32) for _ in range(fields)]
-        for j in range(rows):
-            here = row_of == j
+        least = -ranges_ref[k, first_owner]
+        end = ranges_ref[per_owner + k, first_owner]
+
+        def search(chunk, held):
+            held = list(held)
+            for i in range(at_once):
+                j = chunk * at_once + i
+                here = row_of == j
+                at = pl.ds(pl.multiple_of(j * lanes, lanes), lanes)
+                for c in range(fields):
+                    held[c] = jnp.where(here, pick(source_ref[c : c + 1, at], lane_of), held[c])
+            return tuple(held)
+
+        empty = tuple(jnp.full((8, lanes), far_away, f32) for _ in range(fields))
+        chunks = (lax.div(least, at_once), lax.div(end + at_once - 1, at_once))
+        held = lax.fori_loop(*chunks, search, empty)
+        for i in range(8):
             for c in range(fields):
-                row = source_ref[c : c + 1, j * lanes : (j + 1) * lanes]
-                held[c] = jnp.where(here, pick(row, lane_of), held[c])
-        for i in range(owners_here):
-            for c in range(fields):
-                store(group * owners_here + i, c, held[c][i * per_owner : (i + 1) * per_owner, :])
+                out_ref[first_owner + i, pl.ds(c * per_owner + k, 1), :] = held[c][i : i + 1, :]
         return carry
 
     lax.fori_loop(0, index_ref.shape[0] // 8, one, 0)
 
 
-def index_kernel(devices, owner_ref, index_ref, slot_ref, turned_ref, total_ref):
+def index_kernel(devices, owner_ref, index_ref, slot_ref, ranges_ref, turned_ref, total_ref):
     rows = owner_ref.shape[0]
     per_owner = index_ref.shape[0] // devices
     own = owner_ref[...]
@@ -105,6 +115,30 @@
     offset = jnp.take_along_axis(above, own, axis=1, mode="promise_in_bounds")
     slot = own * (per_owner * lanes) + (prefix + offset).astype(jnp.int32)
     slot_ref[...] = slot
+
+    upto = above + total
+    count_of = upto[rows - 1 : rows]
+    least, end = [], []
+    for k in range(per_owner):
+        some = count_of > k * lanes
+        first_row = jnp.sum(jnp.where(upto <= k * lanes, 1.0, 0.0), axis=0, keepdims=True)
+        limit = jnp.minimum(count_of, (k + 1.0) * lanes)
+        last_row = jnp.sum(jnp.where(above < limit, 1.0, 0.0), axis=0, keepdims=True)
+        least.append(jnp.where(some, -first_row, -float(rows)))
+        end.append(jnp.where(some, last_row, 0.0))
+    spans = jnp.concatenate(least + end + [jnp.zeros((1, lanes), f32)] * (8 - 2 * per_owner), axis=0)
+    for shift in (1, 2, 4):
+        spans = jnp.maximum(spans, pltpu.roll(spans, lanes - shift, 1))
+    ranges_ref[0:8, :] = spans.astype(jnp.int32)
+    total_ref[0:rows, :] = above
+    total_ref[rows : 2 * rows, :] = upto
+    lowest = total_ref[pl.ds(0, 8, stride=8), :].astype(jnp.int32) >> 7
+    lowest = jnp.minimum(lowest, per_owner - 1)
+    highest = total_ref[pl.ds(rows + 7, 8, stride=8), :].astype(jnp.int32)
+    highest = jnp.maximum(highest - 1, 0) >> 7
+    more = jnp.max((highest - lowest).astype(f32), axis=1, keepdims=True)
+    ranges_ref[8:16, :] = lowest
+    ranges_ref[16:24, :] = jnp.broadcast_to(more, (8, lanes)).astype(jnp.int32)
 
     turned_ref[...] = jnp.concatenate([slot & 127] * (lanes // rows), axis=0).T
     down = iota((lanes, lanes), 0)
@@ -139,13 +173,8 @@
     index_ref[...] = (total_ref[0:blocks, :] + lanes * total_ref[blocks:, :]).astype(jnp.int32)
 
 
-def send_kernel(index_ref, x_ref, after_ref, before_ref, out_ref):
-    per_owner = out_ref.shape[1] // 3
-
-    def store(owner, c, values):
-        out_ref[owner, c * per_owner : (c + 1) * per_owner, :] = values
-
-    fill_slots(index_ref, x_ref, per_owner, store)
+def send_kernel(ranges_ref, index_ref, x_ref, after_ref, before_ref, out_ref):
+    fill_slots(index_ref, ranges_ref, x_ref, out_ref, out_ref.shape[1] // 3)
 
 
 def column(block, at):
@@ -234,6 +263,7 @@
     left_ref,
     span_ref,
     anchors_ref,
+    ranges_ref,
     x_ref,
     after_ref,
     before_ref,
@@ -262,10 +292,7 @@
     chain_forces(left_ref, span_ref, anchors_ref, x_ref, ghost, wide_ref, force_ref)
     chain_step(0, x_ref, noise_ref, y_ref, force_ref)
 
-    def store(owner, c, values):
-        out_ref[owner, c * per_owner : (c + 1) * per_owner, :] = values
-
-    fill_slots(index_ref, y_ref, per_owner, store)
+    fill_slots(index_ref, ranges_ref, y_ref, out_ref, per_owner)
 
     asked = [(left_ref[e] - me * mono_dev, True) for e in range(extruders)]
     asked += [(b, wanted) for _, b, wanted in found]
@@ -392,34 +419,65 @@
     lax.fori_loop(0, blocks // 8, finish, 0)
 
 
-def take_slots(slot_ref, source_ref, per_owner, emit):
+def take_slots(slot_ref, ranges_ref, source_ref, per_owner, emit):
+    owners = source_ref.shape[0]
+
     def one(group, carry):
         slot = slot_ref[pl.ds(pl.multiple_of(group * 8, 8), 8), :]
         row_of = slot >> 7
         lane_of = slot & 127
-        held = [jnp.zeros((8, lanes), f32) for _ in range(3)]
-        for s in range(source_ref.shape[0] * per_owner):
-            here = row_of == s
-            for c in range(3):
-                at = c * per_owner + s % per_owner
-                row = source_ref[s // per_owner, at : at + 1, :]
-                held[c] = jnp.where(here, pick(row, lane_of), held[c])
-        for i in range(8):
-            at = pl.ds(pl.multiple_of((group * 8 + i) * lanes, lanes), lanes)
-            for c in range(3):
-                emit(c, at, held[c][i : i + 1, :])
+
+        def search(tries, first):
+            held = [jnp.zeros((8, lanes), f32) for _ in range(3)]
+            for o in range(owners):
+                base = first(o)
+                for t in range(tries):
+                    k = jnp.minimum(base + t, per_owner - 1)
+                    here = row_of == o * per_owner + k
+                    for c in range(3):
+                        row = source_ref[o, pl.ds(c * per_owner + k, 1), :]
+                        held[c] = jnp.where(here, pick(row, lane_of), held[c])
+            for i in range(8):
+                at = pl.ds(pl.multiple_of((group * 8 + i) * lanes, lanes), lanes)
+                for c in range(3):
+                    emit(c, at, held[c][i : i + 1, :])
+
+        if per_owner <= 2:
+            search(per_owner, lambda o: 0)
+        else:
+            few = ranges_ref[16 + group, 0] <= 1
+
+            @pl.when(few)
+            def _():
+                search(2, lambda o: ranges_ref[8 + group, o])
+
+            @pl.when(jnp.logical_not(few))
+            def _():
+                search(per_owner, lambda o: 0)
+
         return carry
 
     lax.fori_loop(0, slot_ref.shape[0] // 8, one, 0)
 
 
 def second_kernel(
-    per_owner, left_ref, span_ref, anchors_ref, slot_ref, back_ref, noise_ref, out_ref, x_ref, wide_ref, force_ref
+    per_owner,
+    left_ref,
+    span_ref,
+    anchors_ref,
+    ranges_ref,
+    slot_ref,
+    back_ref,
+    noise_ref,
+    out_ref,
+    x_ref,
+    wide_ref,
+    force_ref,
 ):
     def emit(c, at, values):
         x_ref[c : c + 1, at] = values
 
-    take_slots(slot_ref, back_ref, per_owner, emit)
+    take_slots(slot_ref, ranges_ref, back_ref, per_owner, emit)
     ghost = [jnp.zeros((1, lanes), f32) for _ in range(3)]
     for o in range(back_ref.shape[0]):
         for c in range(3):
@@ -430,11 +488,11 @@
     chain_step(1, x_ref, noise_ref, out_ref, force_ref)
 
 
-def last_kernel(slot_ref, back_ref, base_ref, out_ref):
+def last_kernel(ranges_ref, slot_ref, back_ref, base_ref, out_ref):
     def emit(c, at, values):
         out_ref[c : c + 1, at] = base_ref[c : c + 1, at] + time_step * values
 
-    take_slots(slot_ref, back_ref, back_ref.shape[1] // 3, emit)
+    take_slots(slot_ref, ranges_ref, back_ref, back_ref.shape[1] // 3, emit)
 
 
 def turn_kernel(cells_ref, later_ref, out_ref):
@@ -526,12 +584,13 @@
     anchors = jnp.concatenate([loop_left, loop_span]).astype(f32)
     anchors = jnp.pad(anchors, (0, mono_dev - 2 * extruders))
     before = shifted(jnp.concatenate([positions, anchors[None]], axis=0), both, 1)
-    after = shifted(positions[:, :longest_loop], both, -1)
-    index, slot = call(
+    after = shifted(positions, both, -1)
+    index, slot, ranges = call(
         functools.partial(index_kernel, devices),
         [
             jax.ShapeDtypeStruct((blocks, lanes), jnp.int32),
             jax.ShapeDtypeStruct((rows, lanes), jnp.int32),
+            jax.ShapeDtypeStruct((24, lanes), jnp.int32),
         ],
         [vmem],
         (cell_owner.reshape(rows, lanes),),
@@ -541,8 +600,8 @@
     x_out = call(
         send_kernel,
         sent,
-        [vmem] * 4,
-        (index, positions, after, before),
+        [smem] + [vmem] * 4,
+        (ranges, index, positions, after, before),
         micros=4,
     )
     anchors_before = before[3, : 2 * extruders].astype(jnp.int32).reshape(2, extruders)
@@ -550,8 +609,8 @@
     y_out = call(
         first_kernel,
         jax.ShapeDtypeStruct((devices, 3 * per_owner + 1, lanes), f32),
-        [smem] * 3 + [vmem] * 6,
-        (loop_left, loop_span, anchors_before, positions, after, before, noise_t, index, slot),
+        [smem] * 4 + [vmem] * 6,
+        (loop_left, loop_span, anchors_before, ranges, positions, after, before, noise_t, index, slot),
         chain_scratch,
         micros=6,
     )
@@ -572,12 +631,12 @@
     z = call(
         functools.partial(second_kernel, per_owner),
         chain,
-        [smem] * 3 + [vmem] * 3,
-        (loop_left, loop_span, anchors_before, slot, x1_back, noise_t),
+        [smem] * 4 + [vmem] * 3,
+        (loop_left, loop_span, anchors_before, ranges, slot, x1_back, noise_t),
         chain_scratch,
         micros=6,
     )
-    return call(last_kernel, chain, [vmem] * 3, (slot, back1, z), micros=4)
+    return call(last_kernel, chain, [smem] + [vmem] * 3, (ranges, slot, back1, z), micros=4)
 
 
 def solution(mesh):

time: 109 us -> 109 us (level)
  waiting for transfers between devices: 10.7 us -> 7.96 us
  starting transfers between devices: 38.1 us -> 40.3 us
  Pallas kernels: 56.7 us -> 57.9 us
    all_to_all x4, starting transfers between devices: 19.1 us -> 21.3 us  [exchange(): return lax.all_to_all(value, both, split_axis=0, concat_axis=0, tiled=True)]
    ppermute x6, waiting for transfers between devices: 3.17 us -> 1.07 us  [shifted(): lax.ppermute(value, axis, [(source, source + steps) for source in range(f...]
    pallas_call x9, Pallas kernels: 56.7 us -> 57.9 us  [call(): pl.pallas_call(body, out_shape=outs, in_specs=in_specs, out_specs=[vmem]...]
  transfers between devices with their start and end apart: 10 -> 10, of which waited for: 5 -> 3; matrix products, arithmetic and copies ran while one was open for 1% -> 2% of each run, Pallas kernels for 43% -> 42%
where the time goes in v6:
time: 109 us
  Pallas kernels  57.9 us (53%)
  starting transfers between devices  40.3 us (37%)
  waiting for transfers between devices  7.96 us (7%)
  other arithmetic  1.75 us (2%)
    pallas_call x9, Pallas kernels, call(): pl.pallas_call(body, out_shape=outs, in_specs=in_specs, out_specs=[vmem]...  57.9 us
    all_to_all x4, starting transfers between devices, exchange(): return lax.all_to_all(value, both, split_axis=0, concat_axis=0, tiled=True)  21.3 us
    ppermute x6, starting transfers between devices, shifted(): lax.ppermute(value, axis, [(source, source + steps) for source in range(f...  19 us
    all_to_all x4, waiting for transfers between devices, exchange(): return lax.all_to_all(value, both, split_axis=0, concat_axis=0, tiled=True)  6.89 us
  transfers between devices with their start and end apart: 10, of which 3 were waited for; matrix products, arithmetic and copies ran while one was open for 2% of the time, Pallas kernels for 42%

profile of v6, /device:TPU:0, one launch (start us, length us, event | category | flops | bytes accessed | tf_op | source)
XLA Modules:
  0.0 108.9 jit_solution(5311734254819401572)
XLA Ops:
  0.0 1.3 %collective-permute-start.1 = (f32[3,8192]{1,0:T(4,128)}, f32[3,8192]{1,0:T(4,128)S(1)}, u32[]{:S(2)}, u32[]{:S(2)}) collective-permute-start(f32[3,8192]{1,0:T(4,128)} %x_ref.3), channel_id=1, source_target_pairs={{1,0},{2,1},{3,2},{4,3},{5,4},{6,5},{7,6},{8,7},{9,8},{10,9},{11,1... | collective-permute-start | bytes 294920 | tf_op jit(solution)/shard_map/ppermute | solution.py:542
  1.3 0.8 add_convert_fusion
  2.0 1.0 pad_maximum_fusion
  3.0 5.6 %collective-permute-start = (f32[4,8192]{1,0:T(4,128)S(1)}, f32[4,8192]{1,0:T(4,128)S(1)}, u32[]{:S(2)}, u32[]{:S(2)}) collective-permute-start(f32[4,8192]{1,0:T(4,128)S(1)} %pad_maximum_fusion), channel_id=1, source_target_pairs={{0,1},{1,2},{2,3},{3,4},{4,5},{5,6},{6,7},{7,8},{8,9},{9,10},{10,1... | collective-permute-start | bytes 393224 | tf_op jit(solution)/shard_map/ppermute | solution.py:542
  8.6 6.0 %shard_map.73 = (s32[128,128]{1,0:T(8,128)S(1)}, s32[64,128]{1,0:T(8,128)S(1)}, s32[24,128]{1,0:T(8,128)S(1)}) custom-call(s32[64,128]{1,0:T(8,128)S(1)} %bitcast.5), custom_call_target="tpu_custom_call" | custom-call | flops 6000000000 | bytes 1000000 | tf_op jit(solution)/shard_map/pallas_call | solution.py:30
  14.7 7.5 %shard_map.75 = f32[32,12,128]{2,1,0:T(8,128)} custom-call(s32[24,128]{1,0:T(8,128)S(1)} %get-tuple-element.10.ranges_ref, s32[128,128]{1,0:T(8,128)S(1)} %get-tuple-element.12.index_ref, f32[3,8192]{1,0:T(4,128)S(1)} %copy-done, f32[3,8192]{1,0:T(4,128)S(1)} %collective-permute-done.1.after_ref, f32[4,8192]{1,0:T(4,128)S(1)} %collective-permute-done.before_ref), custom_call_target="tpu_custom_call" | custom-call | flops 4000000000 | bytes 1000000 | tf_op jit(solution)/shard_map/pallas_call | solution.py:30
  22.2 8.0 %all-to-all-start.1 = ((f32[32,12,128]{2,1,0:T(8,128)}), f32[32,12,128]{2,1,0:T(8,128)S(1)}, u32[]{:S(2)}, u32[]{:S(2)}) async-start(f32[32,12,128]{2,1,0:T(8,128)} %shard_map.75), calls=%async_computation.1 | async-start | bytes 524288 | tf_op jit(solution)/shard_map/all_to_all | solution.py:562
  30.2 0.6 copy-done.5
  30.9 8.7 %shard_map.74.later_ref = f32[32,13,128]{2,1,0:T(8,128)} custom-call(s32[16]{0:T(128)S(1)} %copy-done.5, s32[16]{0:T(128)S(1)} %copy-done.6, s32[2,16]{1,0:T(2,128)S(1)} %convert_element_type.14.anchors_ref, s32[24,128]{1,0:T(8,128)S(1)} %get-tuple-element.10.ranges_ref, f32[3,8192]{1,0:T(4,128)S(1)} %copy-done, ...), custom_call_target="tpu_custom_call" | custom-call | flops 6000000000 | bytes 1000000 | tf_op jit(solution)/shard_map/pallas_call | solution.py:30
  39.6 0.8 all-to-all-done.1.cells_ref
  40.5 1.3 %collective-permute-start.3 = (f32[3,128,128]{2,1,0:T(8,128)S(1)}, f32[3,128,128]{2,1,0:T(8,128)S(1)}, u32[]{:S(2)}, u32[]{:S(2)}) collective-permute-start(f32[3,128,128]{2,1,0:T(8,128)S(1)} %shard_map.76.own_ref), channel_id=1, source_target_pairs={{1,0},{2,1},{3,2},{5,4},{6,5},{7,6},{9,8},{10,9},{11,10},{13,12},{... | collective-permute-start | bytes 589832 | tf_op jit(solution)/shard_map/ppermute | solution.py:542
  41.8 4.6 %collective-permute-start.2 = (f32[3,128,128]{2,1,0:T(8,128)S(1)}, f32[3,128,128]{2,1,0:T(8,128)S(1)}, u32[]{:S(2)}, u32[]{:S(2)}) collective-permute-start(f32[3,128,128]{2,1,0:T(8,128)S(1)} %shard_map.76.own_ref), channel_id=1, source_target_pairs={{0,1},{1,2},{2,3},{4,5},{5,6},{6,7},{8,9},{9,10},{10,11},{12,13},{... | collective-permute-start | bytes 589832 | tf_op jit(solution)/shard_map/ppermute | solution.py:542
  46.3 3.5 %all-to-all-start = ((f32[32,13,128]{2,1,0:T(8,128)}), f32[32,13,128]{2,1,0:T(8,128)S(1)}, u32[]{:S(2)}, u32[]{:S(2)}) async-start(f32[32,13,128]{2,1,0:T(8,128)} %shard_map.74.later_ref), calls=%async_computation | async-start | bytes 524288 | tf_op jit(solution)/shard_map/all_to_all | solution.py:562
  49.9 1.1 collective-permute-done.2.below_ref
  50.9 13.1 %shard_map.77.force_ref = f32[32,12,128]{2,1,0:T(8,128)S(1)} custom-call(s32[512]{0:T(512)S(1)} %copy-done.3, s32[512]{0:T(512)S(1)} %copy-done.4, f32[3,128,128]{2,1,0:T(8,128)S(1)} %collective-permute-done.2.below_ref, f32[3,128,128]{2,1,0:T(8,128)S(1)} %shard_map.76.own_ref, f32[3,128,128]{2,1,0:T(8,128)S(1)} %collective-permute-done.3.above_ref), custom_call_target="tpu_custom_call" | custom-call | flops 14000000000 | bytes 1000000 | tf_op jit(solution)/shard_map/pallas_call | solution.py:30
  64.0 0.9 shard_map.78
  64.9 1.3 %collective-permute-start.5 = (f32[3,128,128]{2,1,0:T(8,128)S(1)}, f32[3,128,128]{2,1,0:T(8,128)S(1)}, u32[]{:S(2)}, u32[]{:S(2)}) collective-permute-start(f32[3,128,128]{2,1,0:T(8,128)S(1)} %get-tuple-element.13.own_ref), channel_id=1, source_target_pairs={{1,0},{2,1},{3,2},{5,4},{6,5},{7,6},{9,8},{10,9},{11,10},{13,12},{... | collective-permute-start | bytes 589832 | tf_op jit(solution)/shard_map/ppermute | solution.py:542
  66.2 5.0 %collective-permute-start.4 = (f32[3,128,128]{2,1,0:T(8,128)S(1)}, f32[3,128,128]{2,1,0:T(8,128)S(1)}, u32[]{:S(2)}, u32[]{:S(2)}) collective-permute-start(f32[3,128,128]{2,1,0:T(8,128)S(1)} %get-tuple-element.13.own_ref), channel_id=1, source_target_pairs={{0,1},{1,2},{2,3},{4,5},{5,6},{6,7},{8,9},{9,10},{10,11},{12,13},{... | collective-permute-start | bytes 589832 | tf_op jit(solution)/shard_map/ppermute | solution.py:542
  71.3 4.2 %all-to-all-start.3 = ((f32[32,15,128]{2,1,0:T(8,128)}), f32[32,15,128]{2,1,0:T(8,128)S(1)}, u32[]{:S(2)}, u32[]{:S(2)}) async-start(f32[32,15,128]{2,1,0:T(8,128)} %get-tuple-element.14), calls=%async_computation.3 | async-start | bytes 524288 | tf_op jit(solution)/shard_map/all_to_all | solution.py:562
  75.4 13.8 %shard_map.79 = f32[32,12,128]{2,1,0:T(8,128)} custom-call(s32[512]{0:T(512)S(1)} %copy-done.3, s32[512]{0:T(512)S(1)} %copy-done.4, f32[3,128,128]{2,1,0:T(8,128)S(1)} %collective-permute-done.4.below_ref, f32[3,128,128]{2,1,0:T(8,128)S(1)} %get-tuple-element.13.own_ref, f32[3,128,128]{2,1,0:T(8,128)S(1)} %collective-permute-done.5.above_ref), custom_call_target="tpu_custom_call" | custom-call | flops 14000000000 | bytes 1000000 | tf_op jit(solution)/shard_map/pallas_call | solution.py:30
  89.2 5.7 %all-to-all-start.2 = ((f32[32,12,128]{2,1,0:T(8,128)}), f32[32,12,128]{2,1,0:T(8,128)S(1)}, u32[]{:S(2)}, u32[]{:S(2)}) async-start(f32[32,12,128]{2,1,0:T(8,128)} %shard_map.79), calls=%async_computation.2 | async-start | bytes 524288 | tf_op jit(solution)/shard_map/all_to_all | solution.py:562
  94.9 4.1 %shard_map.80.base_ref = f32[3,8192]{1,0:T(4,128)S(1)} custom-call(s32[16]{0:T(128)S(1)} %copy-done.5, s32[16]{0:T(128)S(1)} %copy-done.6, s32[2,16]{1,0:T(2,128)S(1)} %convert_element_type.14.anchors_ref, s32[24,128]{1,0:T(8,128)S(1)} %get-tuple-element.10.ranges_ref, s32[64,128]{1,0:T(8,128)S(1)} %get-tuple-element.11.slot_ref, ...), custom_call_target="tpu_custom_call" | custom-call | flops 6000000000 | bytes 1000000 | tf_op jit(solution)/shard_map/pallas_call | solution.py:30
  99.0 6.1 %all-to-all-done.2.back_ref = f32[32,12,128]{2,1,0:T(8,128)S(1)} async-done(((f32[32,12,128]{2,1,0:T(8,128)}), f32[32,12,128]{2,1,0:T(8,128)S(1)}, u32[]{:S(2)}, u32[]{:S(2)}) %all-to-all-start.2) | async-done | bytes 196640 | tf_op jit(solution)/shard_map/all_to_all | solution.py:562
  105.1 3.8 %shard_map.81 = f32[3,8192]{1,0:T(4,128)} custom-call(s32[24,128]{1,0:T(8,128)S(1)} %get-tuple-element.10.ranges_ref, s32[64,128]{1,0:T(8,128)S(1)} %get-tuple-element.11.slot_ref, f32[32,12,128]{2,1,0:T(8,128)S(1)} %all-to-all-done.2.back_ref, f32[3,8192]{1,0:T(4,128)S(1)} %shard_map.80.base_ref), custom_call_target="tpu_custom_call" | custom-call | flops 4000000000 | bytes 1000000 | tf_op jit(solution)/shard_map/pallas_call | solution.py:30
  (24 shorter events, 0.2 us)
Async XLA Ops:
  0.0 14.7 %collective-permute-start.1 = (f32[3,8192]{1,0:T(4,128)}, f32[3,8192]{1,0:T(4,128)S(1)}, u32[]{:S(2)}, u32[]{:S(2)}) collective-permute-start(f32[3,8192]{1,0:T(4,128)} %x_ref.3), channel_id=1, source_target_pairs={{1,0},{2,1},{3,2},{4,3},{5,4},{6,5},{7,6},{8,7},{9,8},{10,9},{11,1... | collective-permute-start | bytes 294920 | tf_op jit(solution)/shard_map/ppermute | solution.py:542
  2.0 6.6 %copy-start.2 = (s32[8192,1]{0,1:T(1,128)S(1)}, s32[8192,1]{0,1:T(1,128)}, u32[]{:S(2)}) copy-start(s32[8192,1]{0,1:T(1,128)} %param.9) | copy-start | bytes 98308
  3.0 11.6 %collective-permute-start = (f32[4,8192]{1,0:T(4,128)S(1)}, f32[4,8192]{1,0:T(4,128)S(1)}, u32[]{:S(2)}, u32[]{:S(2)}) collective-permute-start(f32[4,8192]{1,0:T(4,128)S(1)} %pad_maximum_fusion), channel_id=1, source_target_pairs={{0,1},{1,2},{2,3},{3,4},{4,5},{5,6},{6,7},{7,8},{8,9},{9,10},{10,1... | collective-permute-start | bytes 393224 | tf_op jit(solution)/shard_map/ppermute | solution.py:542
  8.6 6.1 %copy-start = (f32[3,8192]{1,0:T(4,128)S(1)}, f32[3,8192]{1,0:T(4,128)}, u32[]{:S(2)}) copy-start(f32[3,8192]{1,0:T(4,128)} %x_ref.3) | copy-start | bytes 294916
  22.2 8.0 %copy-start.1 = (f32[2,3,8192]{2,0,1:T(2,128)S(1)}, f32[2,3,8192]{2,0,1:T(2,128)}, u32[]{:S(2)}) copy-start(f32[2,3,8192]{2,0,1:T(2,128)} %param.8) | copy-start | bytes 589828
  22.2 18.2 %all-to-all-start.1 = ((f32[32,12,128]{2,1,0:T(8,128)}), f32[32,12,128]{2,1,0:T(8,128)S(1)}, u32[]{:S(2)}, u32[]{:S(2)}) async-start(f32[32,12,128]{2,1,0:T(8,128)} %shard_map.75), calls=%async_computation.1 | async-start | bytes 524288 | tf_op jit(solution)/shard_map/all_to_all | solution.py:562
  30.2 0.7 copy-start.5
  30.2 0.7 copy-start.6
  40.5 10.5 %copy-start.3 = (s32[512]{0:T(512)S(1)}, s32[512]{0:T(512)}, u32[]{:S(2)}) copy-start(s32[512]{0:T(512)} %rows_ref.3) | copy-start | bytes 6148
  40.5 10.5 %copy-start.4 = (s32[512]{0:T(512)S(1)}, s32[512]{0:T(512)}, u32[]{:S(2)}) copy-start(s32[512]{0:T(512)} %cols_ref.3) | copy-start | bytes 6148
  40.5 9.4 %collective-permute-start.3 = (f32[3,128,128]{2,1,0:T(8,128)S(1)}, f32[3,128,128]{2,1,0:T(8,128)S(1)}, u32[]{:S(2)}, u32[]{:S(2)}) collective-permute-start(f32[3,128,128]{2,1,0:T(8,128)S(1)} %shard_map.76.own_ref), channel_id=1, source_target_pairs={{1,0},{2,1},{3,2},{5,4},{6,5},{7,6},{9,8},{10,9},{11,10},{13,12},{... | collective-permute-start | bytes 589832 | tf_op jit(solution)/shard_map/ppermute | solution.py:542
  41.8 9.1 %collective-permute-start.2 = (f32[3,128,128]{2,1,0:T(8,128)S(1)}, f32[3,128,128]{2,1,0:T(8,128)S(1)}, u32[]{:S(2)}, u32[]{:S(2)}) collective-permute-start(f32[3,128,128]{2,1,0:T(8,128)S(1)} %shard_map.76.own_ref), channel_id=1, source_target_pairs={{0,1},{1,2},{2,3},{4,5},{5,6},{6,7},{8,9},{9,10},{10,11},{12,13},{... | collective-permute-start | bytes 589832 | tf_op jit(solution)/shard_map/ppermute | solution.py:542
  46.3 17.6 %all-to-all-start = ((f32[32,13,128]{2,1,0:T(8,128)}), f32[32,13,128]{2,1,0:T(8,128)S(1)}, u32[]{:S(2)}, u32[]{:S(2)}) async-start(f32[32,13,128]{2,1,0:T(8,128)} %shard_map.74.later_ref), calls=%async_computation | async-start | bytes 524288 | tf_op jit(solution)/shard_map/all_to_all | solution.py:562
  64.9 10.5 %collective-permute-start.5 = (f32[3,128,128]{2,1,0:T(8,128)S(1)}, f32[3,128,128]{2,1,0:T(8,128)S(1)}, u32[]{:S(2)}, u32[]{:S(2)}) collective-permute-start(f32[3,128,128]{2,1,0:T(8,128)S(1)} %get-tuple-element.13.own_ref), channel_id=1, source_target_pairs={{1,0},{2,1},{3,2},{5,4},{6,5},{7,6},{9,8},{10,9},{11,10},{13,12},{... | collective-permute-start | bytes 589832 | tf_op jit(solution)/shard_map/ppermute | solution.py:542
  66.2 9.2 %collective-permute-start.4 = (f32[3,128,128]{2,1,0:T(8,128)S(1)}, f32[3,128,128]{2,1,0:T(8,128)S(1)}, u32[]{:S(2)}, u32[]{:S(2)}) collective-permute-start(f32[3,128,128]{2,1,0:T(8,128)S(1)} %get-tuple-element.13.own_ref), channel_id=1, source_target_pairs={{0,1},{1,2},{2,3},{4,5},{5,6},{6,7},{8,9},{9,10},{10,11},{12,13},{... | collective-permute-start | bytes 589832 | tf_op jit(solution)/shard_map/ppermute | solution.py:542
  71.3 17.9 %all-to-all-start.3 = ((f32[32,15,128]{2,1,0:T(8,128)}), f32[32,15,128]{2,1,0:T(8,128)S(1)}, u32[]{:S(2)}, u32[]{:S(2)}) async-start(f32[32,15,128]{2,1,0:T(8,128)} %get-tuple-element.14), calls=%async_computation.3 | async-start | bytes 524288 | tf_op jit(solution)/shard_map/all_to_all | solution.py:562
  89.2 15.9 %all-to-all-start.2 = ((f32[32,12,128]{2,1,0:T(8,128)}), f32[32,12,128]{2,1,0:T(8,128)S(1)}, u32[]{:S(2)}, u32[]{:S(2)}) async-start(f32[32,12,128]{2,1,0:T(8,128)} %shard_map.79), calls=%async_computation.2 | async-start | bytes 524288 | tf_op jit(solution)/shard_map/all_to_all | solution.py:562

commit v7 on v6

--- a/solution.py
+++ b/solution.py
@@ -52,33 +52,43 @@
 
 def fill_slots(index_ref, ranges_ref, source_ref, out_ref, per_owner):
     fields = source_ref.shape[0]
-    at_once = 16
+    rows = source_ref.shape[1] // lanes
+    part = rows * 5 // 8
 
     def one(group, carry):
         first_owner = lax.div(group, per_owner) * 8
         k = lax.rem(group, per_owner)
-        code = index_ref[pl.ds(first_owner * per_owner + k, 8, stride=per_owner), :]
-        row_of = (code >> 7) - 1
-        lane_of = code & 127
         least = -ranges_ref[k, first_owner]
         end = ranges_ref[per_owner + k, first_owner]
 
-        def search(chunk, held):
-            held = list(held)
-            for i in range(at_once):
-                j = chunk * at_once + i
-                here = row_of == j
-                at = pl.ds(pl.multiple_of(j * lanes, lanes), lanes)
+        def search(first, length):
+            code = index_ref[pl.ds(first_owner * per_owner + k, 8, stride=per_owner), :]
+            row_of = (code >> 7) - 1
+            lane_of = code & 127
+            held = [jnp.full((8, lanes), far_away, f32) for _ in range(fields)]
+            for i in range(length):
+                here = row_of == first + i
+                at = pl.ds(pl.multiple_of((first + i) * lanes, lanes), lanes)
                 for c in range(fields):
                     held[c] = jnp.where(here, pick(source_ref[c : c + 1, at], lane_of), held[c])
-            return tuple(held)
-
-        empty = tuple(jnp.full((8, lanes), far_away, f32) for _ in range(fields))
-        chunks = (lax.div(least, at_once), lax.div(end + at_once - 1, at_once))
-        held = lax.fori_loop(*chunks, search, empty)
-        for i in range(8):
-            for c in range(fields):
-                out_ref[first_owner + i, pl.ds(c * per_owner + k, 1), :] = held[c][i : i + 1, :]
+            for i in range(8):
+                for c in range(fields):
+                    out_ref[first_owner + i, pl.ds(c * per_owner + k, 1), :] = held[c][i : i + 1, :]
+
+        fits = end - least <= part
+
+        @pl.when(end <= least)
+        def _():
+            search(0, 0)
+
+        @pl.when(jnp.logical_and(fits, end > least))
+        def _():
+            search(jnp.minimum(least, rows - part), part)
+
+        @pl.when(jnp.logical_not(fits))
+        def _():
+            search(0, rows)
+
         return carry
 
     lax.fori_loop(0, index_ref.shape[0] // 8, one, 0)

time: 109 us -> 107 us (0.982)
  waiting for transfers between devices: 7.96 us -> 11.8 us
  Pallas kernels: 57.9 us -> 54.1 us
  starting transfers between devices: 40.3 us -> 38.3 us
    pallas_call x9, Pallas kernels: 57.9 us -> 54.1 us  [call(): pl.pallas_call(body, out_shape=outs, in_specs=in_specs, out_specs=[vmem]...]
    all_to_all x4, starting transfers between devices: 21.3 us -> 19.3 us  [exchange(): return lax.all_to_all(value, both, split_axis=0, concat_axis=0, tiled=True)]
    all_to_all x4, waiting for transfers between devices: 6.89 us -> 8.83 us  [exchange(): return lax.all_to_all(value, both, split_axis=0, concat_axis=0, tiled=True)]
    ppermute x6, waiting for transfers between devices: 1.07 us -> 2.99 us  [shifted(): lax.ppermute(value, axis, [(source, source + steps) for source in range(f...]
  transfers between devices with their start and end apart: 10 -> 10, of which waited for: 3 -> 5; matrix products, arithmetic and copies ran while one was open for 2% -> 2% of each run, Pallas kernels for 42% -> 41%
where the time goes in v7:
time: 107 us
  Pallas kernels  54.1 us (51%)
  starting transfers between devices  38.3 us (36%)
  waiting for transfers between devices  11.8 us (11%)
  other arithmetic  1.75 us (2%)
    pallas_call x9, Pallas kernels, call(): pl.pallas_call(body, out_shape=outs, in_specs=in_specs, out_specs=[vmem]...  54.1 us
    all_to_all x4, starting transfers between devices, exchange(): return lax.all_to_all(value, both, split_axis=0, concat_axis=0, tiled=True)  19.3 us
    ppermute x6, starting transfers between devices, shifted(): lax.ppermute(value, axis, [(source, source + steps) for source in range(f...  19 us
    all_to_all x4, waiting for transfers between devices, exchange(): return lax.all_to_all(value, both, split_axis=0, concat_axis=0, tiled=True)  8.83 us
    ppermute x6, waiting for transfers between devices, shifted(): lax.ppermute(value, axis, [(source, source + steps) for source in range(f...  2.99 us
  transfers between devices with their start and end apart: 10, of which 5 were waited for; matrix products, arithmetic and copies ran while one was open for 2% of the time, Pallas kernels for 41%

profile of v7, /device:TPU:0, one launch (start us, length us, event | category | flops | bytes accessed | tf_op | source)
XLA Modules:
  0.0 106.9 jit_solution(250733564032367696)
XLA Ops:
  0.0 1.3 %collective-permute-start.1 = (f32[3,8192]{1,0:T(4,128)}, f32[3,8192]{1,0:T(4,128)S(1)}, u32[]{:S(2)}, u32[]{:S(2)}) collective-permute-start(f32[3,8192]{1,0:T(4,128)} %x_ref.3), channel_id=1, source_target_pairs={{1,0},{2,1},{3,2},{4,3},{5,4},{6,5},{7,6},{8,7},{9,8},{10,9},{11,1... | collective-permute-start | bytes 294920 | tf_op jit(solution)/shard_map/ppermute | solution.py:552
  1.3 0.8 add_convert_fusion
  2.0 1.0 pad_maximum_fusion
  3.0 5.6 %collective-permute-start = (f32[4,8192]{1,0:T(4,128)S(1)}, f32[4,8192]{1,0:T(4,128)S(1)}, u32[]{:S(2)}, u32[]{:S(2)}) collective-permute-start(f32[4,8192]{1,0:T(4,128)S(1)} %pad_maximum_fusion), channel_id=1, source_target_pairs={{0,1},{1,2},{2,3},{3,4},{4,5},{5,6},{6,7},{7,8},{8,9},{9,10},{10,1... | collective-permute-start | bytes 393224 | tf_op jit(solution)/shard_map/ppermute | solution.py:552
  8.6 6.0 %shard_map.73 = (s32[128,128]{1,0:T(8,128)S(1)}, s32[64,128]{1,0:T(8,128)S(1)}, s32[24,128]{1,0:T(8,128)S(1)}) custom-call(s32[64,128]{1,0:T(8,128)S(1)} %bitcast.5), custom_call_target="tpu_custom_call" | custom-call | flops 6000000000 | bytes 1000000 | tf_op jit(solution)/shard_map/pallas_call | solution.py:30
  14.7 5.6 %shard_map.75 = f32[32,12,128]{2,1,0:T(8,128)} custom-call(s32[24,128]{1,0:T(8,128)S(1)} %get-tuple-element.10.ranges_ref, s32[128,128]{1,0:T(8,128)S(1)} %get-tuple-element.12.index_ref, f32[3,8192]{1,0:T(4,128)S(1)} %copy-done, f32[3,8192]{1,0:T(4,128)S(1)} %collective-permute-done.1.after_ref, f32[4,8192]{1,0:T(4,128)S(1)} %collective-permute-done.before_ref), custom_call_target="tpu_custom_call" | custom-call | flops 4000000000 | bytes 1000000 | tf_op jit(solution)/shard_map/pallas_call | solution.py:30
  20.3 7.9 %all-to-all-start.1 = ((f32[32,12,128]{2,1,0:T(8,128)}), f32[32,12,128]{2,1,0:T(8,128)S(1)}, u32[]{:S(2)}, u32[]{:S(2)}) async-start(f32[32,12,128]{2,1,0:T(8,128)} %shard_map.75), calls=%async_computation.1 | async-start | bytes 524288 | tf_op jit(solution)/shard_map/all_to_all | solution.py:572
  28.9 6.8 %shard_map.74.later_ref = f32[32,13,128]{2,1,0:T(8,128)} custom-call(s32[16]{0:T(128)S(1)} %copy-done.5, s32[16]{0:T(128)S(1)} %copy-done.6, s32[2,16]{1,0:T(2,128)S(1)} %convert_element_type.14.anchors_ref, s32[24,128]{1,0:T(8,128)S(1)} %get-tuple-element.10.ranges_ref, f32[3,8192]{1,0:T(4,128)S(1)} %copy-done, ...), custom_call_target="tpu_custom_call" | custom-call | flops 6000000000 | bytes 1000000 | tf_op jit(solution)/shard_map/pallas_call | solution.py:30
  35.7 2.7 %all-to-all-done.1.cells_ref = f32[32,12,128]{2,1,0:T(8,128)S(1)} async-done(((f32[32,12,128]{2,1,0:T(8,128)}), f32[32,12,128]{2,1,0:T(8,128)S(1)}, u32[]{:S(2)}, u32[]{:S(2)}) %all-to-all-start.1) | async-done | bytes 196640 | tf_op jit(solution)/shard_map/all_to_all | solution.py:572
  38.5 1.3 %collective-permute-start.3 = (f32[3,128,128]{2,1,0:T(8,128)S(1)}, f32[3,128,128]{2,1,0:T(8,128)S(1)}, u32[]{:S(2)}, u32[]{:S(2)}) collective-permute-start(f32[3,128,128]{2,1,0:T(8,128)S(1)} %shard_map.76.own_ref), channel_id=1, source_target_pairs={{1,0},{2,1},{3,2},{5,4},{6,5},{7,6},{9,8},{10,9},{11,10},{13,12},{... | collective-permute-start | bytes 589832 | tf_op jit(solution)/shard_map/ppermute | solution.py:552
  39.8 4.6 %collective-permute-start.2 = (f32[3,128,128]{2,1,0:T(8,128)S(1)}, f32[3,128,128]{2,1,0:T(8,128)S(1)}, u32[]{:S(2)}, u32[]{:S(2)}) collective-permute-start(f32[3,128,128]{2,1,0:T(8,128)S(1)} %shard_map.76.own_ref), channel_id=1, source_target_pairs={{0,1},{1,2},{2,3},{4,5},{5,6},{6,7},{8,9},{9,10},{10,11},{12,13},{... | collective-permute-start | bytes 589832 | tf_op jit(solution)/shard_map/ppermute | solution.py:552
  44.3 2.6 %all-to-all-start = ((f32[32,13,128]{2,1,0:T(8,128)}), f32[32,13,128]{2,1,0:T(8,128)S(1)}, u32[]{:S(2)}, u32[]{:S(2)}) async-start(f32[32,13,128]{2,1,0:T(8,128)} %shard_map.74.later_ref), calls=%async_computation | async-start | bytes 524288 | tf_op jit(solution)/shard_map/all_to_all | solution.py:572
  47.0 0.7 collective-permute-done.3.above_ref
  47.6 2.0 %collective-permute-done.2.below_ref = f32[3,128,128]{2,1,0:T(8,128)S(1)} collective-permute-done((f32[3,128,128]{2,1,0:T(8,128)S(1)}, f32[3,128,128]{2,1,0:T(8,128)S(1)}, u32[]{:S(2)}, u32[]{:S(2)}) %collective-permute-start.2) | collective-permute-done | bytes 196640 | tf_op jit(solution)/shard_map/ppermute | solution.py:552
  49.6 13.1 %shard_map.77.force_ref = f32[32,12,128]{2,1,0:T(8,128)S(1)} custom-call(s32[512]{0:T(512)S(1)} %copy-done.3, s32[512]{0:T(512)S(1)} %copy-done.4, f32[3,128,128]{2,1,0:T(8,128)S(1)} %collective-permute-done.2.below_ref, f32[3,128,128]{2,1,0:T(8,128)S(1)} %shard_map.76.own_ref, f32[3,128,128]{2,1,0:T(8,128)S(1)} %collective-permute-done.3.above_ref), custom_call_target="tpu_custom_call" | custom-call | flops 14000000000 | bytes 1000000 | tf_op jit(solution)/shard_map/pallas_call | solution.py:30
  62.7 0.9 shard_map.78
  63.6 1.3 %collective-permute-start.5 = (f32[3,128,128]{2,1,0:T(8,128)S(1)}, f32[3,128,128]{2,1,0:T(8,128)S(1)}, u32[]{:S(2)}, u32[]{:S(2)}) collective-permute-start(f32[3,128,128]{2,1,0:T(8,128)S(1)} %get-tuple-element.13.own_ref), channel_id=1, source_target_pairs={{1,0},{2,1},{3,2},{5,4},{6,5},{7,6},{9,8},{10,9},{11,10},{13,12},{... | collective-permute-start | bytes 589832 | tf_op jit(solution)/shard_map/ppermute | solution.py:552
  64.9 5.0 %collective-permute-start.4 = (f32[3,128,128]{2,1,0:T(8,128)S(1)}, f32[3,128,128]{2,1,0:T(8,128)S(1)}, u32[]{:S(2)}, u32[]{:S(2)}) collective-permute-start(f32[3,128,128]{2,1,0:T(8,128)S(1)} %get-tuple-element.13.own_ref), channel_id=1, source_target_pairs={{0,1},{1,2},{2,3},{4,5},{5,6},{6,7},{8,9},{9,10},{10,11},{12,13},{... | collective-permute-start | bytes 589832 | tf_op jit(solution)/shard_map/ppermute | solution.py:552
  69.9 2.8 %all-to-all-start.3 = ((f32[32,15,128]{2,1,0:T(8,128)}), f32[32,15,128]{2,1,0:T(8,128)S(1)}, u32[]{:S(2)}, u32[]{:S(2)}) async-start(f32[32,15,128]{2,1,0:T(8,128)} %get-tuple-element.14), calls=%async_computation.3 | async-start | bytes 524288 | tf_op jit(solution)/shard_map/all_to_all | solution.py:572
  73.1 13.8 %shard_map.79 = f32[32,12,128]{2,1,0:T(8,128)} custom-call(s32[512]{0:T(512)S(1)} %copy-done.3, s32[512]{0:T(512)S(1)} %copy-done.4, f32[3,128,128]{2,1,0:T(8,128)S(1)} %collective-permute-done.4.below_ref, f32[3,128,128]{2,1,0:T(8,128)S(1)} %get-tuple-element.13.own_ref, f32[3,128,128]{2,1,0:T(8,128)S(1)} %collective-permute-done.5.above_ref), custom_call_target="tpu_custom_call" | custom-call | flops 14000000000 | bytes 1000000 | tf_op jit(solution)/shard_map/pallas_call | solution.py:30
  86.8 6.0 %all-to-all-start.2 = ((f32[32,12,128]{2,1,0:T(8,128)}), f32[32,12,128]{2,1,0:T(8,128)S(1)}, u32[]{:S(2)}, u32[]{:S(2)}) async-start(f32[32,12,128]{2,1,0:T(8,128)} %shard_map.79), calls=%async_computation.2 | async-start | bytes 524288 | tf_op jit(solution)/shard_map/all_to_all | solution.py:572
  92.9 4.1 %shard_map.80.base_ref = f32[3,8192]{1,0:T(4,128)S(1)} custom-call(s32[16]{0:T(128)S(1)} %copy-done.5, s32[16]{0:T(128)S(1)} %copy-done.6, s32[2,16]{1,0:T(2,128)S(1)} %convert_element_type.14.anchors_ref, s32[24,128]{1,0:T(8,128)S(1)} %get-tuple-element.10.ranges_ref, s32[64,128]{1,0:T(8,128)S(1)} %get-tuple-element.11.slot_ref, ...), custom_call_target="tpu_custom_call" | custom-call | flops 6000000000 | bytes 1000000 | tf_op jit(solution)/shard_map/pallas_call | solution.py:30
  97.0 6.1 %all-to-all-done.2.back_ref = f32[32,12,128]{2,1,0:T(8,128)S(1)} async-done(((f32[32,12,128]{2,1,0:T(8,128)}), f32[32,12,128]{2,1,0:T(8,128)S(1)}, u32[]{:S(2)}, u32[]{:S(2)}) %all-to-all-start.2) | async-done | bytes 196640 | tf_op jit(solution)/shard_map/all_to_all | solution.py:572
  103.1 3.8 %shard_map.81 = f32[3,8192]{1,0:T(4,128)} custom-call(s32[24,128]{1,0:T(8,128)S(1)} %get-tuple-element.10.ranges_ref, s32[64,128]{1,0:T(8,128)S(1)} %get-tuple-element.11.slot_ref, f32[32,12,128]{2,1,0:T(8,128)S(1)} %all-to-all-done.2.back_ref, f32[3,8192]{1,0:T(4,128)S(1)} %shard_map.80.base_ref), custom_call_target="tpu_custom_call" | custom-call | flops 4000000000 | bytes 1000000 | tf_op jit(solution)/shard_map/pallas_call | solution.py:30
  (24 shorter events, 1.2 us)
Async XLA Ops:
  0.0 14.7 %collective-permute-start.1 = (f32[3,8192]{1,0:T(4,128)}, f32[3,8192]{1,0:T(4,128)S(1)}, u32[]{:S(2)}, u32[]{:S(2)}) collective-permute-start(f32[3,8192]{1,0:T(4,128)} %x_ref.3), channel_id=1, source_target_pairs={{1,0},{2,1},{3,2},{4,3},{5,4},{6,5},{7,6},{8,7},{9,8},{10,9},{11,1... | collective-permute-start | bytes 294920 | tf_op jit(solution)/shard_map/ppermute | solution.py:552
  2.0 6.6 %copy-start.2 = (s32[8192,1]{0,1:T(1,128)S(1)}, s32[8192,1]{0,1:T(1,128)}, u32[]{:S(2)}) copy-start(s32[8192,1]{0,1:T(1,128)} %param.9) | copy-start | bytes 98308
  3.0 11.6 %collective-permute-start = (f32[4,8192]{1,0:T(4,128)S(1)}, f32[4,8192]{1,0:T(4,128)S(1)}, u32[]{:S(2)}, u32[]{:S(2)}) collective-permute-start(f32[4,8192]{1,0:T(4,128)S(1)} %pad_maximum_fusion), channel_id=1, source_target_pairs={{0,1},{1,2},{2,3},{3,4},{4,5},{5,6},{6,7},{7,8},{8,9},{9,10},{10,1... | collective-permute-start | bytes 393224 | tf_op jit(solution)/shard_map/ppermute | solution.py:552
  8.6 6.1 %copy-start = (f32[3,8192]{1,0:T(4,128)S(1)}, f32[3,8192]{1,0:T(4,128)}, u32[]{:S(2)}) copy-start(f32[3,8192]{1,0:T(4,128)} %x_ref.3) | copy-start | bytes 294916
  20.3 7.9 %copy-start.1 = (f32[2,3,8192]{2,0,1:T(2,128)S(1)}, f32[2,3,8192]{2,0,1:T(2,128)}, u32[]{:S(2)}) copy-start(f32[2,3,8192]{2,0,1:T(2,128)} %param.8) | copy-start | bytes 589828
  20.3 18.1 %all-to-all-start.1 = ((f32[32,12,128]{2,1,0:T(8,128)}), f32[32,12,128]{2,1,0:T(8,128)S(1)}, u32[]{:S(2)}, u32[]{:S(2)}) async-start(f32[32,12,128]{2,1,0:T(8,128)} %shard_map.75), calls=%async_computation.1 | async-start | bytes 524288 | tf_op jit(solution)/shard_map/all_to_all | solution.py:572
  28.2 0.7 copy-start.5
  28.2 0.7 copy-start.6
  38.5 11.1 %copy-start.3 = (s32[512]{0:T(512)S(1)}, s32[512]{0:T(512)}, u32[]{:S(2)}) copy-start(s32[512]{0:T(512)} %rows_ref.3) | copy-start | bytes 6148
  38.5 11.1 %copy-start.4 = (s32[512]{0:T(512)S(1)}, s32[512]{0:T(512)}, u32[]{:S(2)}) copy-start(s32[512]{0:T(512)} %cols_ref.3) | copy-start | bytes 6148
  38.5 9.1 %collective-permute-start.3 = (f32[3,128,128]{2,1,0:T(8,128)S(1)}, f32[3,128,128]{2,1,0:T(8,128)S(1)}, u32[]{:S(2)}, u32[]{:S(2)}) collective-permute-start(f32[3,128,128]{2,1,0:T(8,128)S(1)} %shard_map.76.own_ref), channel_id=1, source_target_pairs={{1,0},{2,1},{3,2},{5,4},{6,5},{7,6},{9,8},{10,9},{11,10},{13,12},{... | collective-permute-start | bytes 589832 | tf_op jit(solution)/shard_map/ppermute | solution.py:552
  39.8 9.8 %collective-permute-start.2 = (f32[3,128,128]{2,1,0:T(8,128)S(1)}, f32[3,128,128]{2,1,0:T(8,128)S(1)}, u32[]{:S(2)}, u32[]{:S(2)}) collective-permute-start(f32[3,128,128]{2,1,0:T(8,128)S(1)} %shard_map.76.own_ref), channel_id=1, source_target_pairs={{0,1},{1,2},{2,3},{4,5},{5,6},{6,7},{8,9},{9,10},{10,11},{12,13},{... | collective-permute-start | bytes 589832 | tf_op jit(solution)/shard_map/ppermute | solution.py:552
  44.3 18.3 %all-to-all-start = ((f32[32,13,128]{2,1,0:T(8,128)}), f32[32,13,128]{2,1,0:T(8,128)S(1)}, u32[]{:S(2)}, u32[]{:S(2)}) async-start(f32[32,13,128]{2,1,0:T(8,128)} %shard_map.74.later_ref), calls=%async_computation | async-start | bytes 524288 | tf_op jit(solution)/shard_map/all_to_all | solution.py:572
  63.6 9.1 %collective-permute-start.5 = (f32[3,128,128]{2,1,0:T(8,128)S(1)}, f32[3,128,128]{2,1,0:T(8,128)S(1)}, u32[]{:S(2)}, u32[]{:S(2)}) collective-permute-start(f32[3,128,128]{2,1,0:T(8,128)S(1)} %get-tuple-element.13.own_ref), channel_id=1, source_target_pairs={{1,0},{2,1},{3,2},{5,4},{6,5},{7,6},{9,8},{10,9},{11,10},{13,12},{... | collective-permute-start | bytes 589832 | tf_op jit(solution)/shard_map/ppermute | solution.py:552
  64.9 8.2 %collective-permute-start.4 = (f32[3,128,128]{2,1,0:T(8,128)S(1)}, f32[3,128,128]{2,1,0:T(8,128)S(1)}, u32[]{:S(2)}, u32[]{:S(2)}) collective-permute-start(f32[3,128,128]{2,1,0:T(8,128)S(1)} %get-tuple-element.13.own_ref), channel_id=1, source_target_pairs={{0,1},{1,2},{2,3},{4,5},{5,6},{6,7},{8,9},{9,10},{10,11},{12,13},{... | collective-permute-start | bytes 589832 | tf_op jit(solution)/shard_map/ppermute | solution.py:552
  69.9 16.9 %all-to-all-start.3 = ((f32[32,15,128]{2,1,0:T(8,128)}), f32[32,15,128]{2,1,0:T(8,128)S(1)}, u32[]{:S(2)}, u32[]{:S(2)}) async-start(f32[32,15,128]{2,1,0:T(8,128)} %get-tuple-element.14), calls=%async_computation.3 | async-start | bytes 524288 | tf_op jit(solution)/shard_map/all_to_all | solution.py:572
  86.8 16.2 %all-to-all-start.2 = ((f32[32,12,128]{2,1,0:T(8,128)}), f32[32,12,128]{2,1,0:T(8,128)S(1)}, u32[]{:S(2)}, u32[]{:S(2)}) async-start(f32[32,12,128]{2,1,0:T(8,128)} %shard_map.79), calls=%async_computation.2 | async-start | bytes 524288 | tf_op jit(solution)/shard_map/all_to_all | solution.py:572

commit v8 on v6

--- a/solution.py
+++ b/solution.py
@@ -50,38 +50,29 @@
     )
 
 
-def fill_slots(index_ref, ranges_ref, source_ref, out_ref, per_owner):
+def fill_slots(index_ref, source_ref, out_ref, per_owner):
+    rows = source_ref.shape[1] // lanes
     fields = source_ref.shape[0]
-    at_once = 16
+    owners_here = 8 // per_owner
 
     def one(group, carry):
-        first_owner = lax.div(group, per_owner) * 8
-        k = lax.rem(group, per_owner)
-        code = index_ref[pl.ds(first_owner * per_owner + k, 8, stride=per_owner), :]
+        code = index_ref[pl.ds(pl.multiple_of(group * 8, 8), 8), :]
         row_of = (code >> 7) - 1
         lane_of = code & 127
-        least = -ranges_ref[k, first_owner]
-        end = ranges_ref[per_owner + k, first_owner]
-
-        def search(chunk, held):
-            held = list(held)
-            for i in range(at_once):
-                j = chunk * at_once + i
-                here = row_of == j
-                at = pl.ds(pl.multiple_of(j * lanes, lanes), lanes)
-                for c in range(fields):
-                    held[c] = jnp.where(here, pick(source_ref[c : c + 1, at], lane_of), held[c])
-            return tuple(held)
-
-        empty = tuple(jnp.full((8, lanes), far_away, f32) for _ in range(fields))
-        chunks = (lax.div(least, at_once), lax.div(end + at_once - 1, at_once))
-        held = lax.fori_loop(*chunks, search, empty)
-        for i in range(8):
+        held = [jnp.full((8, lanes), far_away, f32) for _ in range(fields)]
+        for j in range(rows):
+            here = row_of == j
             for c in range(fields):
-                out_ref[first_owner + i, pl.ds(c * per_owner + k, 1), :] = held[c][i : i + 1, :]
+                row = source_ref[c : c + 1, j * lanes : (j + 1) * lanes]
+                held[c] = jnp.where(here, pick(row, lane_of), held[c])
+        for i in range(owners_here):
+            for c in range(fields):
+                out_ref[group * owners_here + i, c * per_owner : (c + 1) * per_owner, :] = held[c][
+                    i * per_owner : (i + 1) * per_owner, :
+                ]
         return carry
 
-    lax.fori_loop(0, index_ref.shape[0] // 8, one, 0)
+    lax.fori_loop(0, index_ref.shape[0] // 8, one, 0, unroll=4)
 
 
 def index_kernel(devices, owner_ref, index_ref, slot_ref, ranges_ref, turned_ref, total_ref):
@@ -95,21 +86,23 @@
         jnp.where(iota((lanes, 2 * lanes), 0) < iota((lanes, 2 * lanes), 1), 1.0, 0.0),
     ).astype(bf16)
 
+    together = min(devices, 32)
+
     def count(chunk, carry):
         prefix, total = carry
         masks = jnp.concatenate(
-            [jnp.where(own == chunk * 8 + i, 1.0, 0.0) for i in range(8)], axis=0
+            [jnp.where(own == chunk * together + i, 1.0, 0.0) for i in range(together)], axis=0
         ).astype(bf16)
         sums = jnp.dot(masks, tri, preferred_element_type=f32)
-        for i in range(8):
-            o = chunk * 8 + i
+        for i in range(together):
+            o = chunk * together + i
             part = sums[i * rows : (i + 1) * rows]
             prefix = jnp.where(own == o, part[:, :lanes], prefix)
             total = jnp.where(lane == o, part[:, lanes:], total)
         return prefix, total
 
     zero = jnp.zeros((rows, lanes), f32)
-    prefix, total = lax.fori_loop(0, devices // 8, count, (zero, zero))
+    prefix, total = lax.fori_loop(0, devices // together, count, (zero, zero))
     lower = jnp.where(iota((rows, rows), 1) < iota((rows, rows), 0), 1.0, 0.0).astype(bf16)
     above = jnp.dot(lower, total.astype(bf16), preferred_element_type=f32)
     offset = jnp.take_along_axis(above, own, axis=1, mode="promise_in_bounds")
@@ -117,19 +110,6 @@
     slot_ref[...] = slot
 
     upto = above + total
-    count_of = upto[rows - 1 : rows]
-    least, end = [], []
-    for k in range(per_owner):
-        some = count_of > k * lanes
-        first_row = jnp.sum(jnp.where(upto <= k * lanes, 1.0, 0.0), axis=0, keepdims=True)
-        limit = jnp.minimum(count_of, (k + 1.0) * lanes)
-        last_row = jnp.sum(jnp.where(above < limit, 1.0, 0.0), axis=0, keepdims=True)
-        least.append(jnp.where(some, -first_row, -float(rows)))
-        end.append(jnp.where(some, last_row, 0.0))
-    spans = jnp.concatenate(least + end + [jnp.zeros((1, lanes), f32)] * (8 - 2 * per_owner), axis=0)
-    for shift in (1, 2, 4):
-        spans = jnp.maximum(spans, pltpu.roll(spans, lanes - shift, 1))
-    ranges_ref[0:8, :] = spans.astype(jnp.int32)
     total_ref[0:rows, :] = above
     total_ref[rows : 2 * rows, :] = upto
     lowest = total_ref[pl.ds(0, 8, stride=8), :].astype(jnp.int32) >> 7
@@ -137,15 +117,16 @@
     highest = total_ref[pl.ds(rows + 7, 8, stride=8), :].astype(jnp.int32)
     highest = jnp.maximum(highest - 1, 0) >> 7
     more = jnp.max((highest - lowest).astype(f32), axis=1, keepdims=True)
-    ranges_ref[8:16, :] = lowest
-    ranges_ref[16:24, :] = jnp.broadcast_to(more, (8, lanes)).astype(jnp.int32)
+    more = jnp.max(more, axis=0, keepdims=True)
+    ranges_ref[0:8, :] = lowest
+    ranges_ref[8:16, :] = jnp.broadcast_to(more, (8, lanes)).astype(jnp.int32)
 
     turned_ref[...] = jnp.concatenate([slot & 127] * (lanes // rows), axis=0).T
     down = iota((lanes, lanes), 0)
     across = iota((lanes, lanes), 1)
     lane_code = across.astype(f32)
     total_ref[...] = jnp.zeros_like(total_ref)
-    at_once = 8
+    at_once = min(rows, 64)
 
     def spread(chunk, carry):
         left, right = [], []
@@ -173,8 +154,8 @@
     index_ref[...] = (total_ref[0:blocks, :] + lanes * total_ref[blocks:, :]).astype(jnp.int32)
 
 
-def send_kernel(ranges_ref, index_ref, x_ref, after_ref, before_ref, out_ref):
-    fill_slots(index_ref, ranges_ref, x_ref, out_ref, out_ref.shape[1] // 3)
+def send_kernel(index_ref, x_ref, after_ref, before_ref, out_ref):
+    fill_slots(index_ref, x_ref, out_ref, out_ref.shape[1] // 3)
 
 
 def column(block, at):
@@ -263,7 +244,6 @@
     left_ref,
     span_ref,
     anchors_ref,
-    ranges_ref,
     x_ref,
     after_ref,
     before_ref,
@@ -292,7 +272,7 @@
     chain_forces(left_ref, span_ref, anchors_ref, x_ref, ghost, wide_ref, force_ref)
     chain_step(0, x_ref, noise_ref, y_ref, force_ref)
 
-    fill_slots(index_ref, ranges_ref, y_ref, out_ref, per_owner)
+    fill_slots(index_ref, y_ref, out_ref, per_owner)
 
     asked = [(left_ref[e] - me * mono_dev, True) for e in range(extruders)]
     asked += [(b, wanted) for _, b, wanted in found]
@@ -364,7 +344,7 @@
                 near_t[pl.ds(pl.multiple_of(group * lanes, lanes), lanes), :] = spot[...].astype(bf16)
         return carry
 
-    lax.fori_loop(0, blocks // 8, build, 0)
+    lax.fori_loop(0, blocks // 8, build, 0, unroll=2)
     zero = jnp.zeros((lanes, lanes), bf16)
 
     def sixteen(ref, block):
@@ -421,16 +401,16 @@
 
 def take_slots(slot_ref, ranges_ref, source_ref, per_owner, emit):
     owners = source_ref.shape[0]
-
-    def one(group, carry):
-        slot = slot_ref[pl.ds(pl.multiple_of(group * 8, 8), 8), :]
-        row_of = slot >> 7
-        lane_of = slot & 127
-
-        def search(tries, first):
+    groups = slot_ref.shape[0] // 8
+
+    def search(tries, first, unroll):
+        def one(group, carry):
+            slot = slot_ref[pl.ds(pl.multiple_of(group * 8, 8), 8), :]
+            row_of = slot >> 7
+            lane_of = slot & 127
             held = [jnp.zeros((8, lanes), f32) for _ in range(3)]
             for o in range(owners):
-                base = first(o)
+                base = first(group, o)
                 for t in range(tries):
                     k = jnp.minimum(base + t, per_owner - 1)
                     here = row_of == o * per_owner + k
@@ -441,23 +421,22 @@
                 at = pl.ds(pl.multiple_of((group * 8 + i) * lanes, lanes), lanes)
                 for c in range(3):
                     emit(c, at, held[c][i : i + 1, :])
-
-        if per_owner <= 2:
-            search(per_owner, lambda o: 0)
-        else:
-            few = ranges_ref[16 + group, 0] <= 1
-
-            @pl.when(few)
-            def _():
-                search(2, lambda o: ranges_ref[8 + group, o])
-
-            @pl.when(jnp.logical_not(few))
-            def _():
-                search(per_owner, lambda o: 0)
-
-        return carry
-
-    lax.fori_loop(0, slot_ref.shape[0] // 8, one, 0)
+            return carry
+
+        lax.fori_loop(0, groups, one, 0, unroll=unroll)
+
+    if per_owner <= 2:
+        search(per_owner, lambda group, o: 0, 2)
+    else:
+        few = ranges_ref[8, 0] <= 1
+
+        @pl.when(few)
+        def _():
+            search(2, lambda group, o: ranges_ref[group, o], 4)
+
+        @pl.when(jnp.logical_not(few))
+        def _():
+            search(per_owner, lambda group, o: 0, 1)
 
 
 def second_kernel(
@@ -590,7 +569,7 @@
         [
             jax.ShapeDtypeStruct((blocks, lanes), jnp.int32),
             jax.ShapeDtypeStruct((rows, lanes), jnp.int32),
-            jax.ShapeDtypeStruct((24, lanes), jnp.int32),
+            jax.ShapeDtypeStruct((16, lanes), jnp.int32),
         ],
         [vmem],
         (cell_owner.reshape(rows, lanes),),
@@ -600,8 +579,8 @@
     x_out = call(
         send_kernel,
         sent,
-        [smem] + [vmem] * 4,
-        (ranges, index, positions, after, before),
+        [vmem] * 4,
+        (index, positions, after, before),
         micros=4,
     )
     anchors_before = before[3, : 2 * extruders].astype(jnp.int32).reshape(2, extruders)
@@ -609,8 +588,8 @@
     y_out = call(
         first_kernel,
         jax.ShapeDtypeStruct((devices, 3 * per_owner + 1, lanes), f32),
-        [smem] * 4 + [vmem] * 6,
-        (loop_left, loop_span, anchors_before, ranges, positions, after, before, noise_t, index, slot),
+        [smem] * 3 + [vmem] * 6,
+        (loop_left, loop_span, anchors_before, positions, after, before, noise_t, index, slot),
         chain_scratch,
         micros=6,
     )

time: 109 us -> 103 us (0.945)
  Pallas kernels: 57.9 us -> 46.4 us
  waiting for transfers between devices: 7.96 us -> 13.2 us
    pallas_call x9, Pallas kernels: 57.9 us -> 46.4 us  [call(): pl.pallas_call(body, out_shape=outs, in_specs=in_specs, out_specs=[vmem]...]
    all_to_all x4, waiting for transfers between devices: 6.89 us -> 10.3 us  [exchange(): return lax.all_to_all(value, both, split_axis=0, concat_axis=0, tiled=True)]
    ppermute x6, waiting for transfers between devices: 1.07 us -> 2.99 us  [shifted(): lax.ppermute(value, axis, [(source, source + steps) for source in range(f...]
  transfers between devices with their start and end apart: 10 -> 10, of which waited for: 3 -> 5; matrix products, arithmetic and copies ran while one was open for 2% -> 2% of each run, Pallas kernels for 42% -> 37%
where the time goes in v8:
time: 103 us
  Pallas kernels  46.4 us (45%)
  starting transfers between devices  40.4 us (39%)
  waiting for transfers between devices  13.2 us (13%)
  other arithmetic  1.75 us (2%)
    pallas_call x9, Pallas kernels, call(): pl.pallas_call(body, out_shape=outs, in_specs=in_specs, out_specs=[vmem]...  46.4 us
    all_to_all x4, starting transfers between devices, exchange(): return lax.all_to_all(value, both, split_axis=0, concat_axis=0, tiled=True)  21.4 us
    ppermute x6, starting transfers between devices, shifted(): lax.ppermute(value, axis, [(source, source + steps) for source in range(f...  19 us
    all_to_all x4, waiting for transfers between devices, exchange(): return lax.all_to_all(value, both, split_axis=0, concat_axis=0, tiled=True)  10.3 us
    ppermute x6, waiting for transfers between devices, shifted(): lax.ppermute(value, axis, [(source, source + steps) for source in range(f...  2.99 us
  transfers between devices with their start and end apart: 10, of which 5 were waited for; matrix products, arithmetic and copies ran while one was open for 2% of the time, Pallas kernels for 37%

profile of v8, /device:TPU:0, one launch (start us, length us, event | category | flops | bytes accessed | tf_op | source)
XLA Modules:
  0.0 102.7 jit_solution(11172430052959124446)
XLA Ops:
  0.0 1.3 %collective-permute-start.1 = (f32[3,8192]{1,0:T(4,128)}, f32[3,8192]{1,0:T(4,128)S(1)}, u32[]{:S(2)}, u32[]{:S(2)}) collective-permute-start(f32[3,8192]{1,0:T(4,128)} %x_ref.3), channel_id=1, source_target_pairs={{1,0},{2,1},{3,2},{4,3},{5,4},{6,5},{7,6},{8,7},{9,8},{10,9},{11,1... | collective-permute-start | bytes 294920 | tf_op jit(solution)/shard_map/ppermute | solution.py:521
  1.3 0.8 add_convert_fusion
  2.0 1.0 pad_maximum_fusion
  3.0 5.6 %collective-permute-start = (f32[4,8192]{1,0:T(4,128)S(1)}, f32[4,8192]{1,0:T(4,128)S(1)}, u32[]{:S(2)}, u32[]{:S(2)}) collective-permute-start(f32[4,8192]{1,0:T(4,128)S(1)} %pad_maximum_fusion), channel_id=1, source_target_pairs={{0,1},{1,2},{2,3},{3,4},{4,5},{5,6},{6,7},{7,8},{8,9},{9,10},{10,1... | collective-permute-start | bytes 393224 | tf_op jit(solution)/shard_map/ppermute | solution.py:521
  8.6 2.7 %shard_map.73 = (s32[128,128]{1,0:T(8,128)S(1)}, s32[64,128]{1,0:T(8,128)S(1)}, s32[16,128]{1,0:T(8,128)S(1)}) custom-call(s32[64,128]{1,0:T(8,128)S(1)} %bitcast.5), custom_call_target="tpu_custom_call" | custom-call | flops 6000000000 | bytes 1000000 | tf_op jit(solution)/shard_map/pallas_call | solution.py:30
  11.4 4.3 %shard_map.75 = f32[32,12,128]{2,1,0:T(8,128)} custom-call(s32[128,128]{1,0:T(8,128)S(1)} %get-tuple-element.12.index_ref, f32[3,8192]{1,0:T(4,128)S(1)} %copy-done, f32[3,8192]{1,0:T(4,128)S(1)} %collective-permute-done.1.after_ref, f32[4,8192]{1,0:T(4,128)S(1)} %collective-permute-done.before_ref), custom_call_target="tpu_custom_call" | custom-call | flops 4000000000 | bytes 1000000 | tf_op jit(solution)/shard_map/pallas_call | solution.py:30
  15.7 10.0 %all-to-all-start.1 = ((f32[32,12,128]{2,1,0:T(8,128)}), f32[32,12,128]{2,1,0:T(8,128)S(1)}, u32[]{:S(2)}, u32[]{:S(2)}) async-start(f32[32,12,128]{2,1,0:T(8,128)} %shard_map.75), calls=%async_computation.1 | async-start | bytes 524288 | tf_op jit(solution)/shard_map/all_to_all | solution.py:541
  26.3 6.0 %shard_map.74.later_ref = f32[32,13,128]{2,1,0:T(8,128)} custom-call(s32[16]{0:T(128)S(1)} %copy-done.5, s32[16]{0:T(128)S(1)} %copy-done.6, s32[2,16]{1,0:T(2,128)S(1)} %convert_element_type.14.anchors_ref, f32[3,8192]{1,0:T(4,128)S(1)} %copy-done, f32[3,8192]{1,0:T(4,128)S(1)} %collective-permute-done.1.after_ref, ...), custom_call_target="tpu_custom_call" | custom-call | flops 6000000000 | bytes 1000000 | tf_op jit(solution)/shard_map/pallas_call | solution.py:30
  32.3 3.5 %all-to-all-done.1.cells_ref = f32[32,12,128]{2,1,0:T(8,128)S(1)} async-done(((f32[32,12,128]{2,1,0:T(8,128)}), f32[32,12,128]{2,1,0:T(8,128)S(1)}, u32[]{:S(2)}, u32[]{:S(2)}) %all-to-all-start.1) | async-done | bytes 196640 | tf_op jit(solution)/shard_map/all_to_all | solution.py:541
  35.9 1.3 %collective-permute-start.3 = (f32[3,128,128]{2,1,0:T(8,128)S(1)}, f32[3,128,128]{2,1,0:T(8,128)S(1)}, u32[]{:S(2)}, u32[]{:S(2)}) collective-permute-start(f32[3,128,128]{2,1,0:T(8,128)S(1)} %shard_map.76.own_ref), channel_id=1, source_target_pairs={{1,0},{2,1},{3,2},{5,4},{6,5},{7,6},{9,8},{10,9},{11,10},{13,12},{... | collective-permute-start | bytes 589832 | tf_op jit(solution)/shard_map/ppermute | solution.py:521
  37.2 4.6 %collective-permute-start.2 = (f32[3,128,128]{2,1,0:T(8,128)S(1)}, f32[3,128,128]{2,1,0:T(8,128)S(1)}, u32[]{:S(2)}, u32[]{:S(2)}) collective-permute-start(f32[3,128,128]{2,1,0:T(8,128)S(1)} %shard_map.76.own_ref), channel_id=1, source_target_pairs={{0,1},{1,2},{2,3},{4,5},{5,6},{6,7},{8,9},{9,10},{10,11},{12,13},{... | collective-permute-start | bytes 589832 | tf_op jit(solution)/shard_map/ppermute | solution.py:521
  41.8 2.6 %all-to-all-start = ((f32[32,13,128]{2,1,0:T(8,128)}), f32[32,13,128]{2,1,0:T(8,128)S(1)}, u32[]{:S(2)}, u32[]{:S(2)}) async-start(f32[32,13,128]{2,1,0:T(8,128)} %shard_map.74.later_ref), calls=%async_computation | async-start | bytes 524288 | tf_op jit(solution)/shard_map/all_to_all | solution.py:541
  44.4 0.7 collective-permute-done.3.above_ref
  45.0 2.0 %collective-permute-done.2.below_ref = f32[3,128,128]{2,1,0:T(8,128)S(1)} collective-permute-done((f32[3,128,128]{2,1,0:T(8,128)S(1)}, f32[3,128,128]{2,1,0:T(8,128)S(1)}, u32[]{:S(2)}, u32[]{:S(2)}) %collective-permute-start.2) | collective-permute-done | bytes 196640 | tf_op jit(solution)/shard_map/ppermute | solution.py:521
  47.0 12.6 %shard_map.77.force_ref = f32[32,12,128]{2,1,0:T(8,128)S(1)} custom-call(s32[512]{0:T(512)S(1)} %copy-done.3, s32[512]{0:T(512)S(1)} %copy-done.4, f32[3,128,128]{2,1,0:T(8,128)S(1)} %collective-permute-done.2.below_ref, f32[3,128,128]{2,1,0:T(8,128)S(1)} %shard_map.76.own_ref, f32[3,128,128]{2,1,0:T(8,128)S(1)} %collective-permute-done.3.above_ref), custom_call_target="tpu_custom_call" | custom-call | flops 14000000000 | bytes 1000000 | tf_op jit(solution)/shard_map/pallas_call | solution.py:30
  59.6 0.9 shard_map.78
  60.5 1.3 %collective-permute-start.5 = (f32[3,128,128]{2,1,0:T(8,128)S(1)}, f32[3,128,128]{2,1,0:T(8,128)S(1)}, u32[]{:S(2)}, u32[]{:S(2)}) collective-permute-start(f32[3,128,128]{2,1,0:T(8,128)S(1)} %get-tuple-element.13.own_ref), channel_id=1, source_target_pairs={{1,0},{2,1},{3,2},{5,4},{6,5},{7,6},{9,8},{10,9},{11,10},{13,12},{... | collective-permute-start | bytes 589832 | tf_op jit(solution)/shard_map/ppermute | solution.py:521
  61.8 5.0 %collective-permute-start.4 = (f32[3,128,128]{2,1,0:T(8,128)S(1)}, f32[3,128,128]{2,1,0:T(8,128)S(1)}, u32[]{:S(2)}, u32[]{:S(2)}) collective-permute-start(f32[3,128,128]{2,1,0:T(8,128)S(1)} %get-tuple-element.13.own_ref), channel_id=1, source_target_pairs={{0,1},{1,2},{2,3},{4,5},{5,6},{6,7},{8,9},{9,10},{10,11},{12,13},{... | collective-permute-start | bytes 589832 | tf_op jit(solution)/shard_map/ppermute | solution.py:521
  66.8 2.8 %all-to-all-start.3 = ((f32[32,15,128]{2,1,0:T(8,128)}), f32[32,15,128]{2,1,0:T(8,128)S(1)}, u32[]{:S(2)}, u32[]{:S(2)}) async-start(f32[32,15,128]{2,1,0:T(8,128)} %get-tuple-element.14), calls=%async_computation.3 | async-start | bytes 524288 | tf_op jit(solution)/shard_map/all_to_all | solution.py:541
  70.0 13.3 %shard_map.79 = f32[32,12,128]{2,1,0:T(8,128)} custom-call(s32[512]{0:T(512)S(1)} %copy-done.3, s32[512]{0:T(512)S(1)} %copy-done.4, f32[3,128,128]{2,1,0:T(8,128)S(1)} %collective-permute-done.4.below_ref, f32[3,128,128]{2,1,0:T(8,128)S(1)} %get-tuple-element.13.own_ref, f32[3,128,128]{2,1,0:T(8,128)S(1)} %collective-permute-done.5.above_ref), custom_call_target="tpu_custom_call" | custom-call | flops 14000000000 | bytes 1000000 | tf_op jit(solution)/shard_map/pallas_call | solution.py:30
  83.3 6.0 %all-to-all-start.2 = ((f32[32,12,128]{2,1,0:T(8,128)}), f32[32,12,128]{2,1,0:T(8,128)S(1)}, u32[]{:S(2)}, u32[]{:S(2)}) async-start(f32[32,12,128]{2,1,0:T(8,128)} %shard_map.79), calls=%async_computation.2 | async-start | bytes 524288 | tf_op jit(solution)/shard_map/all_to_all | solution.py:541
  89.3 3.4 %shard_map.80.base_ref = f32[3,8192]{1,0:T(4,128)S(1)} custom-call(s32[16]{0:T(128)S(1)} %copy-done.5, s32[16]{0:T(128)S(1)} %copy-done.6, s32[2,16]{1,0:T(2,128)S(1)} %convert_element_type.14.anchors_ref, s32[16,128]{1,0:T(8,128)S(1)} %get-tuple-element.10.ranges_ref, s32[64,128]{1,0:T(8,128)S(1)} %get-tuple-element.11.slot_ref, ...), custom_call_target="tpu_custom_call" | custom-call | flops 6000000000 | bytes 1000000 | tf_op jit(solution)/shard_map/pallas_call | solution.py:30
  92.7 6.8 %all-to-all-done.2.back_ref = f32[32,12,128]{2,1,0:T(8,128)S(1)} async-done(((f32[32,12,128]{2,1,0:T(8,128)}), f32[32,12,128]{2,1,0:T(8,128)S(1)}, u32[]{:S(2)}, u32[]{:S(2)}) %all-to-all-start.2) | async-done | bytes 196640 | tf_op jit(solution)/shard_map/all_to_all | solution.py:541
  99.5 3.2 %shard_map.81 = f32[3,8192]{1,0:T(4,128)} custom-call(s32[16,128]{1,0:T(8,128)S(1)} %get-tuple-element.10.ranges_ref, s32[64,128]{1,0:T(8,128)S(1)} %get-tuple-element.11.slot_ref, f32[32,12,128]{2,1,0:T(8,128)S(1)} %all-to-all-done.2.back_ref, f32[3,8192]{1,0:T(4,128)S(1)} %shard_map.80.base_ref), custom_call_target="tpu_custom_call" | custom-call | flops 4000000000 | bytes 1000000 | tf_op jit(solution)/shard_map/pallas_call | solution.py:30
  (24 shorter events, 1.2 us)
Async XLA Ops:
  0.0 11.4 %collective-permute-start.1 = (f32[3,8192]{1,0:T(4,128)}, f32[3,8192]{1,0:T(4,128)S(1)}, u32[]{:S(2)}, u32[]{:S(2)}) collective-permute-start(f32[3,8192]{1,0:T(4,128)} %x_ref.3), channel_id=1, source_target_pairs={{1,0},{2,1},{3,2},{4,3},{5,4},{6,5},{7,6},{8,7},{9,8},{10,9},{11,1... | collective-permute-start | bytes 294920 | tf_op jit(solution)/shard_map/ppermute | solution.py:521
  2.0 6.6 %copy-start.2 = (s32[8192,1]{0,1:T(1,128)S(1)}, s32[8192,1]{0,1:T(1,128)}, u32[]{:S(2)}) copy-start(s32[8192,1]{0,1:T(1,128)} %param.9) | copy-start | bytes 98308
  3.0 8.3 %collective-permute-start = (f32[4,8192]{1,0:T(4,128)S(1)}, f32[4,8192]{1,0:T(4,128)S(1)}, u32[]{:S(2)}, u32[]{:S(2)}) collective-permute-start(f32[4,8192]{1,0:T(4,128)S(1)} %pad_maximum_fusion), channel_id=1, source_target_pairs={{0,1},{1,2},{2,3},{3,4},{4,5},{5,6},{6,7},{7,8},{8,9},{9,10},{10,1... | collective-permute-start | bytes 393224 | tf_op jit(solution)/shard_map/ppermute | solution.py:521
  8.6 2.8 %copy-start = (f32[3,8192]{1,0:T(4,128)S(1)}, f32[3,8192]{1,0:T(4,128)}, u32[]{:S(2)}) copy-start(f32[3,8192]{1,0:T(4,128)} %x_ref.3) | copy-start | bytes 294916
  15.7 10.0 %copy-start.1 = (f32[2,3,8192]{2,0,1:T(2,128)S(1)}, f32[2,3,8192]{2,0,1:T(2,128)}, u32[]{:S(2)}) copy-start(f32[2,3,8192]{2,0,1:T(2,128)} %param.8) | copy-start | bytes 589828
  15.7 20.2 %all-to-all-start.1 = ((f32[32,12,128]{2,1,0:T(8,128)}), f32[32,12,128]{2,1,0:T(8,128)S(1)}, u32[]{:S(2)}, u32[]{:S(2)}) async-start(f32[32,12,128]{2,1,0:T(8,128)} %shard_map.75), calls=%async_computation.1 | async-start | bytes 524288 | tf_op jit(solution)/shard_map/all_to_all | solution.py:541
  25.6 0.7 copy-start.5
  25.6 0.7 copy-start.6
  35.9 11.1 %copy-start.3 = (s32[512]{0:T(512)S(1)}, s32[512]{0:T(512)}, u32[]{:S(2)}) copy-start(s32[512]{0:T(512)} %rows_ref.3) | copy-start | bytes 6148
  35.9 11.1 %copy-start.4 = (s32[512]{0:T(512)S(1)}, s32[512]{0:T(512)}, u32[]{:S(2)}) copy-start(s32[512]{0:T(512)} %cols_ref.3) | copy-start | bytes 6148
  35.9 9.1 %collective-permute-start.3 = (f32[3,128,128]{2,1,0:T(8,128)S(1)}, f32[3,128,128]{2,1,0:T(8,128)S(1)}, u32[]{:S(2)}, u32[]{:S(2)}) collective-permute-start(f32[3,128,128]{2,1,0:T(8,128)S(1)} %shard_map.76.own_ref), channel_id=1, source_target_pairs={{1,0},{2,1},{3,2},{5,4},{6,5},{7,6},{9,8},{10,9},{11,10},{13,12},{... | collective-permute-start | bytes 589832 | tf_op jit(solution)/shard_map/ppermute | solution.py:521
  37.2 9.8 %collective-permute-start.2 = (f32[3,128,128]{2,1,0:T(8,128)S(1)}, f32[3,128,128]{2,1,0:T(8,128)S(1)}, u32[]{:S(2)}, u32[]{:S(2)}) collective-permute-start(f32[3,128,128]{2,1,0:T(8,128)S(1)} %shard_map.76.own_ref), channel_id=1, source_target_pairs={{0,1},{1,2},{2,3},{4,5},{5,6},{6,7},{8,9},{9,10},{10,11},{12,13},{... | collective-permute-start | bytes 589832 | tf_op jit(solution)/shard_map/ppermute | solution.py:521
  41.8 17.8 %all-to-all-start = ((f32[32,13,128]{2,1,0:T(8,128)}), f32[32,13,128]{2,1,0:T(8,128)S(1)}, u32[]{:S(2)}, u32[]{:S(2)}) async-start(f32[32,13,128]{2,1,0:T(8,128)} %shard_map.74.later_ref), calls=%async_computation | async-start | bytes 524288 | tf_op jit(solution)/shard_map/all_to_all | solution.py:541
  60.5 9.1 %collective-permute-start.5 = (f32[3,128,128]{2,1,0:T(8,128)S(1)}, f32[3,128,128]{2,1,0:T(8,128)S(1)}, u32[]{:S(2)}, u32[]{:S(2)}) collective-permute-start(f32[3,128,128]{2,1,0:T(8,128)S(1)} %get-tuple-element.13.own_ref), channel_id=1, source_target_pairs={{1,0},{2,1},{3,2},{5,4},{6,5},{7,6},{9,8},{10,9},{11,10},{13,12},{... | collective-permute-start | bytes 589832 | tf_op jit(solution)/shard_map/ppermute | solution.py:521
  61.8 8.2 %collective-permute-start.4 = (f32[3,128,128]{2,1,0:T(8,128)S(1)}, f32[3,128,128]{2,1,0:T(8,128)S(1)}, u32[]{:S(2)}, u32[]{:S(2)}) collective-permute-start(f32[3,128,128]{2,1,0:T(8,128)S(1)} %get-tuple-element.13.own_ref), channel_id=1, source_target_pairs={{0,1},{1,2},{2,3},{4,5},{5,6},{6,7},{8,9},{9,10},{10,11},{12,13},{... | collective-permute-start | bytes 589832 | tf_op jit(solution)/shard_map/ppermute | solution.py:521
  66.8 16.4 %all-to-all-start.3 = ((f32[32,15,128]{2,1,0:T(8,128)}), f32[32,15,128]{2,1,0:T(8,128)S(1)}, u32[]{:S(2)}, u32[]{:S(2)}) async-start(f32[32,15,128]{2,1,0:T(8,128)} %get-tuple-element.14), calls=%async_computation.3 | async-start | bytes 524288 | tf_op jit(solution)/shard_map/all_to_all | solution.py:541
  83.3 16.2 %all-to-all-start.2 = ((f32[32,12,128]{2,1,0:T(8,128)}), f32[32,12,128]{2,1,0:T(8,128)S(1)}, u32[]{:S(2)}, u32[]{:S(2)}) async-start(f32[32,12,128]{2,1,0:T(8,128)} %shard_map.79), calls=%async_computation.2 | async-start | bytes 524288 | tf_op jit(solution)/shard_map/all_to_all | solution.py:541

commit v9 on v8

--- a/solution.py
+++ b/solution.py
@@ -154,7 +154,7 @@
     index_ref[...] = (total_ref[0:blocks, :] + lanes * total_ref[blocks:, :]).astype(jnp.int32)
 
 
-def send_kernel(index_ref, x_ref, after_ref, before_ref, out_ref):
+def send_kernel(index_ref, x_ref, after_ref, out_ref):
     fill_slots(index_ref, x_ref, out_ref, out_ref.shape[1] // 3)
 
 
@@ -579,8 +579,8 @@
     x_out = call(
         send_kernel,
         sent,
-        [vmem] * 4,
-        (index, positions, after, before),
+        [vmem] * 3,
+        (index, positions, after),
         micros=4,
     )
     anchors_before = before[3, : 2 * extruders].astype(jnp.int32).reshape(2, extruders)

time: 103 us -> 101 us (0.981)
  starting transfers between devices: 40.4 us -> 38.5 us
    all_to_all x4, starting transfers between devices: 21.4 us -> 19.5 us  [exchange(): return lax.all_to_all(value, both, split_axis=0, concat_axis=0, tiled=True)]
  transfers between devices with their start and end apart: 10 -> 10, of which waited for: 5 -> 5; matrix products, arithmetic and copies ran while one was open for 2% -> 2% of each run, Pallas kernels for 37% -> 42%
where the time goes in v9:
time: 101 us
  Pallas kernels  46.4 us (46%)
  starting transfers between devices  38.5 us (38%)
  waiting for transfers between devices  13.1 us (13%)
  other arithmetic  1.75 us (2%)
    pallas_call x9, Pallas kernels, call(): pl.pallas_call(body, out_shape=outs, in_specs=in_specs, out_specs=[vmem]...  46.4 us
    all_to_all x4, starting transfers between devices, exchange(): return lax.all_to_all(value, both, split_axis=0, concat_axis=0, tiled=True)  19.5 us
    ppermute x6, starting transfers between devices, shifted(): lax.ppermute(value, axis, [(source, source + steps) for source in range(f...  19 us
    all_to_all x4, waiting for transfers between devices, exchange(): return lax.all_to_all(value, both, split_axis=0, concat_axis=0, tiled=True)  10.1 us
    ppermute x6, waiting for transfers between devices, shifted(): lax.ppermute(value, axis, [(source, source + steps) for source in range(f...  2.99 us
  transfers between devices with their start and end apart: 10, of which 5 were waited for; matrix products, arithmetic and copies ran while one was open for 2% of the time, Pallas kernels for 42%

profile of v9, /device:TPU:0, one launch (start us, length us, event | category | flops | bytes accessed | tf_op | source)
XLA Modules:
  0.0 100.7 jit_solution(11418898978301144916)
XLA Ops:
  0.0 1.3 %collective-permute-start.1 = (f32[3,8192]{1,0:T(4,128)}, f32[3,8192]{1,0:T(4,128)S(1)}, u32[]{:S(2)}, u32[]{:S(2)}) collective-permute-start(f32[3,8192]{1,0:T(4,128)} %x_ref.3), channel_id=1, source_target_pairs={{1,0},{2,1},{3,2},{4,3},{5,4},{6,5},{7,6},{8,7},{9,8},{10,9},{11,1... | collective-permute-start | bytes 294920 | tf_op jit(solution)/shard_map/ppermute | solution.py:521
  1.3 0.8 add_convert_fusion
  2.0 1.0 pad_maximum_fusion
  3.0 5.6 %collective-permute-start = (f32[4,8192]{1,0:T(4,128)S(1)}, f32[4,8192]{1,0:T(4,128)S(1)}, u32[]{:S(2)}, u32[]{:S(2)}) collective-permute-start(f32[4,8192]{1,0:T(4,128)S(1)} %pad_maximum_fusion), channel_id=1, source_target_pairs={{0,1},{1,2},{2,3},{3,4},{4,5},{5,6},{6,7},{7,8},{8,9},{9,10},{10,1... | collective-permute-start | bytes 393224 | tf_op jit(solution)/shard_map/ppermute | solution.py:521
  8.6 2.7 %shard_map.73 = (s32[128,128]{1,0:T(8,128)S(1)}, s32[64,128]{1,0:T(8,128)S(1)}, s32[16,128]{1,0:T(8,128)S(1)}) custom-call(s32[64,128]{1,0:T(8,128)S(1)} %bitcast.5), custom_call_target="tpu_custom_call" | custom-call | flops 6000000000 | bytes 1000000 | tf_op jit(solution)/shard_map/pallas_call | solution.py:30
  11.3 4.3 %shard_map.75 = f32[32,12,128]{2,1,0:T(8,128)} custom-call(s32[128,128]{1,0:T(8,128)S(1)} %get-tuple-element.12.index_ref, f32[3,8192]{1,0:T(4,128)S(1)} %copy-done, f32[3,8192]{1,0:T(4,128)S(1)} %collective-permute-done.1.after_ref), custom_call_target="tpu_custom_call" | custom-call | flops 4000000000 | bytes 1000000 | tf_op jit(solution)/shard_map/pallas_call | solution.py:30
  15.6 8.1 %all-to-all-start.1 = ((f32[32,12,128]{2,1,0:T(8,128)}), f32[32,12,128]{2,1,0:T(8,128)S(1)}, u32[]{:S(2)}, u32[]{:S(2)}) async-start(f32[32,12,128]{2,1,0:T(8,128)} %shard_map.75), calls=%async_computation.1 | async-start | bytes 524288 | tf_op jit(solution)/shard_map/all_to_all | solution.py:541
  24.4 6.0 %shard_map.74.later_ref = f32[32,13,128]{2,1,0:T(8,128)} custom-call(s32[16]{0:T(128)S(1)} %copy-done.5, s32[16]{0:T(128)S(1)} %copy-done.6, s32[2,16]{1,0:T(2,128)S(1)} %convert_element_type.14.anchors_ref, f32[3,8192]{1,0:T(4,128)S(1)} %copy-done, f32[3,8192]{1,0:T(4,128)S(1)} %collective-permute-done.1.after_ref, ...), custom_call_target="tpu_custom_call" | custom-call | flops 6000000000 | bytes 1000000 | tf_op jit(solution)/shard_map/pallas_call | solution.py:30
  30.5 3.4 %all-to-all-done.1.cells_ref = f32[32,12,128]{2,1,0:T(8,128)S(1)} async-done(((f32[32,12,128]{2,1,0:T(8,128)}), f32[32,12,128]{2,1,0:T(8,128)S(1)}, u32[]{:S(2)}, u32[]{:S(2)}) %all-to-all-start.1) | async-done | bytes 196640 | tf_op jit(solution)/shard_map/all_to_all | solution.py:541
  33.9 1.3 %collective-permute-start.3 = (f32[3,128,128]{2,1,0:T(8,128)S(1)}, f32[3,128,128]{2,1,0:T(8,128)S(1)}, u32[]{:S(2)}, u32[]{:S(2)}) collective-permute-start(f32[3,128,128]{2,1,0:T(8,128)S(1)} %shard_map.76.own_ref), channel_id=1, source_target_pairs={{1,0},{2,1},{3,2},{5,4},{6,5},{7,6},{9,8},{10,9},{11,10},{13,12},{... | collective-permute-start | bytes 589832 | tf_op jit(solution)/shard_map/ppermute | solution.py:521
  35.2 4.6 %collective-permute-start.2 = (f32[3,128,128]{2,1,0:T(8,128)S(1)}, f32[3,128,128]{2,1,0:T(8,128)S(1)}, u32[]{:S(2)}, u32[]{:S(2)}) collective-permute-start(f32[3,128,128]{2,1,0:T(8,128)S(1)} %shard_map.76.own_ref), channel_id=1, source_target_pairs={{0,1},{1,2},{2,3},{4,5},{5,6},{6,7},{8,9},{9,10},{10,11},{12,13},{... | collective-permute-start | bytes 589832 | tf_op jit(solution)/shard_map/ppermute | solution.py:521
  39.8 2.6 %all-to-all-start = ((f32[32,13,128]{2,1,0:T(8,128)}), f32[32,13,128]{2,1,0:T(8,128)S(1)}, u32[]{:S(2)}, u32[]{:S(2)}) async-start(f32[32,13,128]{2,1,0:T(8,128)} %shard_map.74.later_ref), calls=%async_computation | async-start | bytes 524288 | tf_op jit(solution)/shard_map/all_to_all | solution.py:541
  42.4 0.7 collective-permute-done.3.above_ref
  43.0 2.0 %collective-permute-done.2.below_ref = f32[3,128,128]{2,1,0:T(8,128)S(1)} collective-permute-done((f32[3,128,128]{2,1,0:T(8,128)S(1)}, f32[3,128,128]{2,1,0:T(8,128)S(1)}, u32[]{:S(2)}, u32[]{:S(2)}) %collective-permute-start.2) | collective-permute-done | bytes 196640 | tf_op jit(solution)/shard_map/ppermute | solution.py:521
  45.0 12.6 %shard_map.77.force_ref = f32[32,12,128]{2,1,0:T(8,128)S(1)} custom-call(s32[512]{0:T(512)S(1)} %copy-done.3, s32[512]{0:T(512)S(1)} %copy-done.4, f32[3,128,128]{2,1,0:T(8,128)S(1)} %collective-permute-done.2.below_ref, f32[3,128,128]{2,1,0:T(8,128)S(1)} %shard_map.76.own_ref, f32[3,128,128]{2,1,0:T(8,128)S(1)} %collective-permute-done.3.above_ref), custom_call_target="tpu_custom_call" | custom-call | flops 14000000000 | bytes 1000000 | tf_op jit(solution)/shard_map/pallas_call | solution.py:30
  57.6 0.9 shard_map.78
  58.5 1.3 %collective-permute-start.5 = (f32[3,128,128]{2,1,0:T(8,128)S(1)}, f32[3,128,128]{2,1,0:T(8,128)S(1)}, u32[]{:S(2)}, u32[]{:S(2)}) collective-permute-start(f32[3,128,128]{2,1,0:T(8,128)S(1)} %get-tuple-element.13.own_ref), channel_id=1, source_target_pairs={{1,0},{2,1},{3,2},{5,4},{6,5},{7,6},{9,8},{10,9},{11,10},{13,12},{... | collective-permute-start | bytes 589832 | tf_op jit(solution)/shard_map/ppermute | solution.py:521
  59.8 5.0 %collective-permute-start.4 = (f32[3,128,128]{2,1,0:T(8,128)S(1)}, f32[3,128,128]{2,1,0:T(8,128)S(1)}, u32[]{:S(2)}, u32[]{:S(2)}) collective-permute-start(f32[3,128,128]{2,1,0:T(8,128)S(1)} %get-tuple-element.13.own_ref), channel_id=1, source_target_pairs={{0,1},{1,2},{2,3},{4,5},{5,6},{6,7},{8,9},{9,10},{10,11},{12,13},{... | collective-permute-start | bytes 589832 | tf_op jit(solution)/shard_map/ppermute | solution.py:521
  64.9 2.8 %all-to-all-start.3 = ((f32[32,15,128]{2,1,0:T(8,128)}), f32[32,15,128]{2,1,0:T(8,128)S(1)}, u32[]{:S(2)}, u32[]{:S(2)}) async-start(f32[32,15,128]{2,1,0:T(8,128)} %get-tuple-element.14), calls=%async_computation.3 | async-start | bytes 524288 | tf_op jit(solution)/shard_map/all_to_all | solution.py:541
  68.0 13.3 %shard_map.79 = f32[32,12,128]{2,1,0:T(8,128)} custom-call(s32[512]{0:T(512)S(1)} %copy-done.3, s32[512]{0:T(512)S(1)} %copy-done.4, f32[3,128,128]{2,1,0:T(8,128)S(1)} %collective-permute-done.4.below_ref, f32[3,128,128]{2,1,0:T(8,128)S(1)} %get-tuple-element.13.own_ref, f32[3,128,128]{2,1,0:T(8,128)S(1)} %collective-permute-done.5.above_ref), custom_call_target="tpu_custom_call" | custom-call | flops 14000000000 | bytes 1000000 | tf_op jit(solution)/shard_map/pallas_call | solution.py:30
  81.3 6.0 %all-to-all-start.2 = ((f32[32,12,128]{2,1,0:T(8,128)}), f32[32,12,128]{2,1,0:T(8,128)S(1)}, u32[]{:S(2)}, u32[]{:S(2)}) async-start(f32[32,12,128]{2,1,0:T(8,128)} %shard_map.79), calls=%async_computation.2 | async-start | bytes 524288 | tf_op jit(solution)/shard_map/all_to_all | solution.py:541
  87.3 3.4 %shard_map.80.base_ref = f32[3,8192]{1,0:T(4,128)S(1)} custom-call(s32[16]{0:T(128)S(1)} %copy-done.5, s32[16]{0:T(128)S(1)} %copy-done.6, s32[2,16]{1,0:T(2,128)S(1)} %convert_element_type.14.anchors_ref, s32[16,128]{1,0:T(8,128)S(1)} %get-tuple-element.10.ranges_ref, s32[64,128]{1,0:T(8,128)S(1)} %get-tuple-element.11.slot_ref, ...), custom_call_target="tpu_custom_call" | custom-call | flops 6000000000 | bytes 1000000 | tf_op jit(solution)/shard_map/pallas_call | solution.py:30
  90.8 6.8 %all-to-all-done.2.back_ref = f32[32,12,128]{2,1,0:T(8,128)S(1)} async-done(((f32[32,12,128]{2,1,0:T(8,128)}), f32[32,12,128]{2,1,0:T(8,128)S(1)}, u32[]{:S(2)}, u32[]{:S(2)}) %all-to-all-start.2) | async-done | bytes 196640 | tf_op jit(solution)/shard_map/all_to_all | solution.py:541
  97.5 3.2 %shard_map.81 = f32[3,8192]{1,0:T(4,128)} custom-call(s32[16,128]{1,0:T(8,128)S(1)} %get-tuple-element.10.ranges_ref, s32[64,128]{1,0:T(8,128)S(1)} %get-tuple-element.11.slot_ref, f32[32,12,128]{2,1,0:T(8,128)S(1)} %all-to-all-done.2.back_ref, f32[3,8192]{1,0:T(4,128)S(1)} %shard_map.80.base_ref), custom_call_target="tpu_custom_call" | custom-call | flops 4000000000 | bytes 1000000 | tf_op jit(solution)/shard_map/pallas_call | solution.py:30
  (24 shorter events, 1.2 us)
Async XLA Ops:
  0.0 11.3 %collective-permute-start.1 = (f32[3,8192]{1,0:T(4,128)}, f32[3,8192]{1,0:T(4,128)S(1)}, u32[]{:S(2)}, u32[]{:S(2)}) collective-permute-start(f32[3,8192]{1,0:T(4,128)} %x_ref.3), channel_id=1, source_target_pairs={{1,0},{2,1},{3,2},{4,3},{5,4},{6,5},{7,6},{8,7},{9,8},{10,9},{11,1... | collective-permute-start | bytes 294920 | tf_op jit(solution)/shard_map/ppermute | solution.py:521
  2.0 6.6 %copy-start.2 = (s32[8192,1]{0,1:T(1,128)S(1)}, s32[8192,1]{0,1:T(1,128)}, u32[]{:S(2)}) copy-start(s32[8192,1]{0,1:T(1,128)} %param.9) | copy-start | bytes 98308
  3.0 20.6 %collective-permute-start = (f32[4,8192]{1,0:T(4,128)S(1)}, f32[4,8192]{1,0:T(4,128)S(1)}, u32[]{:S(2)}, u32[]{:S(2)}) collective-permute-start(f32[4,8192]{1,0:T(4,128)S(1)} %pad_maximum_fusion), channel_id=1, source_target_pairs={{0,1},{1,2},{2,3},{3,4},{4,5},{5,6},{6,7},{7,8},{8,9},{9,10},{10,1... | collective-permute-start | bytes 393224 | tf_op jit(solution)/shard_map/ppermute | solution.py:521
  8.6 2.7 %copy-start = (f32[3,8192]{1,0:T(4,128)S(1)}, f32[3,8192]{1,0:T(4,128)}, u32[]{:S(2)}) copy-start(f32[3,8192]{1,0:T(4,128)} %x_ref.3) | copy-start | bytes 294916
  15.6 8.2 %copy-start.1 = (f32[2,3,8192]{2,0,1:T(2,128)S(1)}, f32[2,3,8192]{2,0,1:T(2,128)}, u32[]{:S(2)}) copy-start(f32[2,3,8192]{2,0,1:T(2,128)} %param.8) | copy-start | bytes 589828
  15.6 18.3 %all-to-all-start.1 = ((f32[32,12,128]{2,1,0:T(8,128)}), f32[32,12,128]{2,1,0:T(8,128)S(1)}, u32[]{:S(2)}, u32[]{:S(2)}) async-start(f32[32,12,128]{2,1,0:T(8,128)} %shard_map.75), calls=%async_computation.1 | async-start | bytes 524288 | tf_op jit(solution)/shard_map/all_to_all | solution.py:541
  23.8 0.7 copy-start.5
  23.8 0.7 copy-start.6
  33.9 11.1 %copy-start.3 = (s32[512]{0:T(512)S(1)}, s32[512]{0:T(512)}, u32[]{:S(2)}) copy-start(s32[512]{0:T(512)} %rows_ref.3) | copy-start | bytes 6148
  33.9 11.1 %copy-start.4 = (s32[512]{0:T(512)S(1)}, s32[512]{0:T(512)}, u32[]{:S(2)}) copy-start(s32[512]{0:T(512)} %cols_ref.3) | copy-start | bytes 6148
  33.9 9.1 %collective-permute-start.3 = (f32[3,128,128]{2,1,0:T(8,128)S(1)}, f32[3,128,128]{2,1,0:T(8,128)S(1)}, u32[]{:S(2)}, u32[]{:S(2)}) collective-permute-start(f32[3,128,128]{2,1,0:T(8,128)S(1)} %shard_map.76.own_ref), channel_id=1, source_target_pairs={{1,0},{2,1},{3,2},{5,4},{6,5},{7,6},{9,8},{10,9},{11,10},{13,12},{... | collective-permute-start | bytes 589832 | tf_op jit(solution)/shard_map/ppermute | solution.py:521
  35.2 9.8 %collective-permute-start.2 = (f32[3,128,128]{2,1,0:T(8,128)S(1)}, f32[3,128,128]{2,1,0:T(8,128)S(1)}, u32[]{:S(2)}, u32[]{:S(2)}) collective-permute-start(f32[3,128,128]{2,1,0:T(8,128)S(1)} %shard_map.76.own_ref), channel_id=1, source_target_pairs={{0,1},{1,2},{2,3},{4,5},{5,6},{6,7},{8,9},{9,10},{10,11},{12,13},{... | collective-permute-start | bytes 589832 | tf_op jit(solution)/shard_map/ppermute | solution.py:521
  39.8 17.8 %all-to-all-start = ((f32[32,13,128]{2,1,0:T(8,128)}), f32[32,13,128]{2,1,0:T(8,128)S(1)}, u32[]{:S(2)}, u32[]{:S(2)}) async-start(f32[32,13,128]{2,1,0:T(8,128)} %shard_map.74.later_ref), calls=%async_computation | async-start | bytes 524288 | tf_op jit(solution)/shard_map/all_to_all | solution.py:541
  58.5 9.1 %collective-permute-start.5 = (f32[3,128,128]{2,1,0:T(8,128)S(1)}, f32[3,128,128]{2,1,0:T(8,128)S(1)}, u32[]{:S(2)}, u32[]{:S(2)}) collective-permute-start(f32[3,128,128]{2,1,0:T(8,128)S(1)} %get-tuple-element.13.own_ref), channel_id=1, source_target_pairs={{1,0},{2,1},{3,2},{5,4},{6,5},{7,6},{9,8},{10,9},{11,10},{13,12},{... | collective-permute-start | bytes 589832 | tf_op jit(solution)/shard_map/ppermute | solution.py:521
  59.8 8.2 %collective-permute-start.4 = (f32[3,128,128]{2,1,0:T(8,128)S(1)}, f32[3,128,128]{2,1,0:T(8,128)S(1)}, u32[]{:S(2)}, u32[]{:S(2)}) collective-permute-start(f32[3,128,128]{2,1,0:T(8,128)S(1)} %get-tuple-element.13.own_ref), channel_id=1, source_target_pairs={{0,1},{1,2},{2,3},{4,5},{5,6},{6,7},{8,9},{9,10},{10,11},{12,13},{... | collective-permute-start | bytes 589832 | tf_op jit(solution)/shard_map/ppermute | solution.py:521
  64.9 16.4 %all-to-all-start.3 = ((f32[32,15,128]{2,1,0:T(8,128)}), f32[32,15,128]{2,1,0:T(8,128)S(1)}, u32[]{:S(2)}, u32[]{:S(2)}) async-start(f32[32,15,128]{2,1,0:T(8,128)} %get-tuple-element.14), calls=%async_computation.3 | async-start | bytes 524288 | tf_op jit(solution)/shard_map/all_to_all | solution.py:541
  81.3 16.2 %all-to-all-start.2 = ((f32[32,12,128]{2,1,0:T(8,128)}), f32[32,12,128]{2,1,0:T(8,128)S(1)}, u32[]{:S(2)}, u32[]{:S(2)}) async-start(f32[32,12,128]{2,1,0:T(8,128)} %shard_map.79), calls=%async_computation.2 | async-start | bytes 524288 | tf_op jit(solution)/shard_map/all_to_all | solution.py:541
